TPU v7x, 32 devices: a whole 2x2x4 slice. The times are simulated.
32 devices in a mesh: row: 8 (over z, core), col: 4 (over y, x).
Axes of the slice: x: 2, y: 2, z: 4, core: 2. Of those that a mesh axis runs over, the one named last changes fastest.
Arguments:
- factor_a: bfloat16 [16384, 1024], P(('col', 'row')), may hold values from -0.1875 to 0.1875
- factor_b: bfloat16 [16384, 1024], P(('col', 'row')), may hold values from -0.1875 to 0.1875
- factor_c: bfloat16 [16384, 1024], P(('col', 'row')), may hold values from -0.1875 to 0.1875
Outputs:
- grad_a: float32 [16384, 1024], P(('col', 'row'))
- grad_b: float32 [16384, 1024], P(('col', 'row'))
- grad_c: float32 [16384, 1024], P(('col', 'row'))
All inputs are finite; a program needn't handle non-finite values.
Results may differ from a plain program's by a relative error of at most 0.0095.
Values may be sent and summed in bfloat16 or wider, within the bound.
No kernel may reach another device: no remote copies, remote signals or barrier semaphores. Data moves between devices by JAX's collectives and lax.ppermute only.
A program may use at most 192 MiB of HBM per device.

v0:
```python
import jax
import jax.numpy as jnp
from jax import lax
from jax.sharding import PartitionSpec as P

NMAT = 32


def gram_rows(left, right):
    return lax.dot_general(
        left, right, (((1,), (1,)), ((), ())), preferred_element_type=jnp.float32
    )


def apply_rows(hadam, right):
    return jnp.dot(hadam, right, preferred_element_type=jnp.float32)


def block_terms(lefts, rights):
    grams = [gram_rows(l, r) for l, r in zip(lefts, rights)]
    hadam_a = (grams[1] * grams[2]).astype(jnp.bfloat16)
    hadam_b = (grams[2] * grams[0]).astype(jnp.bfloat16)
    hadam_c = (grams[0] * grams[1]).astype(jnp.bfloat16)
    hadams = (hadam_a, hadam_b, hadam_c)
    return jnp.concatenate([apply_rows(h, r) for h, r in zip(hadams, rights)], axis=1)


def shards(factor_a, factor_b, factor_c):
    own_rows = factor_a.shape[0]
    length = factor_a.shape[1]
    block_j = (
        lax.all_gather(factor_a, "row", axis=0, tiled=True),
        lax.all_gather(factor_b, "row", axis=0, tiled=True),
        lax.all_gather(factor_c, "row", axis=0, tiled=True),
    )
    block_i = (
        lax.all_gather(factor_a, "col", axis=0, tiled=True),
        lax.all_gather(factor_b, "col", axis=0, tiled=True),
        lax.all_gather(factor_c, "col", axis=0, tiled=True),
    )
    lefts = [x for x in block_i]
    summed = lax.psum_scatter(
        block_terms(lefts, block_j).astype(jnp.bfloat16), "col", scatter_dimension=0, tiled=True
    ).astype(jnp.float32)
    cube_a = factor_a.astype(jnp.float32).reshape(own_rows, NMAT, NMAT)
    cube_b = factor_b.astype(jnp.float32).reshape(own_rows, NMAT, NMAT)
    cube_c = factor_c.astype(jnp.float32).reshape(own_rows, NMAT, NMAT)
    data_a = jnp.einsum("rjk,rki->rij", cube_b, cube_c).reshape(own_rows, length)
    data_b = jnp.einsum("rki,rij->rjk", cube_c, cube_a).reshape(own_rows, length)
    data_c = jnp.einsum("rij,rjk->rki", cube_a, cube_b).reshape(own_rows, length)
    grad_a = NMAT * (summed[:, :length] - data_a)
    grad_b = NMAT * (summed[:, length : 2 * length] - data_b)
    grad_c = NMAT * (summed[:, 2 * length :] - data_c)
    return (grad_a, grad_b, grad_c)


def solution(mesh):
    in_specs = (P(("col", "row"), None), P(("col", "row"), None), P(("col", "row"), None))
    out_specs = (P(("col", "row"), None), P(("col", "row"), None), P(("col", "row"), None))
    return jax.shard_map(shards, mesh=mesh, in_specs=in_specs, out_specs=out_specs, check_vma=False)
```

profile of v0, /device:TPU:0, one launch (start us, length us, event | category | flops | bytes accessed | tf_op | source)
XLA Modules:
  0.0 691.9 jit_solution(10488646268790767983)
XLA Ops:
  7.2 0.0 all-gather.17.cloned.1.call-start
  7.2 0.7 all-gather.17.cloned.1.call-update
  7.9 0.0 all-gather.15.cloned.1.call-start
  7.9 0.7 all-gather.15.cloned.1.call-update
  8.6 0.0 all-gather.7.cloned.1.call-start
  8.7 0.7 all-gather.7.cloned.1.call-update
  9.4 0.0 all-gather.9.cloned.1.call-start
  9.4 0.5 all-gather.9.cloned.1.call-update
  10.0 0.0 all-gather.11.cloned.1.call-start
  10.0 0.5 all-gather.11.cloned.1.call-update
  10.5 0.0 all-gather.13.cloned.1.call-start
  10.6 0.5 all-gather.13.cloned.1.call-update
  11.1 0.0 reduce-scatter.2.cloned.1.call-start
  11.2 54.1 %all-gather.17.cloned.1.call-done = bf16[2048,1024]{1,0:T(8,128)(2,1)} async-done(((bf16[512,1024]{1,0:T(8,128)(2,1)}), bf16[2048,1024]{1,0:T(8,128)(2,1)}) %all-gather.17.cloned.1.call-update) | async-done | bytes 4194320 | tf_op jit(solution)/shard_map/all_gather | solution.py:37
  65.3 83.7 %all-gather.15.cloned.1.call-done = bf16[4096,1024]{1,0:T(8,128)(2,1)} async-done(((bf16[512,1024]{1,0:T(8,128)(2,1)}), bf16[4096,1024]{1,0:T(8,128)(2,1)}) %all-gather.15.cloned.1.call-update) | async-done | bytes 8388624 | tf_op jit(solution)/shard_map/all_gather | solution.py:32
  149.0 25.1 %fusion.11 = f32[2048,4096]{1,0:T(8,128)} fusion(bf16[2048,1024]{1,0:T(8,128)(2,1)} %all-gather.17.cloned.1.call-done, bf16[4096,1024]{1,0:T(8,128)(2,1)} %all-gather.15.cloned.1.call-done), kind=kOutput, calls=%fused_computation.18 | convolution fusion | flops 17179869184 | bytes 46137344 | tf_op jit(solution)/shard_map/dot_general | solution.py:10
  174.1 28.0 %all-gather.7.cloned.1.call-done = bf16[2048,1024]{1,0:T(8,128)(2,1)} async-done(((bf16[512,1024]{1,0:T(8,128)(2,1)}), bf16[2048,1024]{1,0:T(8,128)(2,1)}) %all-gather.7.cloned.1.call-update) | async-done | bytes 4194320 | tf_op jit(solution)/shard_map/all_gather | solution.py:38
  202.1 83.5 %all-gather.9.cloned.1.call-done = bf16[4096,1024]{1,0:T(8,128)(2,1)} async-done(((bf16[512,1024]{1,0:T(8,128)(2,1)}), bf16[4096,1024]{1,0:T(8,128)(2,1)}) %all-gather.9.cloned.1.call-update) | async-done | bytes 8388624 | tf_op jit(solution)/shard_map/all_gather | solution.py:33
  285.6 25.2 %fusion.9 = f32[2048,4096]{1,0:T(8,128)} fusion(bf16[2048,1024]{1,0:T(8,128)(2,1)} %all-gather.7.cloned.1.call-done, bf16[4096,1024]{1,0:T(8,128)(2,1)} %all-gather.9.cloned.1.call-done), kind=kOutput, calls=%fused_computation.16 | convolution fusion | flops 17179869184 | bytes 46137344 | tf_op jit(solution)/shard_map/dot_general | solution.py:10
  310.8 27.8 %all-gather.11.cloned.1.call-done = bf16[2048,1024]{1,0:T(8,128)(2,1)} async-done(((bf16[512,1024]{1,0:T(8,128)(2,1)}), bf16[2048,1024]{1,0:T(8,128)(2,1)}) %all-gather.11.cloned.1.call-update) | async-done | bytes 4194320 | tf_op jit(solution)/shard_map/all_gather | solution.py:39
  338.6 83.5 %all-gather.13.cloned.1.call-done = bf16[4096,1024]{1,0:T(8,128)(2,1)} async-done(((bf16[512,1024]{1,0:T(8,128)(2,1)}), bf16[4096,1024]{1,0:T(8,128)(2,1)}) %all-gather.13.cloned.1.call-update) | async-done | bytes 8388624 | tf_op jit(solution)/shard_map/all_gather | solution.py:34
  422.1 25.2 %fusion.10 = f32[2048,4096]{1,0:T(8,128)} fusion(bf16[2048,1024]{1,0:T(8,128)(2,1)} %all-gather.11.cloned.1.call-done, bf16[4096,1024]{1,0:T(8,128)(2,1)} %all-gather.13.cloned.1.call-done), kind=kOutput, calls=%fused_computation.17 | convolution fusion | flops 17179869184 | bytes 46137344 | tf_op jit(solution)/shard_map/dot_general | solution.py:10
  447.4 30.8 %fusion.3 = bf16[2048,1024]{0,1:T(8,128)(2,1)} fusion(bf16[4096,1024]{1,0:T(8,128)(2,1)} %all-gather.13.cloned.1.call-done, f32[2048,4096]{1,0:T(8,128)} %fusion.11, f32[2048,4096]{1,0:T(8,128)} %fusion.9), kind=kOutput, calls=%fused_computation.7 | convolution fusion | flops 17198743552 | bytes 79691776 | tf_op jit(solution)/shard_map/dot_general | solution.py:16
  478.1 30.4 %fusion.4 = bf16[2048,1024]{0,1:T(8,128)(2,1)} fusion(bf16[4096,1024]{1,0:T(8,128)(2,1)} %all-gather.9.cloned.1.call-done, f32[2048,4096]{1,0:T(8,128)} %fusion.10, f32[2048,4096]{1,0:T(8,128)} %fusion.11), kind=kOutput, calls=%fused_computation.8 | convolution fusion | flops 17198743552 | bytes 79691776 | tf_op jit(solution)/shard_map/dot_general | solution.py:16
  508.6 30.8 %fusion.5 = bf16[2048,1024]{0,1:T(8,128)(2,1)} fusion(bf16[4096,1024]{1,0:T(8,128)(2,1)} %all-gather.15.cloned.1.call-done, f32[2048,4096]{1,0:T(8,128)} %fusion.9, f32[2048,4096]{1,0:T(8,128)} %fusion.10), kind=kOutput, calls=%fused_computation.9 | convolution fusion | flops 17198743552 | bytes 79691776 | tf_op jit(solution)/shard_map/dot_general | solution.py:16
  539.4 11.4 %pad_maximum_fusion = bf16[2048,3072]{0,1:T(8,128)(2,1)} fusion(bf16[2048,1024]{0,1:T(8,128)(2,1)} %fusion.3, bf16[2048,1024]{0,1:T(8,128)(2,1)} %fusion.4, bf16[2048,1024]{0,1:T(8,128)(2,1)} %fusion.5), kind=kLoop, calls=%fused_computation.6 | loop fusion | flops 37748736 | bytes 25165824 | tf_op jit(solution)/shard_map/concatenate | solution.py:25
  550.8 0.0 reduce-scatter.2.cloned.1.call-update
  550.9 1.2 copy-done
  552.0 1.3 copy.15
  553.4 0.0 copy-done.1
  553.4 0.5 copy.16
  553.9 1.3 copy.20
  555.2 7.3 %copy.22 = bf16[512,32,32]{2,1,0:T(8,128)(2,1)} copy(bf16[512,32,32]{0,2,1:T(8,128)(2,1)} %bitcast.26) | data formatting | bytes 2097152 | tf_op jit(solution)/shard_map/reshape | solution.py:47
  562.6 6.9 %copy.24 = bf16[512,32,32]{1,2,0:T(8,128)(2,1)} copy(bf16[512,32,32]{0,2,1:T(8,128)(2,1)S(1)} %bitcast.25) | data formatting | bytes 2097152 | tf_op jit(solution)/shard_map/reshape | solution.py:46
  569.5 8.3 %fusion.12 = f32[512,32,32]{2,1,0:T(8,128)} fusion(bf16[512,32,32]{2,1,0:T(8,128)(2,1)} %copy.22, bf16[512,32,32]{1,2,0:T(8,128)(2,1)} %copy.24), kind=kOutput, calls=%fused_computation.19 | convolution fusion | flops 33554432 | bytes 4194304 | tf_op jit(solution)/shard_map/rjk,rki->rij/dot_general | solution.py:48
  577.8 5.6 copy.19
  583.4 6.7 copy.25
  590.1 9.0 %fusion.13 = f32[512,32,32]{2,1,0:T(8,128)} fusion(bf16[512,32,32]{2,1,0:T(8,128)(2,1)} %copy.25, bf16[512,32,32]{2,1,0:T(8,128)(2,1)} %copy.22), kind=kOutput, calls=%fused_computation.20 | convolution fusion | flops 33554432 | bytes 4194304 | tf_op jit(solution)/shard_map/rki,rij->rjk/dot_general | solution.py:49
  599.1 6.5 copy.23
  605.6 9.3 %fusion.14 = f32[512,32,32]{2,1,0:T(8,128)} fusion(bf16[512,32,32]{1,2,0:T(8,128)(2,1)} %copy.24, bf16[512,32,32]{2,1,0:T(8,128)(2,1)} %copy.25), kind=kOutput, calls=%fused_computation.21 | convolution fusion | flops 33554432 | bytes 4194304 | tf_op jit(solution)/shard_map/rij,rjk->rki/dot_general | solution.py:50
  614.9 6.4 copy.26
  621.3 49.0 %reduce-scatter.2.cloned.1.call-done = bf16[512,3072]{0,1:T(8,128)(2,1)} async-done(((bf16[2048,3072]{0,1:T(8,128)(2,1)}), bf16[512,3072]{0,1:T(8,128)(2,1)}) %reduce-scatter.2.cloned.1.call-update) | async-done | bytes 3145744 | tf_op jit(solution)/shard_map/reduce_scatter | solution.py:42
  670.2 2.9 convert_element_type.19
  673.2 0.2 copy-done.4
  673.4 3.5 fusion.6
  676.9 3.0 copy.27
  679.9 2.9 copy.28
  682.8 1.8 copy.29
  (11 shorter events, 0.0 us)
Async XLA Ops:
  7.2 58.1 %all-gather.17.cloned.1.call-start = ((), (), s32[]{:S(2)}) async-start(), calls=%async_computation.6 | async-start | bytes 5242880 | tf_op jit(solution)/shard_map/all_gather | solution.py:37
  7.9 141.1 %all-gather.15.cloned.1.call-start = ((), (), s32[]{:S(2)}) async-start(), calls=%async_computation.5 | async-start | bytes 9437184 | tf_op jit(solution)/shard_map/all_gather | solution.py:32
  8.6 193.4 %all-gather.7.cloned.1.call-start = ((), (), s32[]{:S(2)}) async-start(), calls=%async_computation.1 | async-start | bytes 5242880 | tf_op jit(solution)/shard_map/all_gather | solution.py:38
  9.4 276.3 %all-gather.9.cloned.1.call-start = ((), (), s32[]{:S(2)}) async-start(), calls=%async_computation.2 | async-start | bytes 9437184 | tf_op jit(solution)/shard_map/all_gather | solution.py:33
  10.0 328.6 %all-gather.11.cloned.1.call-start = ((), (), s32[]{:S(2)}) async-start(), calls=%async_computation.3 | async-start | bytes 5242880 | tf_op jit(solution)/shard_map/all_gather | solution.py:39
  10.5 411.6 %all-gather.13.cloned.1.call-start = ((), (), s32[]{:S(2)}) async-start(), calls=%async_computation.4 | async-start | bytes 9437184 | tf_op jit(solution)/shard_map/all_gather | solution.py:34
  11.1 659.1 %reduce-scatter.2.cloned.1.call-start = ((), (), s32[]{:S(2)}) async-start(), calls=%async_computation.7 | async-start | bytes 15728640 | tf_op jit(solution)/shard_map/reduce_scatter | solution.py:42
  550.8 1.2 copy-start
  550.8 2.5 copy-start.1
  550.8 3.1 copy-start.2
  577.8 5.6 copy-start.6
  670.2 2.9 copy-start.3
  670.2 3.2 copy-start.4
  676.9 5.9 copy-start.5
Sparse Core Ops, SparseCore 0:
  9.8 55.3 all-gather.16
  66.9 82.0 all-gather.14
  150.8 51.2 all-gather.6
  203.5 82.0 all-gather.8
  287.3 51.2 all-gather.10
  340.0 82.0 all-gather.12
  551.0 119.1 reduce-scatter.1
where the time goes:
time: 701 us; the launch traced here: 692 us
  waiting for transfers between devices  413 us (59%)
  matrix products  194 us (28%)
  local copies, waits for them, and re-layouts  51.7 us (7%)
  other arithmetic  17.9 us (3%)
  between operations  14.6 us (2%)
    dot_general x3, matrix products, apply_rows(): return jnp.dot(hadam, right, preferred_element_type=jnp.float32)  92 us
    all_gather x1, waiting for transfers between devices, shards(): lax.all_gather(factor_a, 'row', axis=0, tiled=True)  83.7 us
    all_gather x1, waiting for transfers between devices, shards(): lax.all_gather(factor_b, 'row', axis=0, tiled=True)  83.5 us
    all_gather x1, waiting for transfers between devices, shards(): lax.all_gather(factor_c, 'row', axis=0, tiled=True)  83.5 us
    dot_general x3, matrix products, gram_rows(): lax.dot_general(left, right, (((1,), (1,)), ((), ())), preferred_element_...  75.5 us
    all_gather x1, waiting for transfers between devices, shards(): lax.all_gather(factor_a, 'col', axis=0, tiled=True)  54.1 us
    reduce_scatter x1, waiting for transfers between devices, shards(): lax.psum_scatter(block_terms(lefts, block_j).astype(jnp.bfloat16), 'col',...  49 us
    all_gather x1, waiting for transfers between devices, shards(): lax.all_gather(factor_b, 'col', axis=0, tiled=True)  28 us
  transfers between devices with their start and end apart: 7, of which 7 were waited for; matrix products, arithmetic and copies ran while one was open for 17% of the time, Pallas kernels for 0%

commit v1 on v0

--- a/solution.py
+++ b/solution.py
@@ -1,9 +1,281 @@
+import functools
+
 import jax
 import jax.numpy as jnp
 from jax import lax
+from jax.experimental import pallas as pl
+from jax.experimental.pallas import tpu as pltpu
 from jax.sharding import PartitionSpec as P
 
 NMAT = 32
+ROW_TILE = 256
+LANES = 128
+VMEM_BYTES = 60 * 1024 * 1024
+
+
+def trace_kernel(feat, x_ref, out_ref, left, right, prod):
+    blocks = [slice(f * feat, (f + 1) * feat) for f in range(3)]
+    for out, (l, r) in enumerate(((1, 2), (2, 0), (0, 1))):
+        left[...] = x_ref[:, blocks[l]].astype(jnp.float32).T
+        right[...] = x_ref[:, blocks[r]].astype(jnp.float32).T
+
+        def rows(step, carry):
+            base = step * 4
+            sums = [None] * 4
+            for k in range(NMAT):
+                line = right[k * NMAT : (k + 1) * NMAT, :]
+                for n in range(4):
+                    term = left[pl.ds((base + n) * NMAT + k, 1), :] * line
+                    sums[n] = term if k == 0 else sums[n] + term
+            for n in range(4):
+                prod[pl.ds(base + n, NMAT, stride=NMAT), :] = sums[n]
+            return carry
+
+        lax.fori_loop(0, NMAT // 4, rows, 0)
+        out_ref[:, blocks[out]] = -prod[...].T
+
+
+def trace_terms(x):
+    rows, width = x.shape
+    feat = width // 3
+    spec = pl.BlockSpec((LANES, width), lambda i: (i, 0))
+    return pl.pallas_call(
+        functools.partial(trace_kernel, feat),
+        grid=(rows // LANES,),
+        in_specs=[spec],
+        out_specs=spec,
+        out_shape=jax.ShapeDtypeStruct((rows, width), jnp.float32),
+        scratch_shapes=[pltpu.VMEM((feat, LANES), jnp.float32)] * 3,
+        compiler_params=pltpu.CompilerParams(vmem_limit_bytes=VMEM_BYTES),
+        cost_estimate=pl.CostEstimate(flops=rows * feat * NMAT * 6 * 200, bytes_accessed=rows * width * 6, transcendentals=0),
+    )(x)
+
+
+def pair_kernel(feat, i_rows, spans, tile, n_sums, narrow, has_y, *refs):
+    refs = list(refs)
+    take = lambda n: [refs.pop(0) for _ in range(n)]
+    tiles = sum(count for _, count in spans) // tile
+    n_i = sum(i_rows) // ROW_TILE
+    per = n_i // n_sums
+    blocks = [slice(f * feat, (f + 1) * feat) for f in range(3)]
+    i_refs, j_refs = take(len(i_rows)), take(len(spans))
+    y_refs = take(n_sums) if has_y else []
+    out_refs = take(n_i if narrow else n_sums)
+    ibuf, jbuf, acc, i_sem, j_sem, y_sem, o_sem = take(7)
+    packed = take(1)[0] if narrow else None
+
+    def block(i):
+        return pl.ds(i * ROW_TILE, ROW_TILE)
+
+    def fill(buf, sem, sources, ranges, t, size):
+        low = 0
+        for ref, (first, count) in zip(sources, ranges):
+            a, b = max(low, t * size), min(low + count, (t + 1) * size)
+            if a < b:
+                src = ref.at[pl.ds(first + a - low, b - a)]
+                pltpu.make_async_copy(src, buf.at[pl.ds(a, b - a)], sem.at[t]).start()
+            low += count
+
+    fill(jbuf, j_sem, j_refs, spans, 0, tile)
+    for i in range(n_i):
+        fill(ibuf, i_sem, i_refs, [(0, count) for count in i_rows], i, ROW_TILE)
+        if has_y:
+            pltpu.make_async_copy(y_refs[i // per].at[block(i % per)], acc.at[block(i)], y_sem.at[i]).start()
+    for t in range(1, tiles):
+        fill(jbuf, j_sem, j_refs, spans, t, tile)
+
+    def wait(ref, sem):
+        pltpu.make_async_copy(ref, ref, sem).wait()
+
+    def over_tiles(t, carry):
+        cols = pl.ds(pl.multiple_of(t * tile, tile), tile)
+        wait(jbuf.at[cols], j_sem.at[t])
+
+        def over_rows(i, inner):
+            span = pl.ds(pl.multiple_of(i * ROW_TILE, ROW_TILE), ROW_TILE)
+
+            @pl.when(t == 0)
+            def _():
+                wait(ibuf.at[span], i_sem.at[i])
+
+            grams = [
+                lax.dot_general(ibuf[span, b], jbuf[cols, b], (((1,), (1,)), ((), ())), preferred_element_type=jnp.float32)
+                for b in blocks
+            ]
+            hadams = [(grams[(f + 1) % 3] * grams[(f + 2) % 3]).astype(jnp.bfloat16) for f in range(3)]
+
+            @pl.when(t == 0)
+            def _():
+                if has_y:
+                    wait(acc.at[span], y_sem.at[i])
+                else:
+                    acc[span, :] = jnp.zeros((ROW_TILE, 3 * feat), jnp.float32)
+
+            for hadam, b in zip(hadams, blocks):
+                acc[span, b] += jnp.dot(hadam, jbuf[cols, b], preferred_element_type=jnp.float32)
+
+            @pl.when(t == tiles - 1)
+            def _():
+                for n in range(n_i):
+                    @pl.when(i == n)
+                    def _():
+                        if narrow:
+                            packed[block(n), :] = acc[block(n), :].astype(jnp.bfloat16)
+                            src, dst = packed.at[block(n)], out_refs[n]
+                        else:
+                            src, dst = acc.at[block(n)], out_refs[n // per].at[block(n % per)]
+                        pltpu.make_async_copy(src, dst, o_sem.at[n]).start()
+            return inner
+
+        return lax.fori_loop(0, n_i, over_rows, carry)
+
+    lax.fori_loop(0, tiles, over_tiles, 0)
+    for i in range(n_i):
+        wait((packed if narrow else acc).at[block(i)], o_sem.at[i])
+
+
+def pair_sums(lefts, rights, sums, tile, narrow=False):
+    width = lefts[0].shape[1]
+    feat = width // 3
+    i_rows = [v.shape[0] for v in lefts]
+    rows = sum(i_rows)
+    rights = [r if isinstance(r, tuple) else (r, 0, r.shape[0]) for r in rights]
+    spans = [(first, count) for _, first, count in rights]
+    total = sum(count for _, count in spans)
+    assert total % tile == 0 and rows % ROW_TILE == 0
+    n_i = rows // ROW_TILE
+    has_y = sums is not None
+    n_sums = len(sums) if has_y else 1
+    any_spec = pl.BlockSpec(memory_space=pl.ANY)
+    operands = [*lefts, *(r for r, _, _ in rights), *(sums or [])]
+    first_y = len(lefts) + len(rights)
+    if narrow:
+        outs = [jax.ShapeDtypeStruct((ROW_TILE, width), jnp.bfloat16)] * n_i
+    else:
+        outs = [jax.ShapeDtypeStruct((rows // n_sums, width), jnp.float32)] * n_sums
+    scratch = [
+        pltpu.VMEM((rows, width), jnp.bfloat16),
+        pltpu.VMEM((total, width), jnp.bfloat16),
+        pltpu.VMEM((rows, width), jnp.float32),
+        pltpu.SemaphoreType.DMA((n_i,)),
+        pltpu.SemaphoreType.DMA((total // tile,)),
+        pltpu.SemaphoreType.DMA((n_i,)),
+        pltpu.SemaphoreType.DMA((n_i,)),
+    ]
+    if narrow:
+        scratch.append(pltpu.VMEM((rows, width), jnp.bfloat16))
+    return pl.pallas_call(
+        functools.partial(pair_kernel, feat, i_rows, spans, tile, n_sums, narrow, has_y),
+        in_specs=[any_spec] * len(operands),
+        out_specs=[any_spec] * len(outs),
+        out_shape=outs,
+        scratch_shapes=scratch,
+        input_output_aliases={first_y + n: n for n in range(n_sums)} if has_y and not narrow else {},
+        compiler_params=pltpu.CompilerParams(vmem_limit_bytes=VMEM_BYTES),
+        cost_estimate=pl.CostEstimate(flops=rows * total * feat, bytes_accessed=width * total, transcendentals=0),
+    )(*operands)
+
+
+def finish_kernel(feat, home_ref, low_ref, high_ref, *out_refs):
+    def write(back_ref):
+        for f, out in enumerate(out_refs):
+            b = slice(f * feat, (f + 1) * feat)
+            out[...] = NMAT * (home_ref[:, b] + back_ref[:, b].astype(jnp.float32))
+
+    steps = pl.num_programs(0) // 2
+    pl.when(pl.program_id(0) < steps)(lambda: write(low_ref))
+    pl.when(pl.program_id(0) >= steps)(lambda: write(high_ref))
+
+
+def finish(home, low, high):
+    rows, width = home.shape
+    feat = width // 3
+    steps = low.shape[0] // LANES
+    return pl.pallas_call(
+        functools.partial(finish_kernel, feat),
+        grid=(2 * steps,),
+        in_specs=[
+            pl.BlockSpec((LANES, width), lambda i: (i, 0)),
+            pl.BlockSpec((LANES, width), lambda i: (jnp.minimum(i, steps - 1), 0)),
+            pl.BlockSpec((LANES, width), lambda i: (jnp.maximum(i - steps, 0), 0)),
+        ],
+        out_specs=[pl.BlockSpec((LANES, feat), lambda i: (i, 0))] * 3,
+        out_shape=[jax.ShapeDtypeStruct((rows, feat), jnp.float32)] * 3,
+        compiler_params=pltpu.CompilerParams(vmem_limit_bytes=VMEM_BYTES),
+        cost_estimate=pl.CostEstimate(flops=rows * width, bytes_accessed=rows * width * 10, transcendentals=0),
+    )(home, low, high)
+
+
+def near_shards(factor_a, factor_b, factor_c):
+    x = jnp.concatenate([factor_a, factor_b, factor_c], axis=1)
+    rows = x.shape[0]
+    early = rows * 5 // 8
+    row = lax.axis_index("row")
+    inner = (row >= 2) & (row < 6)
+    fence = lax.optimization_barrier
+
+    def move(axis, pairs):
+        return lambda v: lax.ppermute(v, axis, pairs)
+
+    core = move("row", [(r, r ^ 1) for r in range(8)])
+    partner = move("row", [(r, r ^ 2) for r in range(8)])
+    across = move("row", [(2, 4), (3, 5), (4, 2), (5, 3)])
+    outward = move("row", [(2, 0), (3, 1), (4, 6), (5, 7)])
+    along_x = move("col", [(c, c ^ 1) for c in range(4)])
+    along_y = move("col", [(c, c ^ 2) for c in range(4)])
+
+    def corner(from_x, from_y):
+        mid = from_x.shape[0] // 2
+        return along_x(from_y[:mid]), along_y(from_x[mid:])
+
+    x_x, x_y, x_s = along_x(x), along_y(x), core(x)
+    part_a, part_c = x[:early], x[early:]
+    guest_a, far_a = partner(part_a), across(part_a)
+    home = trace_terms(x)
+    (home,) = pair_sums([x], [x, x_s], [home], 1024)
+    guest_a, far_a, part_c, home = fence((guest_a, far_a, part_c, home))
+
+    guest_c, far_c = partner(part_c), across(part_c)
+    x_x, x_y, guest_c, far_c = fence((x_x, x_y, guest_c, far_c))
+
+    guest = [guest_a, guest_c]
+    x_d0, x_d1 = corner(x_x, x_y)
+    out_a, next_b = outward(far_a), across(guest_a)
+    x_xs, x_ys = core(x_x), core(x_y)
+    (visit,) = pair_sums(guest, [x, x_s, x_x, x_y, x_xs, x_ys], None, 1024)
+    x_d0, x_d1, out_a, next_b, visit = fence((x_d0, x_d1, out_a, next_b, visit))
+
+    e = jnp.where(inner, next_b, out_a)
+    e_x, e_y = along_x(e), along_y(e)
+    out_c0, next_c = outward(far_c), across(guest_c)
+    x_ds0, x_ds1, e_s = fence((core(x_d0), core(x_d1), core(e)))
+    x_d = [x_d0, x_d1, x_ds0, x_ds1]
+    (home,) = pair_sums([x], [x_x, x_y, x_xs, x_ys, *x_d], [home], 1024)
+    e_x, e_y, next_c, home = fence((e_x, e_y, next_c, home))
+
+    e_d0, e_d1 = corner(e_x, e_y)
+    out_c1 = outward(next_c)
+    e_xs, e_ys = fence((core(e_x), core(e_y)))
+    lead = 3 * rows - 4 * early
+    (visit,) = pair_sums(guest, [*x_d, e, e_s, e_x, e_y, (e_xs, 0, lead)], [visit], 1280)
+    e_d0, e_d1, out_c0, out_c1, visit = fence((e_d0, e_d1, out_c0, out_c1, visit))
+
+    c = jnp.where(inner, jnp.concatenate([far_c, next_c]), jnp.concatenate([out_c0, out_c1]))
+    c_x, c_y = along_x(c), along_y(c)
+    e_ds0, e_ds1, c_s = fence((core(e_d0), core(e_d1), core(c)))
+    e_d = [e_d0, e_d1, e_ds0, e_ds1]
+    visit_0, visit_1 = pair_sums(guest, [(e_xs, lead, early - lead), e_ys, *e_d], [visit], 1024, narrow=True)
+    visit_0, visit_1, home = fence((visit_0, visit_1, home))
+    back_0 = partner(visit_0)
+    (home,) = pair_sums([x], [e, e_s, e_x, e_y, e_xs, e_ys, *e_d], [home], 1280)
+    c_x, c_y, back_0, visit_1, home = fence((c_x, c_y, back_0, visit_1, home))
+
+    back_1 = partner(visit_1)
+    c_d0, c_d1 = corner(c_x, c_y)
+    (home,) = pair_sums([x], [c, c_s, c_x, c_y, core(c_x), core(c_y)], [home], 768)
+    c_d0, c_d1, home = fence((c_d0, c_d1, home))
+    (home,) = pair_sums([x], [c_d0, c_d1, core(c_d0), core(c_d1)], [home], 768)
+    return tuple(finish(home, back_0, back_1))
 
 
 def gram_rows(left, right):
@@ -55,6 +327,8 @@
 
 
 def solution(mesh):
-    in_specs = (P(("col", "row"), None), P(("col", "row"), None), P(("col", "row"), None))
-    out_specs = (P(("col", "row"), None), P(("col", "row"), None), P(("col", "row"), None))
-    return jax.shard_map(shards, mesh=mesh, in_specs=in_specs, out_specs=out_specs, check_vma=False)
+    spec = P(("col", "row"), None)
+    near = (mesh.shape["row"], mesh.shape["col"]) == (8, 4)
+    return jax.shard_map(
+        near_shards if near else shards, mesh=mesh, in_specs=(spec,) * 3, out_specs=(spec,) * 3, check_vma=False
+    )

time: 701 us -> 360 us (0.51); the launches traced: 692 us -> 359 us
  waiting for transfers between devices: 413 us -> 93.6 us
  Pallas kernels: 0 us -> 201 us
  matrix products: 194 us -> 0 us
  starting transfers between devices: 0.27 us -> 37.6 us
  local copies, waits for them, and re-layouts: 51.7 us -> 22.1 us
  between operations: 14.6 us -> 0.94 us
  other arithmetic: 17.9 us -> 4.42 us
    all_gather x6 -> x0, waiting for transfers between devices: 361 us -> none  [the longest x1 83.7 us: shards(): lax.all_gather(factor_a, 'row', axis=0, tiled=True)]
    pallas_call x0 -> x10, Pallas kernels: none -> 201 us  [the longest x8 170 us: pair_sums(): pl.pallas_call(functools.partial(pair_kernel, feat, i_rows, spans, tile,...]
    dot_general x9 -> x0, matrix products: 194 us -> none  [the longest x3 92 us: apply_rows(): return jnp.dot(hadam, right, preferred_element_type=jnp.float32)]
    ppermute x0 -> x38, waiting for transfers between devices: none -> 93.6 us  [move(): return lambda v: lax.ppermute(v, axis, pairs)]
    reduce_scatter x1 -> x0, waiting for transfers between devices: 49 us -> none  [shards(): lax.psum_scatter(block_terms(lefts, block_j).astype(jnp.bfloat16), 'col',...]
    ppermute x0 -> x38, starting transfers between devices: none -> 37.6 us  [move(): return lambda v: lax.ppermute(v, axis, pairs)]
    reshape x3 -> x0, local copies, waits for them, and re-layouts: 21 us -> none  [the longest x1 7.32 us: shards(): cube_c = factor_c.astype(jnp.float32).reshape(own_rows, NMAT, NMAT)]
    dot_general x3 -> x0, local copies, waits for them, and re-layouts: 18.4 us -> none  [the longest x1 6.45 us: shards(): jnp.einsum('rki,rij->rjk', cube_c, cube_a).reshape(own_rows, length)]
  transfers between devices with their start and end apart: 7 -> 38, of which waited for: 7 -> 18; matrix products, arithmetic and copies ran while one was open for 17% -> 5% of each run, Pallas kernels for 0% -> 54%
where the time goes in v1:
time: 360 us; the launch traced here: 359 us
  Pallas kernels  201 us (56%)
  waiting for transfers between devices  93.6 us (26%)
  starting transfers between devices  37.6 us (10%)
  local copies, waits for them, and re-layouts  22.1 us (6%)
  other arithmetic  4.42 us (1%)
    pallas_call x8, Pallas kernels, pair_sums(): pl.pallas_call(functools.partial(pair_kernel, feat, i_rows, spans, tile,...  170 us
    ppermute x38, waiting for transfers between devices, move(): return lambda v: lax.ppermute(v, axis, pairs)  93.6 us
    ppermute x38, starting transfers between devices, move(): return lambda v: lax.ppermute(v, axis, pairs)  37.6 us
    pallas_call x1, Pallas kernels, trace_terms(): pl.pallas_call(functools.partial(trace_kernel, feat), grid=(rows // LANES...  23.9 us
    slice x6, local copies, waits for them, and re-layouts, corner(): return (along_x(from_y[:mid]), along_y(from_x[mid:]))  13.3 us
  transfers between devices with their start and end apart: 38, of which 18 were waited for; matrix products, arithmetic and copies ran while one was open for 5% of the time, Pallas kernels for 54%

profile of v1, /device:TPU:0, one launch (start us, length us, event | category | flops | bytes accessed | tf_op | source)
XLA Modules:
  0.0 359.3 jit_solution(3531282611773116724)
XLA Ops:
  0.7 1.4 constant_dynamic-update-slice_fusion.2
  3.1 1.8 slice.32
  4.9 2.3 collective-permute-start.2
  7.2 1.9 collective-permute-start.3
  9.1 1.5 collective-permute-start
  10.6 1.5 collective-permute-start.1
  13.2 23.9 %shard_map.58.refs_3_ = f32[512,3072]{1,0:T(8,128)} custom-call(bf16[512,3072]{1,0:T(8,128)(2,1)} %copy-done), custom_call_target="tpu_custom_call" | custom-call | flops 20132659200 | bytes 9437184 | tf_op jit(solution)/shard_map/pallas_call | solution.py:42
  37.1 13.3 %shard_map.59.refs_9_ = f32[512,3072]{1,0:T(8,128)} custom-call(bf16[512,3072]{1,0:T(8,128)(2,1)} %copy-done, bf16[512,3072]{1,0:T(8,128)(2,1)} %copy-done, bf16[512,3072]{1,0:T(8,128)(2,1)} %collective-permute-done.4.refs_2_.refs_3_, f32[512,3072]{1,0:T(8,128)} %shard_map.58.refs_3_), custom_call_target="tpu_custom_call", output_to_operand_aliasing={{}: (3, {})} | custom-call | flops 536870912 | bytes 3145728 | tf_op jit(solution)/shard_map/pallas_call | solution.py:167
  51.0 4.8 %collective-permute-start.5 = (bf16[192,3072]{1,0:T(8,128)(2,1)}, bf16[192,3072]{1,0:T(8,128)(2,1)}, u32[]{:S(2)}, u32[]{:S(2)}) collective-permute-start(bf16[192,3072]{1,0:T(8,128)(2,1)} %slice.33), channel_id=1, source_target_pairs={{0,8},{4,12},{8,0},{12,4},{16,24},{20,28},{24,16},{28,20},{1,9},{5... | collective-permute-start | bytes 3538952 | tf_op jit(solution)/shard_map/ppermute | solution.py:218
  55.8 1.7 collective-permute-start.6
  57.5 22.0 %collective-permute-done.refs_4_.refs_1_ = bf16[512,3072]{1,0:T(8,128)(2,1)} collective-permute-done((bf16[512,3072]{1,0:T(8,128)(2,1)S(1)}, bf16[512,3072]{1,0:T(8,128)(2,1)}, u32[]{:S(2)}, u32[]{:S(2)}) %collective-permute-start) | collective-permute-done | bytes 3145760 | tf_op jit(solution)/shard_map/ppermute | solution.py:218
  80.7 1.3 collective-permute-done.5.refs_1_
  82.5 2.0 collective-permute-start.10
  84.5 1.3 collective-permute-start.9
  85.8 2.7 slice.26
  88.4 2.7 slice.27
  91.1 1.5 collective-permute-start.7
  92.6 1.5 collective-permute-start.8
  94.2 28.1 %shard_map.60.refs_11_ = f32[512,3072]{1,0:T(8,128)} custom-call(bf16[320,3072]{1,0:T(8,128)(2,1)} %collective-permute-done.2.refs_0_, bf16[192,3072]{1,0:T(8,128)(2,1)} %collective-permute-done.5.refs_1_, bf16[512,3072]{1,0:T(8,128)(2,1)} %copy-done, bf16[512,3072]{1,0:T(8,128)(2,1)} %collective-permute-done.4.refs_2_.refs_3_, ...), custom_call_target="tpu_custom_call" | custom-call | flops 1610612736 | bytes 9437184 | tf_op jit(solution)/shard_map/pallas_call | solution.py:167
  122.3 11.4 %collective-permute-done.9 = bf16[320,3072]{1,0:T(8,128)(2,1)} collective-permute-done((bf16[320,3072]{1,0:T(8,128)(2,1)}, bf16[320,3072]{1,0:T(8,128)(2,1)}, u32[]{:S(2)}, u32[]{:S(2)}) %collective-permute-start.9) | collective-permute-done | bytes 1966112 | tf_op jit(solution)/shard_map/ppermute | solution.py:218
  133.8 1.8 broadcast_select_fusion.refs_6_.refs_1_
  136.1 1.5 collective-permute-start.13
  137.6 1.5 collective-permute-start.14
  139.1 1.7 collective-permute-start.15
  140.8 2.1 collective-permute-done.17.refs_8_.refs_5_
  142.9 29.6 %shard_map.61.refs_11_ = f32[512,3072]{1,0:T(8,128)} custom-call(bf16[512,3072]{1,0:T(8,128)(2,1)} %copy-done, bf16[512,3072]{1,0:T(8,128)(2,1)} %collective-permute-done.refs_4_.refs_1_, bf16[512,3072]{1,0:T(8,128)(2,1)} %collective-permute-done.1.refs_5_.refs_2_, bf16[512,3072]{1,0:T(8,128)(2,1)} %copy-done.3, ...), custom_call_target="tpu_custom_call", output_to_operand_aliasing={{}: (9, {})} | custom-call | flops 1610612736 | bytes 9437184 | tf_op jit(solution)/shard_map/pallas_call | solution.py:167
  172.5 8.4 %collective-permute-done.13.refs_8_.refs_3_ = bf16[320,3072]{1,0:T(8,128)(2,1)S(1)} collective-permute-done((bf16[320,3072]{1,0:T(8,128)(2,1)S(1)}, bf16[320,3072]{1,0:T(8,128)(2,1)S(1)}, u32[]{:S(2)}, u32[]{:S(2)}) %collective-permute-start.13) | collective-permute-done | bytes 1966112 | tf_op jit(solution)/shard_map/ppermute | solution.py:218
  180.9 1.3 collective-permute-done.14.refs_9_.refs_4_
  184.0 1.3 collective-permute-start.22
  185.3 2.2 slice.28
  189.1 1.5 collective-permute-start.20
  190.6 24.0 %shard_map.62.refs_8_ = f32[512,3072]{1,0:T(8,128)} custom-call(bf16[320,3072]{1,0:T(8,128)(2,1)} %collective-permute-done.2.refs_0_, bf16[192,3072]{1,0:T(8,128)(2,1)} %collective-permute-done.5.refs_1_, bf16[256,3072]{1,0:T(8,128)(2,1)} %collective-permute-done.7.refs_5_.refs_2_, ...), custom_call_target="tpu_custom_call", output_to_operand_aliasing={{}: (11, {})} | custom-call | flops 1342177280 | bytes 7864320 | tf_op jit(solution)/shard_map/pallas_call | solution.py:167
  214.6 23.5 %collective-permute-done.22 = bf16[192,3072]{1,0:T(8,128)(2,1)} collective-permute-done((bf16[192,3072]{1,0:T(8,128)(2,1)}, bf16[192,3072]{1,0:T(8,128)(2,1)}, u32[]{:S(2)}, u32[]{:S(2)}) %collective-permute-start.22) | collective-permute-done | bytes 1179680 | tf_op jit(solution)/shard_map/ppermute | solution.py:218
  238.1 2.7 maximum_select_fusion.refs_1_
  241.9 1.5 collective-permute-start.26
  243.5 4.5 %collective-permute-done.27.refs_6_.refs_9_ = bf16[160,3072]{1,0:T(8,128)(2,1)S(1)} collective-permute-done((bf16[160,3072]{1,0:T(8,128)(2,1)}, bf16[160,3072]{1,0:T(8,128)(2,1)S(1)}, u32[]{:S(2)}, u32[]{:S(2)}) %collective-permute-start.27) | collective-permute-done | bytes 983072 | tf_op jit(solution)/shard_map/ppermute | solution.py:218
  249.0 13.1 %shard_map.63 = (bf16[256,3072]{1,0:T(8,128)(2,1)}, bf16[256,3072]{1,0:T(8,128)(2,1)}) custom-call(bf16[320,3072]{1,0:T(8,128)(2,1)} %collective-permute-done.2.refs_0_, bf16[192,3072]{1,0:T(8,128)(2,1)} %collective-permute-done.5.refs_1_, bf16[320,3072]{1,0:T(8,128)(2,1)} %copy-done.2, bf16[320,3072]{1,0:T(8,128)(2,1)} %collective-permute-done.24.refs_3_.refs_6_, ...), custom_call_target="tpu_custom_call" | custom-call | flops 536870912 | bytes 3145728 | tf_op jit(solution)/shard_map/pallas_call | solution.py:167
  262.2 25.0 %shard_map.64.refs_7_ = f32[512,3072]{1,0:T(8,128)} custom-call(bf16[512,3072]{1,0:T(8,128)(2,1)} %copy-done, bf16[320,3072]{1,0:T(8,128)(2,1)} %copy-done.1, bf16[320,3072]{1,0:T(8,128)(2,1)} %collective-permute-done.18.refs_7_.refs_2_, bf16[320,3072]{1,0:T(8,128)(2,1)} %copy-done.4, ...), custom_call_target="tpu_custom_call", output_to_operand_aliasing={{}: (11, {})} | custom-call | flops 1342177280 | bytes 7864320 | tf_op jit(solution)/shard_map/pallas_call | solution.py:167
  287.2 7.9 %collective-permute-done.25.refs_3_ = bf16[384,3072]{1,0:T(8,128)(2,1)} collective-permute-done((bf16[384,3072]{1,0:T(8,128)(2,1)S(1)}, bf16[384,3072]{1,0:T(8,128)(2,1)}, u32[]{:S(2)}, u32[]{:S(2)}) %collective-permute-start.25) | collective-permute-done | bytes 2359328 | tf_op jit(solution)/shard_map/ppermute | solution.py:218
  295.4 3.7 %collective-permute-done.30.low_ref = bf16[256,3072]{1,0:T(8,128)(2,1)S(1)} collective-permute-done((bf16[256,3072]{1,0:T(8,128)(2,1)}, bf16[256,3072]{1,0:T(8,128)(2,1)S(1)}, u32[]{:S(2)}, u32[]{:S(2)}) %collective-permute-start.30) | collective-permute-done | bytes 1572896 | tf_op jit(solution)/shard_map/ppermute | solution.py:218
  299.5 2.4 slice.30
  301.9 2.4 slice.31
  304.8 1.5 collective-permute-start.32
  308.6 25.3 %shard_map.65.refs_5_ = f32[512,3072]{1,0:T(8,128)} custom-call(bf16[512,3072]{1,0:T(8,128)(2,1)} %copy-done, bf16[384,3072]{1,0:T(8,128)(2,1)} %copy-done.5, bf16[384,3072]{1,0:T(8,128)(2,1)} %collective-permute-done.29.refs_2_, bf16[384,3072]{1,0:T(8,128)(2,1)} %collective-permute-done.25.refs_3_, ...), custom_call_target="tpu_custom_call", output_to_operand_aliasing={{}: (7, {})} | custom-call | flops 1207959552 | bytes 7077888 | tf_op jit(solution)/shard_map/pallas_call | solution.py:167
  334.4 2.5 collective-permute-done.35.refs_3_
  337.0 1.7 collective-permute-done.36.refs_4_
  339.7 11.9 %shard_map.66.home_ref = f32[512,3072]{1,0:T(8,128)} custom-call(bf16[512,3072]{1,0:T(8,128)(2,1)} %copy-done, bf16[192,3072]{1,0:T(8,128)(2,1)} %collective-permute-done.31.refs_1_, bf16[192,3072]{1,0:T(8,128)(2,1)} %collective-permute-done.32.refs_2_, bf16[192,3072]{1,0:T(8,128)(2,1)} %copy-done.10, ...), custom_call_target="tpu_custom_call", output_to_operand_aliasing={{}: (5, {})} | custom-call | flops 402653184 | bytes 2359296 | tf_op jit(solution)/shard_map/pallas_call | solution.py:167
  352.8 6.5 %shard_map.67 = (f32[512,1024]{1,0:T(8,128)}, f32[512,1024]{1,0:T(8,128)}, f32[512,1024]{1,0:T(8,128)}) custom-call(f32[512,3072]{1,0:T(8,128)} %shard_map.66.home_ref, bf16[256,3072]{1,0:T(8,128)(2,1)} %copy-done.8, bf16[256,3072]{1,0:T(8,128)(2,1)} %copy-done.9), custom_call_target="tpu_custom_call" | custom-call | flops 1572864 | bytes 15728640 | tf_op jit(solution)/shard_map/pallas_call | solution.py:194
  (79 shorter events, 16.9 us)
Async XLA Ops:
  0.6 1.5 copy-start.12
  0.6 1.8 copy-start.13
  2.6 10.7 %copy-start = (bf16[512,3072]{1,0:T(8,128)(2,1)}, bf16[512,3072]{1,0:T(8,128)(2,1)S(1)}, u32[]{:S(2)}) copy-start(bf16[512,3072]{1,0:T(8,128)(2,1)S(1)} %constant_dynamic-update-slice_fusion.x_ref.refs_0_.refs_1_.refs_2_) | copy-start | bytes 9437188
  2.6 34.6 %collective-permute-start.4 = (bf16[512,3072]{1,0:T(8,128)(2,1)S(1)}, bf16[512,3072]{1,0:T(8,128)(2,1)}, u32[]{:S(2)}, u32[]{:S(2)}) collective-permute-start(bf16[512,3072]{1,0:T(8,128)(2,1)S(1)} %constant_dynamic-update-slice_fusion.x_ref.refs_0_.refs_1_.refs_2_), channel_id=1, source_target_pairs={{0,4},{4,0},{8,12},{12,8},{16,20},{20,16},{24,28},{28,24},{1,5},{5... | collective-permute-start | bytes 9437192 | tf_op jit(solution)/shard_map/ppermute | solution.py:218
  4.9 46.2 %collective-permute-start.2 = (bf16[320,3072]{1,0:T(8,128)(2,1)}, bf16[320,3072]{1,0:T(8,128)(2,1)}, u32[]{:S(2)}, u32[]{:S(2)}) collective-permute-start(bf16[320,3072]{1,0:T(8,128)(2,1)} %slice.32), channel_id=1, source_target_pairs={{0,8},{4,12},{8,0},{12,4},{16,24},{20,28},{24,16},{28,20},{1,9},{5... | collective-permute-start | bytes 5898248 | tf_op jit(solution)/shard_map/ppermute | solution.py:218
  7.2 43.8 %collective-permute-start.3 = (bf16[320,3072]{1,0:T(8,128)(2,1)}, bf16[320,3072]{1,0:T(8,128)(2,1)}, u32[]{:S(2)}, u32[]{:S(2)}) collective-permute-start(bf16[320,3072]{1,0:T(8,128)(2,1)} %slice.32), channel_id=1, source_target_pairs={{8,16},{12,20},{16,8},{20,12},{9,17},{13,21},{17,9},{21,13},{10,18... | collective-permute-start | bytes 5898248 | tf_op jit(solution)/shard_map/ppermute | solution.py:218
  9.1 70.3 %collective-permute-start = (bf16[512,3072]{1,0:T(8,128)(2,1)S(1)}, bf16[512,3072]{1,0:T(8,128)(2,1)}, u32[]{:S(2)}, u32[]{:S(2)}) collective-permute-start(bf16[512,3072]{1,0:T(8,128)(2,1)S(1)} %constant_dynamic-update-slice_fusion.x_ref.refs_0_.refs_1_.refs_2_), channel_id=1, source_target_pairs={{0,1},{1,0},{2,3},{3,2},{4,5},{5,4},{6,7},{7,6},{8,9},{9,8},{10,11... | collective-permute-start | bytes 9437192 | tf_op jit(solution)/shard_map/ppermute | solution.py:218
  10.6 70.1 %collective-permute-start.1 = (bf16[512,3072]{1,0:T(8,128)(2,1)S(1)}, bf16[512,3072]{1,0:T(8,128)(2,1)}, u32[]{:S(2)}, u32[]{:S(2)}) collective-permute-start(bf16[512,3072]{1,0:T(8,128)(2,1)S(1)} %constant_dynamic-update-slice_fusion.x_ref.refs_0_.refs_1_.refs_2_), channel_id=1, source_target_pairs={{0,2},{1,3},{2,0},{3,1},{4,6},{5,7},{6,4},{7,5},{8,10},{9,11},{10,... | collective-permute-start | bytes 9437192 | tf_op jit(solution)/shard_map/ppermute | solution.py:218
  51.0 30.9 %collective-permute-start.5 = (bf16[192,3072]{1,0:T(8,128)(2,1)}, bf16[192,3072]{1,0:T(8,128)(2,1)}, u32[]{:S(2)}, u32[]{:S(2)}) collective-permute-start(bf16[192,3072]{1,0:T(8,128)(2,1)} %slice.33), channel_id=1, source_target_pairs={{0,8},{4,12},{8,0},{12,4},{16,24},{20,28},{24,16},{28,20},{1,9},{5... | collective-permute-start | bytes 3538952 | tf_op jit(solution)/shard_map/ppermute | solution.py:218
  55.8 26.2 %collective-permute-start.6 = (bf16[192,3072]{1,0:T(8,128)(2,1)}, bf16[192,3072]{1,0:T(8,128)(2,1)}, u32[]{:S(2)}, u32[]{:S(2)}) collective-permute-start(bf16[192,3072]{1,0:T(8,128)(2,1)} %slice.33), channel_id=1, source_target_pairs={{8,16},{12,20},{16,8},{20,12},{9,17},{13,21},{17,9},{21,13},{10,18... | collective-permute-start | bytes 3538952 | tf_op jit(solution)/shard_map/ppermute | solution.py:218
  82.0 10.6 %collective-permute-start.11 = (bf16[512,3072]{1,0:T(8,128)(2,1)}, bf16[512,3072]{1,0:T(8,128)(2,1)S(1)}, u32[]{:S(2)}, u32[]{:S(2)}) collective-permute-start(bf16[512,3072]{1,0:T(8,128)(2,1)} %collective-permute-done.refs_4_.refs_1_), channel_id=1, source_target_pairs={{0,4},{4,0},{8,12},{12,8},{16,20},{20,16},{24,28},{28,24},{1,5},{5... | collective-permute-start | bytes 9437192 | tf_op jit(solution)/shard_map/ppermute | solution.py:218
  82.0 12.1 %collective-permute-start.12 = (bf16[512,3072]{1,0:T(8,128)(2,1)}, bf16[512,3072]{1,0:T(8,128)(2,1)}, u32[]{:S(2)}, u32[]{:S(2)}) collective-permute-start(bf16[512,3072]{1,0:T(8,128)(2,1)} %collective-permute-done.1.refs_5_.refs_2_), channel_id=1, source_target_pairs={{0,4},{4,0},{8,12},{12,8},{16,20},{20,16},{24,28},{28,24},{1,5},{5... | collective-permute-start | bytes 9437192 | tf_op jit(solution)/shard_map/ppermute | solution.py:218
  82.5 39.8 %collective-permute-start.10 = (bf16[320,3072]{1,0:T(8,128)(2,1)}, bf16[320,3072]{1,0:T(8,128)(2,1)}, u32[]{:S(2)}, u32[]{:S(2)}) collective-permute-start(bf16[320,3072]{1,0:T(8,128)(2,1)} %collective-permute-done.2.refs_0_), channel_id=1, source_target_pairs={{8,16},{12,20},{16,8},{20,12},{9,17},{13,21},{17,9},{21,13},{10,18... | collective-permute-start | bytes 5898248 | tf_op jit(solution)/shard_map/ppermute | solution.py:218
  84.5 49.3 %collective-permute-start.9 = (bf16[320,3072]{1,0:T(8,128)(2,1)}, bf16[320,3072]{1,0:T(8,128)(2,1)}, u32[]{:S(2)}, u32[]{:S(2)}) collective-permute-start(bf16[320,3072]{1,0:T(8,128)(2,1)} %collective-permute-done.3), channel_id=1, source_target_pairs={{8,0},{12,4},{16,24},{20,28},{9,1},{13,5},{17,25},{21,29},{10,2},{... | collective-permute-start | bytes 5898248 | tf_op jit(solution)/shard_map/ppermute | solution.py:218
  91.1 42.7 %collective-permute-start.7 = (bf16[256,3072]{1,0:T(8,128)(2,1)}, bf16[256,3072]{1,0:T(8,128)(2,1)}, u32[]{:S(2)}, u32[]{:S(2)}) collective-permute-start(bf16[256,3072]{1,0:T(8,128)(2,1)} %slice.26), channel_id=1, source_target_pairs={{0,1},{1,0},{2,3},{3,2},{4,5},{5,4},{6,7},{7,6},{8,9},{9,8},{10,11... | collective-permute-start | bytes 4718600 | tf_op jit(solution)/shard_map/ppermute | solution.py:218
  92.5 1.6 copy-start.3
  92.6 41.2 %collective-permute-start.8 = (bf16[256,3072]{1,0:T(8,128)(2,1)}, bf16[256,3072]{1,0:T(8,128)(2,1)}, u32[]{:S(2)}, u32[]{:S(2)}) collective-permute-start(bf16[256,3072]{1,0:T(8,128)(2,1)} %slice.27), channel_id=1, source_target_pairs={{0,2},{1,3},{2,0},{3,1},{4,6},{5,7},{6,4},{7,5},{8,10},{9,11},{10,... | collective-permute-start | bytes 4718600 | tf_op jit(solution)/shard_map/ppermute | solution.py:218
  133.7 5.4 %collective-permute-start.16 = (bf16[256,3072]{1,0:T(8,128)(2,1)}, bf16[256,3072]{1,0:T(8,128)(2,1)}, u32[]{:S(2)}, u32[]{:S(2)}) collective-permute-start(bf16[256,3072]{1,0:T(8,128)(2,1)} %collective-permute-done.7.refs_5_.refs_2_), channel_id=1, source_target_pairs={{0,4},{4,0},{8,12},{12,8},{16,20},{20,16},{24,28},{28,24},{1,5},{5... | collective-permute-start | bytes 4718600 | tf_op jit(solution)/shard_map/ppermute | solution.py:218
  135.5 36.9 %copy-start.1 = (bf16[320,3072]{1,0:T(8,128)(2,1)}, bf16[320,3072]{1,0:T(8,128)(2,1)S(1)}, u32[]{:S(2)}) copy-start(bf16[320,3072]{1,0:T(8,128)(2,1)S(1)} %broadcast_select_fusion.refs_6_.refs_1_) | copy-start | bytes 5898244
  135.5 7.3 %collective-permute-start.18 = (bf16[320,3072]{1,0:T(8,128)(2,1)S(1)}, bf16[320,3072]{1,0:T(8,128)(2,1)}, u32[]{:S(2)}, u32[]{:S(2)}) collective-permute-start(bf16[320,3072]{1,0:T(8,128)(2,1)S(1)} %broadcast_select_fusion.refs_6_.refs_1_), channel_id=1, source_target_pairs={{0,4},{4,0},{8,12},{12,8},{16,20},{20,16},{24,28},{28,24},{1,5},{5... | collective-permute-start | bytes 5898248 | tf_op jit(solution)/shard_map/ppermute | solution.py:218
  136.1 44.8 %collective-permute-start.13 = (bf16[320,3072]{1,0:T(8,128)(2,1)S(1)}, bf16[320,3072]{1,0:T(8,128)(2,1)S(1)}, u32[]{:S(2)}, u32[]{:S(2)}) collective-permute-start(bf16[320,3072]{1,0:T(8,128)(2,1)S(1)} %broadcast_select_fusion.refs_6_.refs_1_), channel_id=1, source_target_pairs={{0,1},{1,0},{2,3},{3,2},{4,5},{5,4},{6,7},{7,6},{8,9},{9,8},{10,11... | collective-permute-start | bytes 5898248 | tf_op jit(solution)/shard_map/ppermute | solution.py:218
  137.6 44.6 %collective-permute-start.14 = (bf16[320,3072]{1,0:T(8,128)(2,1)S(1)}, bf16[320,3072]{1,0:T(8,128)(2,1)}, u32[]{:S(2)}, u32[]{:S(2)}) collective-permute-start(bf16[320,3072]{1,0:T(8,128)(2,1)S(1)} %broadcast_select_fusion.refs_6_.refs_1_), channel_id=1, source_target_pairs={{0,2},{1,3},{2,0},{3,1},{4,6},{5,7},{6,4},{7,5},{8,10},{9,11},{10,... | collective-permute-start | bytes 5898248 | tf_op jit(solution)/shard_map/ppermute | solution.py:218
  139.1 3.8 %collective-permute-start.17 = (bf16[256,3072]{1,0:T(8,128)(2,1)}, bf16[256,3072]{1,0:T(8,128)(2,1)}, u32[]{:S(2)}, u32[]{:S(2)}) collective-permute-start(bf16[256,3072]{1,0:T(8,128)(2,1)} %collective-permute-done.8.refs_6_.refs_3_), channel_id=1, source_target_pairs={{0,4},{4,0},{8,12},{12,8},{16,20},{20,16},{24,28},{28,24},{1,5},{5... | collective-permute-start | bytes 4718600 | tf_op jit(solution)/shard_map/ppermute | solution.py:218
  139.1 33.4 %collective-permute-start.15 = (bf16[192,3072]{1,0:T(8,128)(2,1)}, bf16[192,3072]{1,0:T(8,128)(2,1)}, u32[]{:S(2)}, u32[]{:S(2)}) collective-permute-start(bf16[192,3072]{1,0:T(8,128)(2,1)} %collective-permute-done.5.refs_1_), channel_id=1, source_target_pairs={{8,16},{12,20},{16,8},{20,12},{9,17},{13,21},{17,9},{21,13},{10,18... | collective-permute-start | bytes 3538952 | tf_op jit(solution)/shard_map/ppermute | solution.py:218
  180.9 9.7 %copy-start.4 = (bf16[320,3072]{1,0:T(8,128)(2,1)}, bf16[320,3072]{1,0:T(8,128)(2,1)S(1)}, u32[]{:S(2)}) copy-start(bf16[320,3072]{1,0:T(8,128)(2,1)S(1)} %collective-permute-done.13.refs_8_.refs_3_) | copy-start | bytes 5898244
  182.2 6.9 %collective-permute-start.23 = (bf16[320,3072]{1,0:T(8,128)(2,1)S(1)}, bf16[320,3072]{1,0:T(8,128)(2,1)S(1)}, u32[]{:S(2)}, u32[]{:S(2)}) collective-permute-start(bf16[320,3072]{1,0:T(8,128)(2,1)S(1)} %collective-permute-done.13.refs_8_.refs_3_), channel_id=1, source_target_pairs={{0,4},{4,0},{8,12},{12,8},{16,20},{20,16},{24,28},{28,24},{1,5},{5... | collective-permute-start | bytes 5898248 | tf_op jit(solution)/shard_map/ppermute | solution.py:218
  182.2 8.4 %collective-permute-start.24 = (bf16[320,3072]{1,0:T(8,128)(2,1)}, bf16[320,3072]{1,0:T(8,128)(2,1)}, u32[]{:S(2)}, u32[]{:S(2)}) collective-permute-start(bf16[320,3072]{1,0:T(8,128)(2,1)} %collective-permute-done.14.refs_9_.refs_4_), channel_id=1, source_target_pairs={{0,4},{4,0},{8,12},{12,8},{16,20},{20,16},{24,28},{28,24},{1,5},{5... | collective-permute-start | bytes 5898248 | tf_op jit(solution)/shard_map/ppermute | solution.py:218
  182.7 31.9 %collective-permute-start.21 = (bf16[192,3072]{1,0:T(8,128)(2,1)}, bf16[192,3072]{1,0:T(8,128)(2,1)}, u32[]{:S(2)}, u32[]{:S(2)}) collective-permute-start(bf16[192,3072]{1,0:T(8,128)(2,1)} %collective-permute-done.6), channel_id=1, source_target_pairs={{8,0},{12,4},{16,24},{20,28},{9,1},{13,5},{17,25},{21,29},{10,2},{... | collective-permute-start | bytes 3538952 | tf_op jit(solution)/shard_map/ppermute | solution.py:218
  184.0 54.1 %collective-permute-start.22 = (bf16[192,3072]{1,0:T(8,128)(2,1)}, bf16[192,3072]{1,0:T(8,128)(2,1)}, u32[]{:S(2)}, u32[]{:S(2)}) collective-permute-start(bf16[192,3072]{1,0:T(8,128)(2,1)} %collective-permute-done.15), channel_id=1, source_target_pairs={{8,0},{12,4},{16,24},{20,28},{9,1},{13,5},{17,25},{21,29},{10,2},{... | collective-permute-start | bytes 3538952 | tf_op jit(solution)/shard_map/ppermute | solution.py:218
  188.5 26.1 %collective-permute-start.19 = (bf16[160,3072]{1,0:T(8,128)(2,1)}, bf16[160,3072]{1,0:T(8,128)(2,1)}, u32[]{:S(2)}, u32[]{:S(2)}) collective-permute-start(bf16[160,3072]{1,0:T(8,128)(2,1)} %slice.28), channel_id=1, source_target_pairs={{0,1},{1,0},{2,3},{3,2},{4,5},{5,4},{6,7},{7,6},{8,9},{9,8},{10,11... | collective-permute-start | bytes 2949128 | tf_op jit(solution)/shard_map/ppermute | solution.py:218
  189.1 1.5 copy-start.2
  189.1 25.5 %collective-permute-start.20 = (bf16[160,3072]{1,0:T(8,128)(2,1)}, bf16[160,3072]{1,0:T(8,128)(2,1)}, u32[]{:S(2)}, u32[]{:S(2)}) collective-permute-start(bf16[160,3072]{1,0:T(8,128)(2,1)} %slice.29), channel_id=1, source_target_pairs={{0,2},{1,3},{2,0},{3,1},{4,6},{5,7},{6,4},{7,5},{8,10},{9,11},{10,... | collective-permute-start | bytes 2949128 | tf_op jit(solution)/shard_map/ppermute | solution.py:218
  240.7 21.3 %copy-start.5 = (bf16[384,3072]{1,0:T(8,128)(2,1)}, bf16[384,3072]{1,0:T(8,128)(2,1)S(1)}, u32[]{:S(2)}) copy-start(bf16[384,3072]{1,0:T(8,128)(2,1)S(1)} %maximum_select_fusion.refs_1_) | copy-start | bytes 7077892
  240.7 7.8 %collective-permute-start.29 = (bf16[384,3072]{1,0:T(8,128)(2,1)S(1)}, bf16[384,3072]{1,0:T(8,128)(2,1)}, u32[]{:S(2)}, u32[]{:S(2)}) collective-permute-start(bf16[384,3072]{1,0:T(8,128)(2,1)S(1)} %maximum_select_fusion.refs_1_), channel_id=1, source_target_pairs={{0,4},{4,0},{8,12},{12,8},{16,20},{20,16},{24,28},{28,24},{1,5},{5... | collective-permute-start | bytes 7077896 | tf_op jit(solution)/shard_map/ppermute | solution.py:218
  240.8 7.2 %collective-permute-start.27 = (bf16[160,3072]{1,0:T(8,128)(2,1)}, bf16[160,3072]{1,0:T(8,128)(2,1)S(1)}, u32[]{:S(2)}, u32[]{:S(2)}) collective-permute-start(bf16[160,3072]{1,0:T(8,128)(2,1)} %collective-permute-done.19.refs_4_.refs_7_), channel_id=1, source_target_pairs={{0,4},{4,0},{8,12},{12,8},{16,20},{20,16},{24,28},{28,24},{1,5},{5... | collective-permute-start | bytes 2949128 | tf_op jit(solution)/shard_map/ppermute | solution.py:218
  241.3 7.2 %collective-permute-start.28 = (bf16[160,3072]{1,0:T(8,128)(2,1)}, bf16[160,3072]{1,0:T(8,128)(2,1)}, u32[]{:S(2)}, u32[]{:S(2)}) collective-permute-start(bf16[160,3072]{1,0:T(8,128)(2,1)} %collective-permute-done.20.refs_5_.refs_8_), channel_id=1, source_target_pairs={{0,4},{4,0},{8,12},{12,8},{16,20},{20,16},{24,28},{28,24},{1,5},{5... | collective-permute-start | bytes 2949128 | tf_op jit(solution)/shard_map/ppermute | solution.py:218
  241.4 53.7 %collective-permute-start.25 = (bf16[384,3072]{1,0:T(8,128)(2,1)S(1)}, bf16[384,3072]{1,0:T(8,128)(2,1)}, u32[]{:S(2)}, u32[]{:S(2)}) collective-permute-start(bf16[384,3072]{1,0:T(8,128)(2,1)S(1)} %maximum_select_fusion.refs_1_), channel_id=1, source_target_pairs={{0,1},{1,0},{2,3},{3,2},{4,5},{5,4},{6,7},{7,6},{8,9},{9,8},{10,11... | collective-permute-start | bytes 7077896 | tf_op jit(solution)/shard_map/ppermute | solution.py:218
  241.9 53.4 %collective-permute-start.26 = (bf16[384,3072]{1,0:T(8,128)(2,1)S(1)}, bf16[384,3072]{1,0:T(8,128)(2,1)}, u32[]{:S(2)}, u32[]{:S(2)}) collective-permute-start(bf16[384,3072]{1,0:T(8,128)(2,1)S(1)} %maximum_select_fusion.refs_1_), channel_id=1, source_target_pairs={{0,2},{1,3},{2,0},{3,1},{4,6},{5,7},{6,4},{7,5},{8,10},{9,11},{10,... | collective-permute-start | bytes 7077896 | tf_op jit(solution)/shard_map/ppermute | solution.py:218
  262.1 36.9 %collective-permute-start.30 = (bf16[256,3072]{1,0:T(8,128)(2,1)}, bf16[256,3072]{1,0:T(8,128)(2,1)S(1)}, u32[]{:S(2)}, u32[]{:S(2)}) collective-permute-start(bf16[256,3072]{1,0:T(8,128)(2,1)} %get-tuple-element.77), channel_id=1, source_target_pairs={{0,8},{4,12},{8,0},{12,4},{16,24},{20,28},{24,16},{28,20},{1,9},{5... | collective-permute-start | bytes 4718600 | tf_op jit(solution)/shard_map/ppermute | solution.py:218
  299.0 5.3 %copy-start.8 = (bf16[256,3072]{1,0:T(8,128)(2,1)}, bf16[256,3072]{1,0:T(8,128)(2,1)S(1)}, u32[]{:S(2)}) copy-start(bf16[256,3072]{1,0:T(8,128)(2,1)S(1)} %collective-permute-done.30.low_ref) | copy-start | bytes 4718596
  299.0 8.1 %collective-permute-start.33 = (bf16[384,3072]{1,0:T(8,128)(2,1)}, bf16[384,3072]{1,0:T(8,128)(2,1)S(1)}, u32[]{:S(2)}, u32[]{:S(2)}) collective-permute-start(bf16[384,3072]{1,0:T(8,128)(2,1)} %collective-permute-done.25.refs_3_), channel_id=1, source_target_pairs={{0,4},{4,0},{8,12},{12,8},{16,20},{20,16},{24,28},{28,24},{1,5},{5... | collective-permute-start | bytes 7077896 | tf_op jit(solution)/shard_map/ppermute | solution.py:218
  299.0 8.2 %collective-permute-start.34 = (bf16[384,3072]{1,0:T(8,128)(2,1)}, bf16[384,3072]{1,0:T(8,128)(2,1)}, u32[]{:S(2)}, u32[]{:S(2)}) collective-permute-start(bf16[384,3072]{1,0:T(8,128)(2,1)} %collective-permute-done.26.refs_4_), channel_id=1, source_target_pairs={{0,4},{4,0},{8,12},{12,8},{16,20},{20,16},{24,28},{28,24},{1,5},{5... | collective-permute-start | bytes 7077896 | tf_op jit(solution)/shard_map/ppermute | solution.py:218
  304.3 29.5 %collective-permute-start.31 = (bf16[192,3072]{1,0:T(8,128)(2,1)}, bf16[192,3072]{1,0:T(8,128)(2,1)}, u32[]{:S(2)}, u32[]{:S(2)}) collective-permute-start(bf16[192,3072]{1,0:T(8,128)(2,1)} %slice.30), channel_id=1, source_target_pairs={{0,1},{1,0},{2,3},{3,2},{4,5},{5,4},{6,7},{7,6},{8,9},{9,8},{10,11... | collective-permute-start | bytes 3538952 | tf_op jit(solution)/shard_map/ppermute | solution.py:218
  304.8 29.0 %collective-permute-start.32 = (bf16[192,3072]{1,0:T(8,128)(2,1)}, bf16[192,3072]{1,0:T(8,128)(2,1)}, u32[]{:S(2)}, u32[]{:S(2)}) collective-permute-start(bf16[192,3072]{1,0:T(8,128)(2,1)} %slice.31), channel_id=1, source_target_pairs={{0,2},{1,3},{2,0},{3,1},{4,6},{5,7},{6,4},{7,5},{8,10},{9,11},{10,... | collective-permute-start | bytes 3538952 | tf_op jit(solution)/shard_map/ppermute | solution.py:218
  306.4 45.3 %collective-permute-start.37 = (bf16[256,3072]{1,0:T(8,128)(2,1)}, bf16[256,3072]{1,0:T(8,128)(2,1)S(1)}, u32[]{:S(2)}, u32[]{:S(2)}) collective-permute-start(bf16[256,3072]{1,0:T(8,128)(2,1)} %get-tuple-element.88), channel_id=1, source_target_pairs={{0,8},{4,12},{8,0},{12,4},{16,24},{20,28},{24,16},{28,20},{1,9},{5... | collective-permute-start | bytes 4718600 | tf_op jit(solution)/shard_map/ppermute | solution.py:218
  333.9 3.1 collective-permute-start.35
  334.1 4.6 %collective-permute-start.36 = (bf16[192,3072]{1,0:T(8,128)(2,1)}, bf16[192,3072]{1,0:T(8,128)(2,1)S(1)}, u32[]{:S(2)}, u32[]{:S(2)}) collective-permute-start(bf16[192,3072]{1,0:T(8,128)(2,1)} %collective-permute-done.32.refs_2_), channel_id=1, source_target_pairs={{0,4},{4,0},{8,12},{12,8},{16,20},{20,16},{24,28},{28,24},{1,5},{5... | collective-permute-start | bytes 3538952 | tf_op jit(solution)/shard_map/ppermute | solution.py:218
  337.0 1.7 copy-start.10
  (4 other events, 4.6 us)

commit v2 on v1

--- a/solution.py
+++ b/solution.py
@@ -47,11 +47,11 @@
         out_shape=jax.ShapeDtypeStruct((rows, width), jnp.float32),
         scratch_shapes=[pltpu.VMEM((feat, LANES), jnp.float32)] * 3,
         compiler_params=pltpu.CompilerParams(vmem_limit_bytes=VMEM_BYTES),
-        cost_estimate=pl.CostEstimate(flops=rows * feat * NMAT * 6 * 200, bytes_accessed=rows * width * 6, transcendentals=0),
+        cost_estimate=pl.CostEstimate(flops=rows, bytes_accessed=width, transcendentals=0),
     )(x)
 
 
-def pair_kernel(feat, i_rows, spans, tile, n_sums, narrow, has_y, *refs):
+def pair_kernel(feat, i_rows, spans, tile, n_sums, narrow, has_y, final, *refs):
     refs = list(refs)
     take = lambda n: [refs.pop(0) for _ in range(n)]
     tiles = sum(count for _, count in spans) // tile
@@ -60,9 +60,10 @@
     blocks = [slice(f * feat, (f + 1) * feat) for f in range(3)]
     i_refs, j_refs = take(len(i_rows)), take(len(spans))
     y_refs = take(n_sums) if has_y else []
-    out_refs = take(n_i if narrow else n_sums)
+    back_refs = take(n_i) if final else []
+    out_refs = take(n_i if narrow else 3 if final else n_sums)
     ibuf, jbuf, acc, i_sem, j_sem, y_sem, o_sem = take(7)
-    packed = take(1)[0] if narrow else None
+    packed, b_sem = take(2) if narrow or final else (None, None)
 
     def block(i):
         return pl.ds(i * ROW_TILE, ROW_TILE)
@@ -83,6 +84,8 @@
             pltpu.make_async_copy(y_refs[i // per].at[block(i % per)], acc.at[block(i)], y_sem.at[i]).start()
     for t in range(1, tiles):
         fill(jbuf, j_sem, j_refs, spans, t, tile)
+    for i, ref in enumerate(back_refs):
+        pltpu.make_async_copy(ref, packed.at[block(i)], b_sem.at[i]).start()
 
     def wait(ref, sem):
         pltpu.make_async_copy(ref, ref, sem).wait()
@@ -116,7 +119,12 @@
 
             @pl.when(t == tiles - 1)
             def _():
-                for n in range(n_i):
+                if final:
+                    wait(packed.at[span], b_sem.at[i])
+                    acc[span, :] = NMAT * (acc[span, :] + packed[span, :].astype(jnp.float32))
+                    for out, b in zip(out_refs, blocks):
+                        pltpu.make_async_copy(acc.at[span, b], out.at[span], o_sem.at[i]).start()
+                for n in range(0 if final else n_i):
                     @pl.when(i == n)
                     def _():
                         if narrow:
@@ -134,7 +142,7 @@
         wait((packed if narrow else acc).at[block(i)], o_sem.at[i])
 
 
-def pair_sums(lefts, rights, sums, tile, narrow=False):
+def pair_sums(lefts, rights, sums, tile, narrow=False, back=None):
     width = lefts[0].shape[1]
     feat = width // 3
     i_rows = [v.shape[0] for v in lefts]
@@ -144,13 +152,15 @@
     total = sum(count for _, count in spans)
     assert total % tile == 0 and rows % ROW_TILE == 0
     n_i = rows // ROW_TILE
-    has_y = sums is not None
+    has_y, final = sums is not None, back is not None
     n_sums = len(sums) if has_y else 1
-    any_spec = pl.BlockSpec(memory_space=pl.ANY)
-    operands = [*lefts, *(r for r, _, _ in rights), *(sums or [])]
+    any_spec = pl.BlockSpec(memory_space=pltpu.HBM)
+    operands = [*lefts, *(r for r, _, _ in rights), *(sums or []), *(back or [])]
     first_y = len(lefts) + len(rights)
     if narrow:
         outs = [jax.ShapeDtypeStruct((ROW_TILE, width), jnp.bfloat16)] * n_i
+    elif final:
+        outs = [jax.ShapeDtypeStruct((rows, feat), jnp.float32)] * 3
     else:
         outs = [jax.ShapeDtypeStruct((rows // n_sums, width), jnp.float32)] * n_sums
     scratch = [
@@ -162,48 +172,50 @@
         pltpu.SemaphoreType.DMA((n_i,)),
         pltpu.SemaphoreType.DMA((n_i,)),
     ]
-    if narrow:
-        scratch.append(pltpu.VMEM((rows, width), jnp.bfloat16))
+    if narrow or final:
+        scratch += [pltpu.VMEM((rows, width), jnp.bfloat16), pltpu.SemaphoreType.DMA((n_i,))]
     return pl.pallas_call(
-        functools.partial(pair_kernel, feat, i_rows, spans, tile, n_sums, narrow, has_y),
+        functools.partial(pair_kernel, feat, i_rows, spans, tile, n_sums, narrow, has_y, final),
         in_specs=[any_spec] * len(operands),
         out_specs=[any_spec] * len(outs),
         out_shape=outs,
         scratch_shapes=scratch,
-        input_output_aliases={first_y + n: n for n in range(n_sums)} if has_y and not narrow else {},
+        input_output_aliases={first_y + n: n for n in range(n_sums)} if has_y and not narrow and not final else {},
         compiler_params=pltpu.CompilerParams(vmem_limit_bytes=VMEM_BYTES),
-        cost_estimate=pl.CostEstimate(flops=rows * total * feat, bytes_accessed=width * total, transcendentals=0),
+        cost_estimate=pl.CostEstimate(flops=rows, bytes_accessed=width, transcendentals=0),
     )(*operands)
 
 
-def finish_kernel(feat, home_ref, low_ref, high_ref, *out_refs):
-    def write(back_ref):
-        for f, out in enumerate(out_refs):
-            b = slice(f * feat, (f + 1) * feat)
-            out[...] = NMAT * (home_ref[:, b] + back_ref[:, b].astype(jnp.float32))
-
-    steps = pl.num_programs(0) // 2
-    pl.when(pl.program_id(0) < steps)(lambda: write(low_ref))
-    pl.when(pl.program_id(0) >= steps)(lambda: write(high_ref))
-
-
-def finish(home, low, high):
-    rows, width = home.shape
-    feat = width // 3
-    steps = low.shape[0] // LANES
+def cut_kernel(mid, parts, x_ref, y_ref, low_ref, high_ref, low, high, sem):
+    size = mid // parts
+    spans = [pl.ds(n * size, size) for n in range(parts)]
+    moves = []
+    for n, span in enumerate(spans):
+        moves.append((y_ref.at[span], low.at[span], low_ref.at[span], n))
+        moves.append((x_ref.at[pl.ds(mid + n * size, size)], high.at[span], high_ref.at[span], parts + n))
+    first = [pltpu.make_async_copy(src, buf, sem.at[0, n]) for src, buf, _, n in moves]
+    last = [pltpu.make_async_copy(buf, dst, sem.at[1, n]) for _, buf, dst, n in moves]
+    for copy in first:
+        copy.start()
+    for copy, then in zip(first, last):
+        copy.wait()
+        then.start()
+    for copy in last:
+        copy.wait()
+
+
+def cut(from_x, from_y):
+    rows, width = from_x.shape
+    mid, parts = rows // 2, 2
+    spec = pl.BlockSpec(memory_space=pltpu.HBM)
     return pl.pallas_call(
-        functools.partial(finish_kernel, feat),
-        grid=(2 * steps,),
-        in_specs=[
-            pl.BlockSpec((LANES, width), lambda i: (i, 0)),
-            pl.BlockSpec((LANES, width), lambda i: (jnp.minimum(i, steps - 1), 0)),
-            pl.BlockSpec((LANES, width), lambda i: (jnp.maximum(i - steps, 0), 0)),
-        ],
-        out_specs=[pl.BlockSpec((LANES, feat), lambda i: (i, 0))] * 3,
-        out_shape=[jax.ShapeDtypeStruct((rows, feat), jnp.float32)] * 3,
-        compiler_params=pltpu.CompilerParams(vmem_limit_bytes=VMEM_BYTES),
-        cost_estimate=pl.CostEstimate(flops=rows * width, bytes_accessed=rows * width * 10, transcendentals=0),
-    )(home, low, high)
+        functools.partial(cut_kernel, mid, parts),
+        in_specs=[spec] * 2,
+        out_specs=[spec] * 2,
+        out_shape=[jax.ShapeDtypeStruct((mid, width), from_x.dtype)] * 2,
+        scratch_shapes=[pltpu.VMEM((mid, width), from_x.dtype)] * 2 + [pltpu.SemaphoreType.DMA((2, 2 * parts))],
+        cost_estimate=pl.CostEstimate(flops=0, bytes_accessed=rows * width, transcendentals=0),
+    )(from_x, from_y)
 
 
 def near_shards(factor_a, factor_b, factor_c):
@@ -225,40 +237,46 @@
     along_y = move("col", [(c, c ^ 2) for c in range(4)])
 
     def corner(from_x, from_y):
-        mid = from_x.shape[0] // 2
-        return along_x(from_y[:mid]), along_y(from_x[mid:])
+        low, high = cut(from_x, from_y)
+        return along_x(low), along_y(high)
 
     x_x, x_y, x_s = along_x(x), along_y(x), core(x)
-    part_a, part_c = x[:early], x[early:]
+    x_z, x_s = fence((x, x_s))
+    part_a, part_c = x_z[:early], x_z[early:]
     guest_a, far_a = partner(part_a), across(part_a)
     home = trace_terms(x)
     (home,) = pair_sums([x], [x, x_s], [home], 1024)
-    guest_a, far_a, part_c, home = fence((guest_a, far_a, part_c, home))
+    guest_a, far_a, home = fence((guest_a, far_a, home))
+
+    out_a, next_b = outward(far_a), across(guest_a)
+    x_x, x_y, home = fence((x_x, x_y, home))
+
+    x_d0, x_d1 = corner(x_x, x_y)
+    x_xs, x_ys = fence((core(x_x), core(x_y)))
+    (home,) = pair_sums([x], [x_x, x_y, x_xs, x_ys], [home], 1024)
+    out_a, next_b, part_c, home = fence((out_a, next_b, part_c, home))
 
     guest_c, far_c = partner(part_c), across(part_c)
-    x_x, x_y, guest_c, far_c = fence((x_x, x_y, guest_c, far_c))
-
-    guest = [guest_a, guest_c]
-    x_d0, x_d1 = corner(x_x, x_y)
-    out_a, next_b = outward(far_a), across(guest_a)
-    x_xs, x_ys = core(x_x), core(x_y)
-    (visit,) = pair_sums(guest, [x, x_s, x_x, x_y, x_xs, x_ys], None, 1024)
-    x_d0, x_d1, out_a, next_b, visit = fence((x_d0, x_d1, out_a, next_b, visit))
+    x_d0, x_d1, out_a, next_b, home = fence((x_d0, x_d1, out_a, next_b, home))
 
     e = jnp.where(inner, next_b, out_a)
     e_x, e_y = along_x(e), along_y(e)
-    out_c0, next_c = outward(far_c), across(guest_c)
     x_ds0, x_ds1, e_s = fence((core(x_d0), core(x_d1), core(e)))
     x_d = [x_d0, x_d1, x_ds0, x_ds1]
-    (home,) = pair_sums([x], [x_x, x_y, x_xs, x_ys, *x_d], [home], 1024)
-    e_x, e_y, next_c, home = fence((e_x, e_y, next_c, home))
+    (home,) = pair_sums([x], x_d, [home], 1024)
+    guest_c, far_c, home = fence((guest_c, far_c, home))
+
+    guest = [guest_a, guest_c]
+    out_c0, next_c = outward(far_c), across(guest_c)
+    (visit,) = pair_sums(guest, [x, x_s, x_x, x_y, x_xs, x_ys], None, 1024)
+    e_x, e_y, out_c0, next_c, home, visit = fence((e_x, e_y, out_c0, next_c, home, visit))
 
     e_d0, e_d1 = corner(e_x, e_y)
     out_c1 = outward(next_c)
     e_xs, e_ys = fence((core(e_x), core(e_y)))
     lead = 3 * rows - 4 * early
     (visit,) = pair_sums(guest, [*x_d, e, e_s, e_x, e_y, (e_xs, 0, lead)], [visit], 1280)
-    e_d0, e_d1, out_c0, out_c1, visit = fence((e_d0, e_d1, out_c0, out_c1, visit))
+    e_d0, e_d1, out_c1, visit = fence((e_d0, e_d1, out_c1, visit))
 
     c = jnp.where(inner, jnp.concatenate([far_c, next_c]), jnp.concatenate([out_c0, out_c1]))
     c_x, c_y = along_x(c), along_y(c)
@@ -274,8 +292,8 @@
     c_d0, c_d1 = corner(c_x, c_y)
     (home,) = pair_sums([x], [c, c_s, c_x, c_y, core(c_x), core(c_y)], [home], 768)
     c_d0, c_d1, home = fence((c_d0, c_d1, home))
-    (home,) = pair_sums([x], [c_d0, c_d1, core(c_d0), core(c_d1)], [home], 768)
-    return tuple(finish(home, back_0, back_1))
+    c_d = [c_d0, c_d1, core(c_d0), core(c_d1)]
+    return tuple(pair_sums([x], c_d, [home], 768, back=[back_0, back_1]))
 
 
 def gram_rows(left, right):

time: 360 us -> 349 us (0.969)
  waiting for transfers between devices: 93.6 us -> 77.2 us
  Pallas kernels: 201 us -> 206 us
  local copies, waits for them, and re-layouts: 22.1 us -> 17.9 us
  starting transfers between devices: 37.6 us -> 41.2 us
    ppermute x38, waiting for transfers between devices: 93.6 us -> 77.2 us  [move(): return lambda v: lax.ppermute(v, axis, pairs)]
    slice x8 -> x2, local copies, waits for them, and re-layouts: 16.1 us -> 5.29 us  [near_shards(): part_a, part_c = (x_z[:early], x_z[early:])]
    unnamed x30 -> x34, local copies, waits for them, and re-layouts: 5.85 us -> 11.5 us
    pallas_call x8 -> x9, Pallas kernels: 170 us -> 175 us  [pair_sums(): pl.pallas_call(functools.partial(pair_kernel, feat, i_rows, spans, tile,...]
    ppermute x38, starting transfers between devices: 37.6 us -> 41.2 us  [move(): return lambda v: lax.ppermute(v, axis, pairs)]
    pallas_call x1 -> x3, Pallas kernels: 6.53 us -> 7.74 us  [cut(): pl.pallas_call(functools.partial(cut_kernel, mid, parts), in_specs=[spec]...]
  transfers between devices with their start and end apart: 38 -> 38, of which waited for: 18 -> 16; matrix products, arithmetic and copies ran while one was open for 5% -> 2% of each run, Pallas kernels for 54% -> 56%
where the time goes in v2:
time: 349 us; the launch traced here: 348 us
  Pallas kernels  206 us (59%)
  waiting for transfers between devices  77.2 us (22%)
  starting transfers between devices  41.2 us (12%)
  local copies, waits for them, and re-layouts  17.9 us (5%)
  other arithmetic  4.41 us (1%)
    pallas_call x9, Pallas kernels, pair_sums(): pl.pallas_call(functools.partial(pair_kernel, feat, i_rows, spans, tile,...  175 us
    ppermute x38, waiting for transfers between devices, move(): return lambda v: lax.ppermute(v, axis, pairs)  77.2 us
    ppermute x38, starting transfers between devices, move(): return lambda v: lax.ppermute(v, axis, pairs)  41.2 us
    pallas_call x1, Pallas kernels, trace_terms(): pl.pallas_call(functools.partial(trace_kernel, feat), grid=(rows // LANES...  23.9 us
    unnamed x34, local copies, waits for them, and re-layouts  11.5 us
    pallas_call x3, Pallas kernels, cut(): pl.pallas_call(functools.partial(cut_kernel, mid, parts), in_specs=[spec]...  7.74 us
  transfers between devices with their start and end apart: 38, of which 16 were waited for; matrix products, arithmetic and copies ran while one was open for 2% of the time, Pallas kernels for 56%

profile of v2, /device:TPU:0, one launch (start us, length us, event | category | flops | bytes accessed | tf_op | source)
XLA Modules:
  0.0 348.4 jit_solution(11648692962194203929)
XLA Ops:
  0.7 2.5 constant_dynamic-update-slice_fusion.2
  5.8 2.5 collective-permute-start.5
  8.3 1.5 collective-permute-start.6
  9.8 1.6 collective-permute-done.refs_2_.refs_3_
  11.4 2.9 slice.6
  14.4 2.9 collective-permute-start.1
  17.3 1.9 collective-permute-start.2
  19.3 23.9 %shard_map.58.refs_3_ = f32[512,3072]{1,0:T(8,128)} custom-call(bf16[512,3072]{1,0:T(8,128)(2,1)} %constant_dynamic-update-slice_fusion.x_ref.refs_0_.refs_1_.refs_2_), custom_call_target="tpu_custom_call" | custom-call | flops 512 | bytes 3072 | tf_op jit(solution)/shard_map/pallas_call | solution.py:42
  43.2 13.4 %shard_map.59.refs_5_ = f32[512,3072]{1,0:T(8,128)} custom-call(bf16[512,3072]{1,0:T(8,128)(2,1)} %constant_dynamic-update-slice_fusion.x_ref.refs_0_.refs_1_.refs_2_, bf16[512,3072]{1,0:T(8,128)(2,1)} %constant_dynamic-update-slice_fusion.x_ref.refs_0_.refs_1_.refs_2_, ...), custom_call_target="tpu_custom_call", output_to_operand_aliasing={{}: (3, {})} | custom-call | flops 512 | bytes 3072 | tf_op jit(solution)/shard_map/pallas_call | solution.py:177
  56.5 4.2 %collective-permute-done.1.refs_0_ = bf16[320,3072]{1,0:T(8,128)(2,1)} collective-permute-done((bf16[320,3072]{1,0:T(8,128)(2,1)}, bf16[320,3072]{1,0:T(8,128)(2,1)}, u32[]{:S(2)}, u32[]{:S(2)}) %collective-permute-start.1) | collective-permute-done | bytes 1966112 | tf_op jit(solution)/shard_map/ppermute | solution.py:230
  60.8 16.5 %collective-permute-done.5.refs_1_.x_ref.refs_4_ = bf16[512,3072]{1,0:T(8,128)(2,1)S(1)} collective-permute-done((bf16[512,3072]{1,0:T(8,128)(2,1)}, bf16[512,3072]{1,0:T(8,128)(2,1)S(1)}, u32[]{:S(2)}, u32[]{:S(2)}) %collective-permute-start.5) | collective-permute-done | bytes 3145760 | tf_op jit(solution)/shard_map/ppermute | solution.py:230
  77.3 1.6 collective-permute-done.6.refs_2_.y_ref.refs_5_
  79.4 2.0 collective-permute-start.4
  82.6 2.9 shard_map.61
  85.9 3.2 collective-permute-done.7.refs_3_.refs_6_
  89.1 1.5 collective-permute-start.12
  90.6 2.3 slice.7
  93.0 19.6 %shard_map.60.refs_5_ = f32[512,3072]{1,0:T(8,128)} custom-call(bf16[512,3072]{1,0:T(8,128)(2,1)} %constant_dynamic-update-slice_fusion.x_ref.refs_0_.refs_1_.refs_2_, bf16[512,3072]{1,0:T(8,128)(2,1)} %copy-done, bf16[512,3072]{1,0:T(8,128)(2,1)} %collective-permute-done.6.refs_2_.y_ref.refs_5_, ...), custom_call_target="tpu_custom_call", output_to_operand_aliasing={{}: (5, {})} | custom-call | flops 512 | bytes 3072 | tf_op jit(solution)/shard_map/pallas_call | solution.py:177
  112.6 16.1 %collective-permute-done.3 = bf16[320,3072]{1,0:T(8,128)(2,1)} collective-permute-done((bf16[320,3072]{1,0:T(8,128)(2,1)}, bf16[320,3072]{1,0:T(8,128)(2,1)}, u32[]{:S(2)}, u32[]{:S(2)}) %collective-permute-start.3) | collective-permute-done | bytes 1966112 | tf_op jit(solution)/shard_map/ppermute | solution.py:230
  129.2 1.8 broadcast_select_fusion.refs_6_.refs_1_
  131.1 1.7 collective-permute-start.10
  132.8 2.2 collective-permute-start.9
  137.4 1.5 collective-permute-start.17
  138.9 13.3 %shard_map.62.refs_11_ = f32[512,3072]{1,0:T(8,128)} custom-call(bf16[512,3072]{1,0:T(8,128)(2,1)} %constant_dynamic-update-slice_fusion.x_ref.refs_0_.refs_1_.refs_2_, bf16[256,3072]{1,0:T(8,128)(2,1)} %collective-permute-done.11.refs_1_.refs_2_, bf16[256,3072]{1,0:T(8,128)(2,1)} %collective-permute-done.12.refs_2_.refs_3_, ...), custom_call_target="tpu_custom_call", output_to_operand_aliasing={{}: (5, {})} | custom-call | flops 512 | bytes 3072 | tf_op jit(solution)/shard_map/pallas_call | solution.py:177
  152.2 9.4 %collective-permute-done.9.refs_1_ = bf16[192,3072]{1,0:T(8,128)(2,1)S(1)} collective-permute-done((bf16[192,3072]{1,0:T(8,128)(2,1)}, bf16[192,3072]{1,0:T(8,128)(2,1)S(1)}, u32[]{:S(2)}, u32[]{:S(2)}) %collective-permute-start.9) | collective-permute-done | bytes 1179680 | tf_op jit(solution)/shard_map/ppermute | solution.py:230
  161.6 1.3 collective-permute-start.18
  162.9 1.7 collective-permute-start.19
  164.6 28.1 %shard_map.63.refs_11_ = f32[512,3072]{1,0:T(8,128)} custom-call(bf16[320,3072]{1,0:T(8,128)(2,1)} %collective-permute-done.1.refs_0_, bf16[192,3072]{1,0:T(8,128)(2,1)} %copy-done.3, bf16[512,3072]{1,0:T(8,128)(2,1)} %constant_dynamic-update-slice_fusion.x_ref.refs_0_.refs_1_.refs_2_, bf16[512,3072]{1,0:T(8,128)(2,1)} %collective-permute-done.refs_2_.refs_3_, ...), custom_call_target="tpu_custom_call" | custom-call | flops 512 | bytes 3072 | tf_op jit(solution)/shard_map/pallas_call | solution.py:177
  193.3 1.5 collective-permute-start.22
  194.9 2.4 shard_map.64
  197.8 1.5 collective-permute-start.21
  200.6 24.0 %shard_map.65.refs_8_ = f32[512,3072]{1,0:T(8,128)} custom-call(bf16[320,3072]{1,0:T(8,128)(2,1)} %collective-permute-done.1.refs_0_, bf16[192,3072]{1,0:T(8,128)(2,1)} %copy-done.3, bf16[256,3072]{1,0:T(8,128)(2,1)} %collective-permute-done.11.refs_1_.refs_2_, ...), custom_call_target="tpu_custom_call", output_to_operand_aliasing={{}: (11, {})} | custom-call | flops 512 | bytes 3072 | tf_op jit(solution)/shard_map/pallas_call | solution.py:177
  224.6 2.4 collective-permute-done.22
  227.0 2.7 maximum_select_fusion.refs_1_
  230.9 1.5 collective-permute-start.26
  232.4 4.3 %collective-permute-done.27.refs_6_.refs_9_ = bf16[160,3072]{1,0:T(8,128)(2,1)S(1)} collective-permute-done((bf16[160,3072]{1,0:T(8,128)(2,1)S(1)}, bf16[160,3072]{1,0:T(8,128)(2,1)S(1)}, u32[]{:S(2)}, u32[]{:S(2)}) %collective-permute-start.27) | collective-permute-done | bytes 983072 | tf_op jit(solution)/shard_map/ppermute | solution.py:230
  238.7 13.2 %shard_map.66 = (bf16[256,3072]{1,0:T(8,128)(2,1)}, bf16[256,3072]{1,0:T(8,128)(2,1)}) custom-call(bf16[320,3072]{1,0:T(8,128)(2,1)} %collective-permute-done.1.refs_0_, bf16[192,3072]{1,0:T(8,128)(2,1)} %copy-done.3, bf16[320,3072]{1,0:T(8,128)(2,1)} %copy-done.2, bf16[320,3072]{1,0:T(8,128)(2,1)} %collective-permute-done.24.refs_3_.refs_6_, ...), custom_call_target="tpu_custom_call" | custom-call | flops 512 | bytes 3072 | tf_op jit(solution)/shard_map/pallas_call | solution.py:177
  251.9 4.8 %collective-permute-start.30 = (bf16[256,3072]{1,0:T(8,128)(2,1)}, bf16[256,3072]{1,0:T(8,128)(2,1)}, u32[]{:S(2)}, u32[]{:S(2)}) collective-permute-start(bf16[256,3072]{1,0:T(8,128)(2,1)} %get-tuple-element.107), channel_id=1, source_target_pairs={{0,8},{4,12},{8,0},{12,4},{16,24},{20,28},{24,16},{28,20},{1,9},{5... | collective-permute-start | bytes 4718600 | tf_op jit(solution)/shard_map/ppermute | solution.py:230
  256.7 25.0 %shard_map.67.refs_7_ = f32[512,3072]{1,0:T(8,128)} custom-call(bf16[512,3072]{1,0:T(8,128)(2,1)} %constant_dynamic-update-slice_fusion.x_ref.refs_0_.refs_1_.refs_2_, bf16[320,3072]{1,0:T(8,128)(2,1)} %copy-done.1, bf16[320,3072]{1,0:T(8,128)(2,1)} %collective-permute-done.15.refs_7_.refs_2_, ...), custom_call_target="tpu_custom_call", output_to_operand_aliasing={{}: (11, {})} | custom-call | flops 512 | bytes 3072 | tf_op jit(solution)/shard_map/pallas_call | solution.py:177
  281.7 2.3 collective-permute-done.25.x_ref.refs_3_
  284.3 7.6 %collective-permute-done.30.refs_6_ = bf16[256,3072]{1,0:T(8,128)(2,1)} collective-permute-done((bf16[256,3072]{1,0:T(8,128)(2,1)}, bf16[256,3072]{1,0:T(8,128)(2,1)}, u32[]{:S(2)}, u32[]{:S(2)}) %collective-permute-start.30) | collective-permute-done | bytes 1572896 | tf_op jit(solution)/shard_map/ppermute | solution.py:230
  292.4 2.5 shard_map.68
  294.9 1.6 collective-permute-start.31
  297.0 1.7 collective-permute-start.37
  300.1 1.3 copy-done.10
  301.5 25.3 %shard_map.69.refs_5_ = f32[512,3072]{1,0:T(8,128)} custom-call(bf16[512,3072]{1,0:T(8,128)(2,1)} %constant_dynamic-update-slice_fusion.x_ref.refs_0_.refs_1_.refs_2_, bf16[384,3072]{1,0:T(8,128)(2,1)} %copy-done.4, bf16[384,3072]{1,0:T(8,128)(2,1)} %collective-permute-done.29.refs_2_, ...), custom_call_target="tpu_custom_call", output_to_operand_aliasing={{}: (7, {})} | custom-call | flops 512 | bytes 3072 | tf_op jit(solution)/shard_map/pallas_call | solution.py:177
  327.4 5.7 %collective-permute-done.37.refs_7_ = bf16[256,3072]{1,0:T(8,128)(2,1)} collective-permute-done((bf16[256,3072]{1,0:T(8,128)(2,1)}, bf16[256,3072]{1,0:T(8,128)(2,1)}, u32[]{:S(2)}, u32[]{:S(2)}) %collective-permute-start.37) | collective-permute-done | bytes 1572896 | tf_op jit(solution)/shard_map/ppermute | solution.py:230
  335.2 12.9 %shard_map.70 = (f32[512,1024]{1,0:T(8,128)}, f32[512,1024]{1,0:T(8,128)}, f32[512,1024]{1,0:T(8,128)}) custom-call(bf16[512,3072]{1,0:T(8,128)(2,1)} %constant_dynamic-update-slice_fusion.x_ref.refs_0_.refs_1_.refs_2_, bf16[192,3072]{1,0:T(8,128)(2,1)} %copy-done.11, bf16[192,3072]{1,0:T(8,128)(2,1)} %collective-permute-done.32.refs_2_, ...), custom_call_target="tpu_custom_call" | custom-call | flops 512 | bytes 3072 | tf_op jit(solution)/shard_map/pallas_call | solution.py:177
  (80 shorter events, 18.9 us)
Async XLA Ops:
  0.6 2.5 copy-start.14
  0.6 3.6 %copy-start.15 = (bf16[512,1024]{1,0:T(8,128)(2,1)S(1)}, bf16[512,1024]{1,0:T(8,128)(2,1)}, u32[]{:S(2)}) copy-start(bf16[512,1024]{1,0:T(8,128)(2,1)} %param.5) | copy-start | bytes 3145732
  5.4 6.1 %collective-permute-start = (bf16[512,3072]{1,0:T(8,128)(2,1)}, bf16[512,3072]{1,0:T(8,128)(2,1)}, u32[]{:S(2)}, u32[]{:S(2)}) collective-permute-start(bf16[512,3072]{1,0:T(8,128)(2,1)} %constant_dynamic-update-slice_fusion.x_ref.refs_0_.refs_1_.refs_2_), channel_id=1, source_target_pairs={{0,4},{4,0},{8,12},{12,8},{16,20},{20,16},{24,28},{28,24},{1,5},{5... | collective-permute-start | bytes 9437192 | tf_op jit(solution)/shard_map/ppermute | solution.py:230
  5.8 71.5 %collective-permute-start.5 = (bf16[512,3072]{1,0:T(8,128)(2,1)}, bf16[512,3072]{1,0:T(8,128)(2,1)S(1)}, u32[]{:S(2)}, u32[]{:S(2)}) collective-permute-start(bf16[512,3072]{1,0:T(8,128)(2,1)} %constant_dynamic-update-slice_fusion.x_ref.refs_0_.refs_1_.refs_2_), channel_id=1, source_target_pairs={{0,1},{1,0},{2,3},{3,2},{4,5},{5,4},{6,7},{7,6},{8,9},{9,8},{10,11... | collective-permute-start | bytes 9437192 | tf_op jit(solution)/shard_map/ppermute | solution.py:230
  8.3 70.5 %collective-permute-start.6 = (bf16[512,3072]{1,0:T(8,128)(2,1)}, bf16[512,3072]{1,0:T(8,128)(2,1)}, u32[]{:S(2)}, u32[]{:S(2)}) collective-permute-start(bf16[512,3072]{1,0:T(8,128)(2,1)} %constant_dynamic-update-slice_fusion.x_ref.refs_0_.refs_1_.refs_2_), channel_id=1, source_target_pairs={{0,2},{1,3},{2,0},{3,1},{4,6},{5,7},{6,4},{7,5},{8,10},{9,11},{10,... | collective-permute-start | bytes 9437192 | tf_op jit(solution)/shard_map/ppermute | solution.py:230
  14.4 46.4 %collective-permute-start.1 = (bf16[320,3072]{1,0:T(8,128)(2,1)}, bf16[320,3072]{1,0:T(8,128)(2,1)}, u32[]{:S(2)}, u32[]{:S(2)}) collective-permute-start(bf16[320,3072]{1,0:T(8,128)(2,1)} %slice.6), channel_id=1, source_target_pairs={{0,8},{4,12},{8,0},{12,4},{16,24},{20,28},{24,16},{28,20},{1,9},{5... | collective-permute-start | bytes 5898248 | tf_op jit(solution)/shard_map/ppermute | solution.py:230
  17.3 43.4 %collective-permute-start.2 = (bf16[320,3072]{1,0:T(8,128)(2,1)}, bf16[320,3072]{1,0:T(8,128)(2,1)}, u32[]{:S(2)}, u32[]{:S(2)}) collective-permute-start(bf16[320,3072]{1,0:T(8,128)(2,1)} %slice.6), channel_id=1, source_target_pairs={{8,16},{12,20},{16,8},{20,12},{9,17},{13,21},{17,9},{21,13},{10,18... | collective-permute-start | bytes 5898248 | tf_op jit(solution)/shard_map/ppermute | solution.py:230
  77.3 5.3 %copy-start = (bf16[512,3072]{1,0:T(8,128)(2,1)}, bf16[512,3072]{1,0:T(8,128)(2,1)S(1)}, u32[]{:S(2)}) copy-start(bf16[512,3072]{1,0:T(8,128)(2,1)S(1)} %collective-permute-done.5.refs_1_.x_ref.refs_4_) | copy-start | bytes 9437188
  78.9 10.3 %collective-permute-start.7 = (bf16[512,3072]{1,0:T(8,128)(2,1)S(1)}, bf16[512,3072]{1,0:T(8,128)(2,1)}, u32[]{:S(2)}, u32[]{:S(2)}) collective-permute-start(bf16[512,3072]{1,0:T(8,128)(2,1)S(1)} %collective-permute-done.5.refs_1_.x_ref.refs_4_), channel_id=1, source_target_pairs={{0,4},{4,0},{8,12},{12,8},{16,20},{20,16},{24,28},{28,24},{1,5},{5... | collective-permute-start | bytes 9437192 | tf_op jit(solution)/shard_map/ppermute | solution.py:230
  78.9 14.1 %collective-permute-start.8 = (bf16[512,3072]{1,0:T(8,128)(2,1)}, bf16[512,3072]{1,0:T(8,128)(2,1)}, u32[]{:S(2)}, u32[]{:S(2)}) collective-permute-start(bf16[512,3072]{1,0:T(8,128)(2,1)} %collective-permute-done.6.refs_2_.y_ref.refs_5_), channel_id=1, source_target_pairs={{0,4},{4,0},{8,12},{12,8},{16,20},{20,16},{24,28},{28,24},{1,5},{5... | collective-permute-start | bytes 9437192 | tf_op jit(solution)/shard_map/ppermute | solution.py:230
  79.4 33.2 %collective-permute-start.4 = (bf16[320,3072]{1,0:T(8,128)(2,1)}, bf16[320,3072]{1,0:T(8,128)(2,1)}, u32[]{:S(2)}, u32[]{:S(2)}) collective-permute-start(bf16[320,3072]{1,0:T(8,128)(2,1)} %collective-permute-done.1.refs_0_), channel_id=1, source_target_pairs={{8,16},{12,20},{16,8},{20,12},{9,17},{13,21},{17,9},{21,13},{10,18... | collective-permute-start | bytes 5898248 | tf_op jit(solution)/shard_map/ppermute | solution.py:230
  81.3 47.4 %collective-permute-start.3 = (bf16[320,3072]{1,0:T(8,128)(2,1)}, bf16[320,3072]{1,0:T(8,128)(2,1)}, u32[]{:S(2)}, u32[]{:S(2)}) collective-permute-start(bf16[320,3072]{1,0:T(8,128)(2,1)} %collective-permute-done.2), channel_id=1, source_target_pairs={{8,0},{12,4},{16,24},{20,28},{9,1},{13,5},{17,25},{21,29},{10,2},{... | collective-permute-start | bytes 5898248 | tf_op jit(solution)/shard_map/ppermute | solution.py:230
  85.5 43.2 %collective-permute-start.11 = (bf16[256,3072]{1,0:T(8,128)(2,1)}, bf16[256,3072]{1,0:T(8,128)(2,1)}, u32[]{:S(2)}, u32[]{:S(2)}) collective-permute-start(bf16[256,3072]{1,0:T(8,128)(2,1)} %get-tuple-element.73), channel_id=1, source_target_pairs={{0,1},{1,0},{2,3},{3,2},{4,5},{5,4},{6,7},{7,6},{8,9},{9,8},{10,11... | collective-permute-start | bytes 4718600 | tf_op jit(solution)/shard_map/ppermute | solution.py:230
  89.1 39.6 %collective-permute-start.12 = (bf16[256,3072]{1,0:T(8,128)(2,1)}, bf16[256,3072]{1,0:T(8,128)(2,1)}, u32[]{:S(2)}, u32[]{:S(2)}) collective-permute-start(bf16[256,3072]{1,0:T(8,128)(2,1)} %get-tuple-element.74), channel_id=1, source_target_pairs={{0,2},{1,3},{2,0},{3,1},{4,6},{5,7},{6,4},{7,5},{8,10},{9,11},{10,... | collective-permute-start | bytes 4718600 | tf_op jit(solution)/shard_map/ppermute | solution.py:230
  128.7 6.3 %collective-permute-start.13 = (bf16[256,3072]{1,0:T(8,128)(2,1)}, bf16[256,3072]{1,0:T(8,128)(2,1)S(1)}, u32[]{:S(2)}, u32[]{:S(2)}) collective-permute-start(bf16[256,3072]{1,0:T(8,128)(2,1)} %collective-permute-done.11.refs_1_.refs_2_), channel_id=1, source_target_pairs={{0,4},{4,0},{8,12},{12,8},{16,20},{20,16},{24,28},{28,24},{1,5},{5... | collective-permute-start | bytes 4718600 | tf_op jit(solution)/shard_map/ppermute | solution.py:230
  128.7 7.5 %collective-permute-start.14 = (bf16[256,3072]{1,0:T(8,128)(2,1)}, bf16[256,3072]{1,0:T(8,128)(2,1)S(1)}, u32[]{:S(2)}, u32[]{:S(2)}) collective-permute-start(bf16[256,3072]{1,0:T(8,128)(2,1)} %collective-permute-done.12.refs_2_.refs_3_), channel_id=1, source_target_pairs={{0,4},{4,0},{8,12},{12,8},{16,20},{20,16},{24,28},{28,24},{1,5},{5... | collective-permute-start | bytes 4718600 | tf_op jit(solution)/shard_map/ppermute | solution.py:230
  131.0 21.2 %copy-start.1 = (bf16[320,3072]{1,0:T(8,128)(2,1)}, bf16[320,3072]{1,0:T(8,128)(2,1)S(1)}, u32[]{:S(2)}) copy-start(bf16[320,3072]{1,0:T(8,128)(2,1)S(1)} %broadcast_select_fusion.refs_6_.refs_1_) | copy-start | bytes 5898244
  131.0 7.9 %collective-permute-start.15 = (bf16[320,3072]{1,0:T(8,128)(2,1)S(1)}, bf16[320,3072]{1,0:T(8,128)(2,1)}, u32[]{:S(2)}, u32[]{:S(2)}) collective-permute-start(bf16[320,3072]{1,0:T(8,128)(2,1)S(1)} %broadcast_select_fusion.refs_6_.refs_1_), channel_id=1, source_target_pairs={{0,4},{4,0},{8,12},{12,8},{16,20},{20,16},{24,28},{28,24},{1,5},{5... | collective-permute-start | bytes 5898248 | tf_op jit(solution)/shard_map/ppermute | solution.py:230
  131.1 21.0 %collective-permute-start.10 = (bf16[192,3072]{1,0:T(8,128)(2,1)}, bf16[192,3072]{1,0:T(8,128)(2,1)}, u32[]{:S(2)}, u32[]{:S(2)}) collective-permute-start(bf16[192,3072]{1,0:T(8,128)(2,1)} %slice.7), channel_id=1, source_target_pairs={{8,16},{12,20},{16,8},{20,12},{9,17},{13,21},{17,9},{21,13},{10,18... | collective-permute-start | bytes 3538952 | tf_op jit(solution)/shard_map/ppermute | solution.py:230
  132.8 28.7 %collective-permute-start.9 = (bf16[192,3072]{1,0:T(8,128)(2,1)}, bf16[192,3072]{1,0:T(8,128)(2,1)S(1)}, u32[]{:S(2)}, u32[]{:S(2)}) collective-permute-start(bf16[192,3072]{1,0:T(8,128)(2,1)} %slice.7), channel_id=1, source_target_pairs={{0,8},{4,12},{8,0},{12,4},{16,24},{20,28},{24,16},{28,20},{1,9},{5... | collective-permute-start | bytes 3538952 | tf_op jit(solution)/shard_map/ppermute | solution.py:230
  135.1 57.7 %collective-permute-start.16 = (bf16[320,3072]{1,0:T(8,128)(2,1)S(1)}, bf16[320,3072]{1,0:T(8,128)(2,1)}, u32[]{:S(2)}, u32[]{:S(2)}) collective-permute-start(bf16[320,3072]{1,0:T(8,128)(2,1)S(1)} %broadcast_select_fusion.refs_6_.refs_1_), channel_id=1, source_target_pairs={{0,1},{1,0},{2,3},{3,2},{4,5},{5,4},{6,7},{7,6},{8,9},{9,8},{10,11... | collective-permute-start | bytes 5898248 | tf_op jit(solution)/shard_map/ppermute | solution.py:230
  137.4 55.4 %collective-permute-start.17 = (bf16[320,3072]{1,0:T(8,128)(2,1)S(1)}, bf16[320,3072]{1,0:T(8,128)(2,1)}, u32[]{:S(2)}, u32[]{:S(2)}) collective-permute-start(bf16[320,3072]{1,0:T(8,128)(2,1)S(1)} %broadcast_select_fusion.refs_6_.refs_1_), channel_id=1, source_target_pairs={{0,2},{1,3},{2,0},{3,1},{4,6},{5,7},{6,4},{7,5},{8,10},{9,11},{10,... | collective-permute-start | bytes 5898248 | tf_op jit(solution)/shard_map/ppermute | solution.py:230
  161.6 3.0 copy-start.3
  161.6 31.2 %collective-permute-start.18 = (bf16[192,3072]{1,0:T(8,128)(2,1)}, bf16[192,3072]{1,0:T(8,128)(2,1)}, u32[]{:S(2)}, u32[]{:S(2)}) collective-permute-start(bf16[192,3072]{1,0:T(8,128)(2,1)} %collective-permute-done.10), channel_id=1, source_target_pairs={{8,0},{12,4},{16,24},{20,28},{9,1},{13,5},{17,25},{21,29},{10,2},{... | collective-permute-start | bytes 3538952 | tf_op jit(solution)/shard_map/ppermute | solution.py:230
  162.9 29.9 %collective-permute-start.19 = (bf16[192,3072]{1,0:T(8,128)(2,1)S(1)}, bf16[192,3072]{1,0:T(8,128)(2,1)}, u32[]{:S(2)}, u32[]{:S(2)}) collective-permute-start(bf16[192,3072]{1,0:T(8,128)(2,1)S(1)} %collective-permute-done.9.refs_1_), channel_id=1, source_target_pairs={{8,16},{12,20},{16,8},{20,12},{9,17},{13,21},{17,9},{21,13},{10,18... | collective-permute-start | bytes 3538952 | tf_op jit(solution)/shard_map/ppermute | solution.py:230
  192.8 6.6 %collective-permute-start.23 = (bf16[320,3072]{1,0:T(8,128)(2,1)}, bf16[320,3072]{1,0:T(8,128)(2,1)S(1)}, u32[]{:S(2)}, u32[]{:S(2)}) collective-permute-start(bf16[320,3072]{1,0:T(8,128)(2,1)} %collective-permute-done.16.x_ref.refs_8_.refs_3_), channel_id=1, source_target_pairs={{0,4},{4,0},{8,12},{12,8},{16,20},{20,16},{24,28},{28,24},{1,5},{5... | collective-permute-start | bytes 5898248 | tf_op jit(solution)/shard_map/ppermute | solution.py:230
  192.8 7.1 %collective-permute-start.24 = (bf16[320,3072]{1,0:T(8,128)(2,1)}, bf16[320,3072]{1,0:T(8,128)(2,1)}, u32[]{:S(2)}, u32[]{:S(2)}) collective-permute-start(bf16[320,3072]{1,0:T(8,128)(2,1)} %collective-permute-done.17.y_ref.refs_9_.refs_4_), channel_id=1, source_target_pairs={{0,4},{4,0},{8,12},{12,8},{16,20},{20,16},{24,28},{28,24},{1,5},{5... | collective-permute-start | bytes 5898248 | tf_op jit(solution)/shard_map/ppermute | solution.py:230
  193.3 33.6 %collective-permute-start.22 = (bf16[192,3072]{1,0:T(8,128)(2,1)}, bf16[192,3072]{1,0:T(8,128)(2,1)}, u32[]{:S(2)}, u32[]{:S(2)}) collective-permute-start(bf16[192,3072]{1,0:T(8,128)(2,1)} %collective-permute-done.19), channel_id=1, source_target_pairs={{8,0},{12,4},{16,24},{20,28},{9,1},{13,5},{17,25},{21,29},{10,2},{... | collective-permute-start | bytes 3538952 | tf_op jit(solution)/shard_map/ppermute | solution.py:230
  197.2 27.4 %collective-permute-start.20 = (bf16[160,3072]{1,0:T(8,128)(2,1)}, bf16[160,3072]{1,0:T(8,128)(2,1)S(1)}, u32[]{:S(2)}, u32[]{:S(2)}) collective-permute-start(bf16[160,3072]{1,0:T(8,128)(2,1)} %get-tuple-element.92), channel_id=1, source_target_pairs={{0,1},{1,0},{2,3},{3,2},{4,5},{5,4},{6,7},{7,6},{8,9},{9,8},{10,11... | collective-permute-start | bytes 2949128 | tf_op jit(solution)/shard_map/ppermute | solution.py:230
  197.8 26.8 %collective-permute-start.21 = (bf16[160,3072]{1,0:T(8,128)(2,1)}, bf16[160,3072]{1,0:T(8,128)(2,1)}, u32[]{:S(2)}, u32[]{:S(2)}) collective-permute-start(bf16[160,3072]{1,0:T(8,128)(2,1)} %get-tuple-element.93), channel_id=1, source_target_pairs={{0,2},{1,3},{2,0},{3,1},{4,6},{5,7},{6,4},{7,5},{8,10},{9,11},{10,... | collective-permute-start | bytes 2949128 | tf_op jit(solution)/shard_map/ppermute | solution.py:230
  199.3 1.3 copy-start.2
  224.6 5.1 %copy-start.7 = (bf16[160,3072]{1,0:T(8,128)(2,1)}, bf16[160,3072]{1,0:T(8,128)(2,1)S(1)}, u32[]{:S(2)}) copy-start(bf16[160,3072]{1,0:T(8,128)(2,1)S(1)} %collective-permute-done.20.refs_4_.refs_7_) | copy-start | bytes 2949124
  229.7 22.2 %copy-start.4 = (bf16[384,3072]{1,0:T(8,128)(2,1)}, bf16[384,3072]{1,0:T(8,128)(2,1)S(1)}, u32[]{:S(2)}) copy-start(bf16[384,3072]{1,0:T(8,128)(2,1)S(1)} %maximum_select_fusion.refs_1_) | copy-start | bytes 7077892
  229.7 9.0 %collective-permute-start.29 = (bf16[384,3072]{1,0:T(8,128)(2,1)S(1)}, bf16[384,3072]{1,0:T(8,128)(2,1)}, u32[]{:S(2)}, u32[]{:S(2)}) collective-permute-start(bf16[384,3072]{1,0:T(8,128)(2,1)S(1)} %maximum_select_fusion.refs_1_), channel_id=1, source_target_pairs={{0,4},{4,0},{8,12},{12,8},{16,20},{20,16},{24,28},{28,24},{1,5},{5... | collective-permute-start | bytes 7077896 | tf_op jit(solution)/shard_map/ppermute | solution.py:230
  229.8 7.0 %collective-permute-start.27 = (bf16[160,3072]{1,0:T(8,128)(2,1)S(1)}, bf16[160,3072]{1,0:T(8,128)(2,1)S(1)}, u32[]{:S(2)}, u32[]{:S(2)}) collective-permute-start(bf16[160,3072]{1,0:T(8,128)(2,1)S(1)} %collective-permute-done.20.refs_4_.refs_7_), channel_id=1, source_target_pairs={{0,4},{4,0},{8,12},{12,8},{16,20},{20,16},{24,28},{28,24},{1,5},{5... | collective-permute-start | bytes 2949128 | tf_op jit(solution)/shard_map/ppermute | solution.py:230
  230.2 7.4 %collective-permute-start.28 = (bf16[160,3072]{1,0:T(8,128)(2,1)}, bf16[160,3072]{1,0:T(8,128)(2,1)S(1)}, u32[]{:S(2)}, u32[]{:S(2)}) collective-permute-start(bf16[160,3072]{1,0:T(8,128)(2,1)} %collective-permute-done.21.refs_5_.refs_8_), channel_id=1, source_target_pairs={{0,4},{4,0},{8,12},{12,8},{16,20},{20,16},{24,28},{28,24},{1,5},{5... | collective-permute-start | bytes 2949128 | tf_op jit(solution)/shard_map/ppermute | solution.py:230
  230.3 53.7 %collective-permute-start.25 = (bf16[384,3072]{1,0:T(8,128)(2,1)S(1)}, bf16[384,3072]{1,0:T(8,128)(2,1)}, u32[]{:S(2)}, u32[]{:S(2)}) collective-permute-start(bf16[384,3072]{1,0:T(8,128)(2,1)S(1)} %maximum_select_fusion.refs_1_), channel_id=1, source_target_pairs={{0,1},{1,0},{2,3},{3,2},{4,5},{5,4},{6,7},{7,6},{8,9},{9,8},{10,11... | collective-permute-start | bytes 7077896 | tf_op jit(solution)/shard_map/ppermute | solution.py:230
  230.9 53.4 %collective-permute-start.26 = (bf16[384,3072]{1,0:T(8,128)(2,1)S(1)}, bf16[384,3072]{1,0:T(8,128)(2,1)}, u32[]{:S(2)}, u32[]{:S(2)}) collective-permute-start(bf16[384,3072]{1,0:T(8,128)(2,1)S(1)} %maximum_select_fusion.refs_1_), channel_id=1, source_target_pairs={{0,2},{1,3},{2,0},{3,1},{4,6},{5,7},{6,4},{7,5},{8,10},{9,11},{10,... | collective-permute-start | bytes 7077896 | tf_op jit(solution)/shard_map/ppermute | solution.py:230
  251.9 40.0 %collective-permute-start.30 = (bf16[256,3072]{1,0:T(8,128)(2,1)}, bf16[256,3072]{1,0:T(8,128)(2,1)}, u32[]{:S(2)}, u32[]{:S(2)}) collective-permute-start(bf16[256,3072]{1,0:T(8,128)(2,1)} %get-tuple-element.107), channel_id=1, source_target_pairs={{0,8},{4,12},{8,0},{12,4},{16,24},{20,28},{24,16},{28,20},{1,9},{5... | collective-permute-start | bytes 4718600 | tf_op jit(solution)/shard_map/ppermute | solution.py:230
  291.9 8.1 %collective-permute-start.33 = (bf16[384,3072]{1,0:T(8,128)(2,1)}, bf16[384,3072]{1,0:T(8,128)(2,1)S(1)}, u32[]{:S(2)}, u32[]{:S(2)}) collective-permute-start(bf16[384,3072]{1,0:T(8,128)(2,1)} %collective-permute-done.25.x_ref.refs_3_), channel_id=1, source_target_pairs={{0,4},{4,0},{8,12},{12,8},{16,20},{20,16},{24,28},{28,24},{1,5},{5... | collective-permute-start | bytes 7077896 | tf_op jit(solution)/shard_map/ppermute | solution.py:230
  291.9 8.2 %collective-permute-start.34 = (bf16[384,3072]{1,0:T(8,128)(2,1)}, bf16[384,3072]{1,0:T(8,128)(2,1)}, u32[]{:S(2)}, u32[]{:S(2)}) collective-permute-start(bf16[384,3072]{1,0:T(8,128)(2,1)} %collective-permute-done.26.y_ref.refs_4_), channel_id=1, source_target_pairs={{0,4},{4,0},{8,12},{12,8},{16,20},{20,16},{24,28},{28,24},{1,5},{5... | collective-permute-start | bytes 7077896 | tf_op jit(solution)/shard_map/ppermute | solution.py:230
  294.9 31.8 %collective-permute-start.31 = (bf16[192,3072]{1,0:T(8,128)(2,1)}, bf16[192,3072]{1,0:T(8,128)(2,1)S(1)}, u32[]{:S(2)}, u32[]{:S(2)}) collective-permute-start(bf16[192,3072]{1,0:T(8,128)(2,1)} %get-tuple-element.112), channel_id=1, source_target_pairs={{0,1},{1,0},{2,3},{3,2},{4,5},{5,4},{6,7},{7,6},{8,9},{9,8},{10,11... | collective-permute-start | bytes 3538952 | tf_op jit(solution)/shard_map/ppermute | solution.py:230
  296.5 30.3 %collective-permute-start.32 = (bf16[192,3072]{1,0:T(8,128)(2,1)}, bf16[192,3072]{1,0:T(8,128)(2,1)}, u32[]{:S(2)}, u32[]{:S(2)}) collective-permute-start(bf16[192,3072]{1,0:T(8,128)(2,1)} %get-tuple-element.113), channel_id=1, source_target_pairs={{0,2},{1,3},{2,0},{3,1},{4,6},{5,7},{6,4},{7,5},{8,10},{9,11},{10,... | collective-permute-start | bytes 3538952 | tf_op jit(solution)/shard_map/ppermute | solution.py:230
  297.0 36.1 %collective-permute-start.37 = (bf16[256,3072]{1,0:T(8,128)(2,1)}, bf16[256,3072]{1,0:T(8,128)(2,1)}, u32[]{:S(2)}, u32[]{:S(2)}) collective-permute-start(bf16[256,3072]{1,0:T(8,128)(2,1)} %get-tuple-element.120), channel_id=1, source_target_pairs={{0,8},{4,12},{8,0},{12,4},{16,24},{20,28},{24,16},{28,20},{1,9},{5... | collective-permute-start | bytes 4718600 | tf_op jit(solution)/shard_map/ppermute | solution.py:230
  300.0 1.5 copy-start.10
  326.8 6.3 %copy-start.11 = (bf16[192,3072]{1,0:T(8,128)(2,1)}, bf16[192,3072]{1,0:T(8,128)(2,1)S(1)}, u32[]{:S(2)}) copy-start(bf16[192,3072]{1,0:T(8,128)(2,1)S(1)} %collective-permute-done.31.refs_1_) | copy-start | bytes 3538948
  326.8 6.3 %collective-permute-start.35 = (bf16[192,3072]{1,0:T(8,128)(2,1)S(1)}, bf16[192,3072]{1,0:T(8,128)(2,1)S(1)}, u32[]{:S(2)}, u32[]{:S(2)}) collective-permute-start(bf16[192,3072]{1,0:T(8,128)(2,1)S(1)} %collective-permute-done.31.refs_1_), channel_id=1, source_target_pairs={{0,4},{4,0},{8,12},{12,8},{16,20},{20,16},{24,28},{28,24},{1,5},{5... | collective-permute-start | bytes 3538952 | tf_op jit(solution)/shard_map/ppermute | solution.py:230
  327.0 6.1 %collective-permute-start.36 = (bf16[192,3072]{1,0:T(8,128)(2,1)}, bf16[192,3072]{1,0:T(8,128)(2,1)S(1)}, u32[]{:S(2)}, u32[]{:S(2)}) collective-permute-start(bf16[192,3072]{1,0:T(8,128)(2,1)} %collective-permute-done.32.refs_2_), channel_id=1, source_target_pairs={{0,4},{4,0},{8,12},{12,8},{16,20},{20,16},{24,28},{28,24},{1,5},{5... | collective-permute-start | bytes 3538952 | tf_op jit(solution)/shard_map/ppermute | solution.py:230
  (6 other events, 6.5 us)

commit v3 on v2

--- a/solution.py
+++ b/solution.py
@@ -10,7 +10,7 @@
 NMAT = 32
 ROW_TILE = 256
 LANES = 128
-VMEM_BYTES = 60 * 1024 * 1024
+VMEM_BYTES = 63 * 1024 * 1024 + 512 * 1024
 
 
 def trace_kernel(feat, x_ref, out_ref, left, right, prod):
@@ -218,10 +218,53 @@
     )(from_x, from_y)
 
 
+def join_kernel(parts, a_ref, b_ref, c_ref, out_ref, low_ref, high_ref, buf, sem):
+    rows, feat = a_ref.shape
+    size = rows // parts
+    spans = [pl.ds(n * size, size) for n in range(parts)]
+    loads = [
+        [
+            pltpu.make_async_copy(ref.at[span], buf.at[span, pl.ds(f * feat, feat)], sem.at[f, n])
+            for f, ref in enumerate((a_ref, b_ref, c_ref))
+        ]
+        for n, span in enumerate(spans)
+    ]
+    stores = [pltpu.make_async_copy(buf.at[span], out_ref.at[span], sem.at[3, n]) for n, span in enumerate(spans)]
+    for copies in loads:
+        for copy in copies:
+            copy.start()
+    for copies, store in zip(loads, stores):
+        for copy in copies:
+            copy.wait()
+        store.start()
+    low = low_ref.shape[0]
+    stores.append(pltpu.make_async_copy(buf.at[pl.ds(0, low)], low_ref, sem.at[4, 0]))
+    stores.append(pltpu.make_async_copy(buf.at[pl.ds(low, rows - low)], high_ref, sem.at[4, 1]))
+    for store in stores[-2:]:
+        store.start()
+    for store in stores:
+        store.wait()
+
+
+def side_by_side(a, b, c, low):
+    rows, feat = a.shape
+    parts = 4
+    spec = pl.BlockSpec(memory_space=pltpu.HBM)
+    outs = [jax.ShapeDtypeStruct((n, 3 * feat), a.dtype) for n in (rows, low, rows - low)]
+    return pl.pallas_call(
+        functools.partial(join_kernel, parts),
+        in_specs=[spec] * 3,
+        out_specs=[spec] * 3,
+        out_shape=outs,
+        scratch_shapes=[pltpu.VMEM(outs[0].shape, a.dtype), pltpu.SemaphoreType.DMA((5, parts))],
+        cost_estimate=pl.CostEstimate(flops=rows, bytes_accessed=feat, transcendentals=0),
+    )(a, b, c)
+
+
 def near_shards(factor_a, factor_b, factor_c):
-    x = jnp.concatenate([factor_a, factor_b, factor_c], axis=1)
-    rows = x.shape[0]
+    rows = factor_a.shape[0]
     early = rows * 5 // 8
+    x, part_a, part_c = side_by_side(factor_a, factor_b, factor_c, early)
     row = lax.axis_index("row")
     inner = (row >= 2) & (row < 6)
     fence = lax.optimization_barrier
@@ -241,35 +284,28 @@
         return along_x(low), along_y(high)
 
     x_x, x_y, x_s = along_x(x), along_y(x), core(x)
-    x_z, x_s = fence((x, x_s))
-    part_a, part_c = x_z[:early], x_z[early:]
     guest_a, far_a = partner(part_a), across(part_a)
     home = trace_terms(x)
     (home,) = pair_sums([x], [x, x_s], [home], 1024)
-    guest_a, far_a, home = fence((guest_a, far_a, home))
-
+    guest_a, far_a, part_c, home = fence((guest_a, far_a, part_c, home))
+
+    guest_c, far_c = partner(part_c), across(part_c)
+    x_x, x_y, guest_c, far_c, home = fence((x_x, x_y, guest_c, far_c, home))
+
+    guest = [guest_a, guest_c]
     out_a, next_b = outward(far_a), across(guest_a)
-    x_x, x_y, home = fence((x_x, x_y, home))
-
     x_d0, x_d1 = corner(x_x, x_y)
     x_xs, x_ys = fence((core(x_x), core(x_y)))
-    (home,) = pair_sums([x], [x_x, x_y, x_xs, x_ys], [home], 1024)
-    out_a, next_b, part_c, home = fence((out_a, next_b, part_c, home))
-
-    guest_c, far_c = partner(part_c), across(part_c)
-    x_d0, x_d1, out_a, next_b, home = fence((x_d0, x_d1, out_a, next_b, home))
+    (visit,) = pair_sums(guest, [x, x_s, x_x, x_y, x_xs, x_ys], None, 1024)
+    x_d0, x_d1, out_a, next_b, visit = fence((x_d0, x_d1, out_a, next_b, visit))
 
     e = jnp.where(inner, next_b, out_a)
     e_x, e_y = along_x(e), along_y(e)
     x_ds0, x_ds1, e_s = fence((core(x_d0), core(x_d1), core(e)))
     x_d = [x_d0, x_d1, x_ds0, x_ds1]
-    (home,) = pair_sums([x], x_d, [home], 1024)
-    guest_c, far_c, home = fence((guest_c, far_c, home))
-
-    guest = [guest_a, guest_c]
     out_c0, next_c = outward(far_c), across(guest_c)
-    (visit,) = pair_sums(guest, [x, x_s, x_x, x_y, x_xs, x_ys], None, 1024)
-    e_x, e_y, out_c0, next_c, home, visit = fence((e_x, e_y, out_c0, next_c, home, visit))
+    (home,) = pair_sums([x], [x_x, x_y, x_xs, x_ys, *x_d], [home], 1024)
+    e_x, e_y, out_c0, next_c, home = fence((e_x, e_y, out_c0, next_c, home))
 
     e_d0, e_d1 = corner(e_x, e_y)
     out_c1 = outward(next_c)

time: 349 us -> 333 us (0.954)
  local copies, waits for them, and re-layouts: 17.9 us -> 0 us
    unnamed x34 -> x0, local copies, waits for them, and re-layouts: 11.5 us -> none
    slice x2 -> x0, local copies, waits for them, and re-layouts: 5.29 us -> none  [near_shards(): part_a, part_c = (x_z[:early], x_z[early:])]
    pallas_call x0 -> x1, Pallas kernels: none -> 3.98 us  [side_by_side(): pl.pallas_call(functools.partial(join_kernel, parts), in_specs=[spec] * 3...]
    pallas_call x9 -> x8, Pallas kernels: 175 us -> 171 us  [pair_sums(): pl.pallas_call(functools.partial(pair_kernel, feat, i_rows, spans, tile,...]
  transfers between devices with their start and end apart: 38 -> 38, of which waited for: 16 -> 16; matrix products, arithmetic and copies ran while one was open for 2% -> 1% of each run, Pallas kernels for 56% -> 57%
where the time goes in v3:
time: 333 us; the launch traced here: 332 us
  Pallas kernels  207 us (62%)
  waiting for transfers between devices  75.2 us (23%)
  starting transfers between devices  42.7 us (13%)
  other arithmetic  6.72 us (2%)
    pallas_call x8, Pallas kernels, pair_sums(): pl.pallas_call(functools.partial(pair_kernel, feat, i_rows, spans, tile,...  171 us
    ppermute x38, waiting for transfers between devices, move(): return lambda v: lax.ppermute(v, axis, pairs)  75.2 us
    ppermute x38, starting transfers between devices, move(): return lambda v: lax.ppermute(v, axis, pairs)  42.7 us
    pallas_call x1, Pallas kernels, trace_terms(): pl.pallas_call(functools.partial(trace_kernel, feat), grid=(rows // LANES...  23.9 us
    pallas_call x3, Pallas kernels, cut(): pl.pallas_call(functools.partial(cut_kernel, mid, parts), in_specs=[spec]...  7.75 us
  transfers between devices with their start and end apart: 38, of which 16 were waited for; matrix products, arithmetic and copies ran while one was open for 1% of the time, Pallas kernels for 57%

profile of v3, /device:TPU:0, one launch (start us, length us, event | category | flops | bytes accessed | tf_op | source)
XLA Modules:
  0.0 332.4 jit_solution(11211543162289554829)
XLA Ops:
  0.6 4.0 %shard_map.58 = (bf16[512,3072]{1,0:T(8,128)(2,1)}, bf16[320,3072]{1,0:T(8,128)(2,1)}, bf16[192,3072]{1,0:T(8,128)(2,1)}) custom-call(bf16[512,1024]{1,0:T(8,128)(2,1)} %a_ref.1, bf16[512,1024]{1,0:T(8,128)(2,1)} %b_ref.1, bf16[512,1024]{1,0:T(8,128)(2,1)} %c_ref.1), custom_call_target="tpu_custom_call" | custom-call | flops 512 | bytes 1024 | tf_op jit(solution)/shard_map/pallas_call | solution.py:254
  5.1 2.7 collective-permute-start.2
  7.8 1.9 collective-permute-start.3
  9.7 1.5 collective-permute-start
  11.2 1.5 collective-permute-start.1
  12.7 23.9 %shard_map.59.refs_3_ = f32[512,3072]{1,0:T(8,128)} custom-call(bf16[512,3072]{1,0:T(8,128)(2,1)} %get-tuple-element.58.x_ref.refs_0_.refs_1_.refs_2_), custom_call_target="tpu_custom_call" | custom-call | flops 512 | bytes 3072 | tf_op jit(solution)/shard_map/pallas_call | solution.py:42
  36.6 13.2 %shard_map.60.refs_9_ = f32[512,3072]{1,0:T(8,128)} custom-call(bf16[512,3072]{1,0:T(8,128)(2,1)} %get-tuple-element.58.x_ref.refs_0_.refs_1_.refs_2_, bf16[512,3072]{1,0:T(8,128)(2,1)} %get-tuple-element.58.x_ref.refs_0_.refs_1_.refs_2_, bf16[512,3072]{1,0:T(8,128)(2,1)} %collective-permute-done.4.refs_2_.refs_3_, ...), custom_call_target="tpu_custom_call", output_to_operand_aliasing={{}: (3, {})} | custom-call | flops 512 | bytes 3072 | tf_op jit(solution)/shard_map/pallas_call | solution.py:177
  49.9 1.7 collective-permute-done.2.refs_0_
  51.5 4.8 %collective-permute-start.5 = (bf16[192,3072]{1,0:T(8,128)(2,1)}, bf16[192,3072]{1,0:T(8,128)(2,1)}, u32[]{:S(2)}, u32[]{:S(2)}) collective-permute-start(bf16[192,3072]{1,0:T(8,128)(2,1)} %get-tuple-element.61), channel_id=1, source_target_pairs={{0,8},{4,12},{8,0},{12,4},{16,24},{20,28},{24,16},{28,20},{1,9},{5... | collective-permute-start | bytes 3538952 | tf_op jit(solution)/shard_map/ppermute | solution.py:273
  56.3 1.8 collective-permute-start.6
  58.1 22.1 %collective-permute-done.x_ref.refs_4_.refs_1_ = bf16[512,3072]{1,0:T(8,128)(2,1)} collective-permute-done((bf16[512,3072]{1,0:T(8,128)(2,1)}, bf16[512,3072]{1,0:T(8,128)(2,1)}, u32[]{:S(2)}, u32[]{:S(2)}) %collective-permute-start) | collective-permute-done | bytes 3145760 | tf_op jit(solution)/shard_map/ppermute | solution.py:273
  80.2 1.2 collective-permute-done.1.y_ref.refs_5_.refs_2_
  81.4 1.0 collective-permute-done.5.refs_1_
  82.9 1.9 collective-permute-start.10
  84.9 1.3 collective-permute-start.9
  86.2 2.9 shard_map.61
  89.0 1.6 collective-permute-start.7
  90.6 1.5 collective-permute-start.8
  92.9 28.1 %shard_map.62.refs_11_ = f32[512,3072]{1,0:T(8,128)} custom-call(bf16[320,3072]{1,0:T(8,128)(2,1)} %collective-permute-done.2.refs_0_, bf16[192,3072]{1,0:T(8,128)(2,1)} %collective-permute-done.5.refs_1_, bf16[512,3072]{1,0:T(8,128)(2,1)} %get-tuple-element.58.x_ref.refs_0_.refs_1_.refs_2_, bf16[512,3072]{1,0:T(8,128)(2,1)} %collective-permute-done.4.refs_2_.refs_3_, ...), custom_call_target="tpu_custom_call" | custom-call | flops 512 | bytes 3072 | tf_op jit(solution)/shard_map/pallas_call | solution.py:177
  121.1 13.1 %collective-permute-done.9 = bf16[320,3072]{1,0:T(8,128)(2,1)} collective-permute-done((bf16[320,3072]{1,0:T(8,128)(2,1)}, bf16[320,3072]{1,0:T(8,128)(2,1)}, u32[]{:S(2)}, u32[]{:S(2)}) %collective-permute-start.9) | collective-permute-done | bytes 1966112 | tf_op jit(solution)/shard_map/ppermute | solution.py:273
  134.7 3.0 broadcast_select_fusion.refs_6_.refs_1_
  137.8 1.5 collective-permute-start.13
  139.3 1.5 collective-permute-start.14
  140.8 1.7 collective-permute-start.16
  142.5 1.5 collective-permute-start.15
  144.0 29.6 %shard_map.63.refs_11_ = f32[512,3072]{1,0:T(8,128)} custom-call(bf16[512,3072]{1,0:T(8,128)(2,1)} %get-tuple-element.58.x_ref.refs_0_.refs_1_.refs_2_, bf16[512,3072]{1,0:T(8,128)(2,1)} %collective-permute-done.x_ref.refs_4_.refs_1_, bf16[512,3072]{1,0:T(8,128)(2,1)} %collective-permute-done.1.y_ref.refs_5_.refs_2_, ...), custom_call_target="tpu_custom_call", output_to_operand_aliasing={{}: (9, {})} | custom-call | flops 512 | bytes 3072 | tf_op jit(solution)/shard_map/pallas_call | solution.py:177
  173.5 9.7 %collective-permute-done.13.x_ref.refs_8_.refs_3_ = bf16[320,3072]{1,0:T(8,128)(2,1)} collective-permute-done((bf16[320,3072]{1,0:T(8,128)(2,1)}, bf16[320,3072]{1,0:T(8,128)(2,1)}, u32[]{:S(2)}, u32[]{:S(2)}) %collective-permute-start.13) | collective-permute-done | bytes 1966112 | tf_op jit(solution)/shard_map/ppermute | solution.py:273
  183.3 1.2 collective-permute-done.14.y_ref.refs_9_.refs_4_
  185.0 1.3 collective-permute-start.22
  186.3 2.4 shard_map.64
  189.2 1.5 collective-permute-start.21
  191.6 24.0 %shard_map.65.refs_8_ = f32[512,3072]{1,0:T(8,128)} custom-call(bf16[320,3072]{1,0:T(8,128)(2,1)} %collective-permute-done.2.refs_0_, bf16[192,3072]{1,0:T(8,128)(2,1)} %collective-permute-done.5.refs_1_, bf16[256,3072]{1,0:T(8,128)(2,1)} %collective-permute-done.7.refs_5_.refs_2_, ...), custom_call_target="tpu_custom_call", output_to_operand_aliasing={{}: (11, {})} | custom-call | flops 512 | bytes 3072 | tf_op jit(solution)/shard_map/pallas_call | solution.py:177
  215.6 3.7 %maximum_select_fusion.refs_1_ = bf16[384,3072]{1,0:T(8,128)(2,1)} fusion(bf16[192,3072]{1,0:T(8,128)(2,1)} %collective-permute-done.16, bf16[192,3072]{1,0:T(8,128)(2,1)} %collective-permute-done.6, bf16[192,3072]{1,0:T(8,128)(2,1)} %collective-permute-done.22, bf16[192,3072]{1,0:T(8,128)(2,1)} %collective-permute-done.15, pred[]{:T(512)S(6)} %and.4), kind=kLoop, calls=%fused_computation | loop fusion | flops 10616832 | bytes 7077889 | tf_op jit(solution)/shard_map/jit(_where)/select_n | solution.py:317
  220.5 1.5 collective-permute-start.26
  222.0 3.6 %collective-permute-done.27.refs_6_.refs_9_ = bf16[160,3072]{1,0:T(8,128)(2,1)} collective-permute-done((bf16[160,3072]{1,0:T(8,128)(2,1)}, bf16[160,3072]{1,0:T(8,128)(2,1)}, u32[]{:S(2)}, u32[]{:S(2)}) %collective-permute-start.27) | collective-permute-done | bytes 983072 | tf_op jit(solution)/shard_map/ppermute | solution.py:273
  225.6 1.4 collective-permute-done.28.refs_7_.refs_10_
  227.0 13.1 %shard_map.66 = (bf16[256,3072]{1,0:T(8,128)(2,1)}, bf16[256,3072]{1,0:T(8,128)(2,1)}) custom-call(bf16[320,3072]{1,0:T(8,128)(2,1)} %collective-permute-done.2.refs_0_, bf16[192,3072]{1,0:T(8,128)(2,1)} %collective-permute-done.5.refs_1_, bf16[320,3072]{1,0:T(8,128)(2,1)} %collective-permute-done.23.refs_10_.refs_2_.refs_5_, ...), custom_call_target="tpu_custom_call" | custom-call | flops 512 | bytes 3072 | tf_op jit(solution)/shard_map/pallas_call | solution.py:177
  240.1 3.0 collective-permute-start.30
  243.0 25.0 %shard_map.67.refs_7_ = f32[512,3072]{1,0:T(8,128)} custom-call(bf16[512,3072]{1,0:T(8,128)(2,1)} %get-tuple-element.58.x_ref.refs_0_.refs_1_.refs_2_, bf16[320,3072]{1,0:T(8,128)(2,1)} %broadcast_select_fusion.refs_6_.refs_1_, bf16[320,3072]{1,0:T(8,128)(2,1)} %collective-permute-done.19.refs_7_.refs_2_, ...), custom_call_target="tpu_custom_call", output_to_operand_aliasing={{}: (11, {})} | custom-call | flops 512 | bytes 3072 | tf_op jit(solution)/shard_map/pallas_call | solution.py:177
  268.0 5.8 %collective-permute-done.25.x_ref.refs_3_ = bf16[384,3072]{1,0:T(8,128)(2,1)} collective-permute-done((bf16[384,3072]{1,0:T(8,128)(2,1)}, bf16[384,3072]{1,0:T(8,128)(2,1)}, u32[]{:S(2)}, u32[]{:S(2)}) %collective-permute-start.25) | collective-permute-done | bytes 2359328 | tf_op jit(solution)/shard_map/ppermute | solution.py:273
  274.2 3.9 %collective-permute-done.30.refs_6_ = bf16[256,3072]{1,0:T(8,128)(2,1)} collective-permute-done((bf16[256,3072]{1,0:T(8,128)(2,1)}, bf16[256,3072]{1,0:T(8,128)(2,1)}, u32[]{:S(2)}, u32[]{:S(2)}) %collective-permute-start.30) | collective-permute-done | bytes 1572896 | tf_op jit(solution)/shard_map/ppermute | solution.py:273
  278.6 2.5 shard_map.68
  281.1 1.6 collective-permute-start.31
  283.2 1.7 collective-permute-start.37
  284.9 1.4 collective-permute-done.34.refs_6_
  286.3 25.2 %shard_map.69.refs_5_ = f32[512,3072]{1,0:T(8,128)} custom-call(bf16[512,3072]{1,0:T(8,128)(2,1)} %get-tuple-element.58.x_ref.refs_0_.refs_1_.refs_2_, bf16[384,3072]{1,0:T(8,128)(2,1)} %maximum_select_fusion.refs_1_, bf16[384,3072]{1,0:T(8,128)(2,1)} %collective-permute-done.29.refs_2_, ...), custom_call_target="tpu_custom_call", output_to_operand_aliasing={{}: (7, {})} | custom-call | flops 512 | bytes 3072 | tf_op jit(solution)/shard_map/pallas_call | solution.py:177
  312.2 7.1 %collective-permute-done.37.refs_7_ = bf16[256,3072]{1,0:T(8,128)(2,1)} collective-permute-done((bf16[256,3072]{1,0:T(8,128)(2,1)}, bf16[256,3072]{1,0:T(8,128)(2,1)}, u32[]{:S(2)}, u32[]{:S(2)}) %collective-permute-start.37) | collective-permute-done | bytes 1572896 | tf_op jit(solution)/shard_map/ppermute | solution.py:273
  319.2 12.9 %shard_map.70 = (f32[512,1024]{1,0:T(8,128)}, f32[512,1024]{1,0:T(8,128)}, f32[512,1024]{1,0:T(8,128)}) custom-call(bf16[512,3072]{1,0:T(8,128)(2,1)} %get-tuple-element.58.x_ref.refs_0_.refs_1_.refs_2_, bf16[192,3072]{1,0:T(8,128)(2,1)} %collective-permute-done.31.refs_1_, bf16[192,3072]{1,0:T(8,128)(2,1)} %collective-permute-done.32.refs_2_, ...), custom_call_target="tpu_custom_call" | custom-call | flops 512 | bytes 3072 | tf_op jit(solution)/shard_map/pallas_call | solution.py:177
  (43 shorter events, 7.6 us)
Async XLA Ops:
  4.6 32.0 %collective-permute-start.4 = (bf16[512,3072]{1,0:T(8,128)(2,1)}, bf16[512,3072]{1,0:T(8,128)(2,1)}, u32[]{:S(2)}, u32[]{:S(2)}) collective-permute-start(bf16[512,3072]{1,0:T(8,128)(2,1)} %get-tuple-element.58.x_ref.refs_0_.refs_1_.refs_2_), channel_id=1, source_target_pairs={{0,4},{4,0},{8,12},{12,8},{16,20},{20,16},{24,28},{28,24},{1,5},{5... | collective-permute-start | bytes 9437192 | tf_op jit(solution)/shard_map/ppermute | solution.py:273
  5.1 46.4 %collective-permute-start.2 = (bf16[320,3072]{1,0:T(8,128)(2,1)}, bf16[320,3072]{1,0:T(8,128)(2,1)}, u32[]{:S(2)}, u32[]{:S(2)}) collective-permute-start(bf16[320,3072]{1,0:T(8,128)(2,1)} %get-tuple-element.59), channel_id=1, source_target_pairs={{0,8},{4,12},{8,0},{12,4},{16,24},{20,28},{24,16},{28,20},{1,9},{5... | collective-permute-start | bytes 5898248 | tf_op jit(solution)/shard_map/ppermute | solution.py:273
  7.8 43.7 %collective-permute-start.3 = (bf16[320,3072]{1,0:T(8,128)(2,1)}, bf16[320,3072]{1,0:T(8,128)(2,1)}, u32[]{:S(2)}, u32[]{:S(2)}) collective-permute-start(bf16[320,3072]{1,0:T(8,128)(2,1)} %get-tuple-element.59), channel_id=1, source_target_pairs={{8,16},{12,20},{16,8},{20,12},{9,17},{13,21},{17,9},{21,13},{10,18... | collective-permute-start | bytes 5898248 | tf_op jit(solution)/shard_map/ppermute | solution.py:273
  9.7 70.5 %collective-permute-start = (bf16[512,3072]{1,0:T(8,128)(2,1)}, bf16[512,3072]{1,0:T(8,128)(2,1)}, u32[]{:S(2)}, u32[]{:S(2)}) collective-permute-start(bf16[512,3072]{1,0:T(8,128)(2,1)} %get-tuple-element.58.x_ref.refs_0_.refs_1_.refs_2_), channel_id=1, source_target_pairs={{0,1},{1,0},{2,3},{3,2},{4,5},{5,4},{6,7},{7,6},{8,9},{9,8},{10,11... | collective-permute-start | bytes 9437192 | tf_op jit(solution)/shard_map/ppermute | solution.py:273
  11.2 70.2 %collective-permute-start.1 = (bf16[512,3072]{1,0:T(8,128)(2,1)}, bf16[512,3072]{1,0:T(8,128)(2,1)}, u32[]{:S(2)}, u32[]{:S(2)}) collective-permute-start(bf16[512,3072]{1,0:T(8,128)(2,1)} %get-tuple-element.58.x_ref.refs_0_.refs_1_.refs_2_), channel_id=1, source_target_pairs={{0,2},{1,3},{2,0},{3,1},{4,6},{5,7},{6,4},{7,5},{8,10},{9,11},{10,... | collective-permute-start | bytes 9437192 | tf_op jit(solution)/shard_map/ppermute | solution.py:273
  51.5 30.9 %collective-permute-start.5 = (bf16[192,3072]{1,0:T(8,128)(2,1)}, bf16[192,3072]{1,0:T(8,128)(2,1)}, u32[]{:S(2)}, u32[]{:S(2)}) collective-permute-start(bf16[192,3072]{1,0:T(8,128)(2,1)} %get-tuple-element.61), channel_id=1, source_target_pairs={{0,8},{4,12},{8,0},{12,4},{16,24},{20,28},{24,16},{28,20},{1,9},{5... | collective-permute-start | bytes 3538952 | tf_op jit(solution)/shard_map/ppermute | solution.py:273
  56.3 26.1 %collective-permute-start.6 = (bf16[192,3072]{1,0:T(8,128)(2,1)}, bf16[192,3072]{1,0:T(8,128)(2,1)}, u32[]{:S(2)}, u32[]{:S(2)}) collective-permute-start(bf16[192,3072]{1,0:T(8,128)(2,1)} %get-tuple-element.61), channel_id=1, source_target_pairs={{8,16},{12,20},{16,8},{20,12},{9,17},{13,21},{17,9},{21,13},{10,18... | collective-permute-start | bytes 3538952 | tf_op jit(solution)/shard_map/ppermute | solution.py:273
  82.4 8.2 %collective-permute-start.11 = (bf16[512,3072]{1,0:T(8,128)(2,1)}, bf16[512,3072]{1,0:T(8,128)(2,1)}, u32[]{:S(2)}, u32[]{:S(2)}) collective-permute-start(bf16[512,3072]{1,0:T(8,128)(2,1)} %collective-permute-done.x_ref.refs_4_.refs_1_), channel_id=1, source_target_pairs={{0,4},{4,0},{8,12},{12,8},{16,20},{20,16},{24,28},{28,24},{1,5},{5... | collective-permute-start | bytes 9437192 | tf_op jit(solution)/shard_map/ppermute | solution.py:273
  82.4 10.5 %collective-permute-start.12 = (bf16[512,3072]{1,0:T(8,128)(2,1)}, bf16[512,3072]{1,0:T(8,128)(2,1)}, u32[]{:S(2)}, u32[]{:S(2)}) collective-permute-start(bf16[512,3072]{1,0:T(8,128)(2,1)} %collective-permute-done.1.y_ref.refs_5_.refs_2_), channel_id=1, source_target_pairs={{0,4},{4,0},{8,12},{12,8},{16,20},{20,16},{24,28},{28,24},{1,5},{5... | collective-permute-start | bytes 9437192 | tf_op jit(solution)/shard_map/ppermute | solution.py:273
  82.9 38.1 %collective-permute-start.10 = (bf16[320,3072]{1,0:T(8,128)(2,1)}, bf16[320,3072]{1,0:T(8,128)(2,1)}, u32[]{:S(2)}, u32[]{:S(2)}) collective-permute-start(bf16[320,3072]{1,0:T(8,128)(2,1)} %collective-permute-done.2.refs_0_), channel_id=1, source_target_pairs={{8,16},{12,20},{16,8},{20,12},{9,17},{13,21},{17,9},{21,13},{10,18... | collective-permute-start | bytes 5898248 | tf_op jit(solution)/shard_map/ppermute | solution.py:273
  84.9 49.3 %collective-permute-start.9 = (bf16[320,3072]{1,0:T(8,128)(2,1)}, bf16[320,3072]{1,0:T(8,128)(2,1)}, u32[]{:S(2)}, u32[]{:S(2)}) collective-permute-start(bf16[320,3072]{1,0:T(8,128)(2,1)} %collective-permute-done.3), channel_id=1, source_target_pairs={{8,0},{12,4},{16,24},{20,28},{9,1},{13,5},{17,25},{21,29},{10,2},{... | collective-permute-start | bytes 5898248 | tf_op jit(solution)/shard_map/ppermute | solution.py:273
  89.0 45.1 %collective-permute-start.7 = (bf16[256,3072]{1,0:T(8,128)(2,1)}, bf16[256,3072]{1,0:T(8,128)(2,1)}, u32[]{:S(2)}, u32[]{:S(2)}) collective-permute-start(bf16[256,3072]{1,0:T(8,128)(2,1)} %get-tuple-element.66), channel_id=1, source_target_pairs={{0,1},{1,0},{2,3},{3,2},{4,5},{5,4},{6,7},{7,6},{8,9},{9,8},{10,11... | collective-permute-start | bytes 4718600 | tf_op jit(solution)/shard_map/ppermute | solution.py:273
  90.6 43.6 %collective-permute-start.8 = (bf16[256,3072]{1,0:T(8,128)(2,1)}, bf16[256,3072]{1,0:T(8,128)(2,1)}, u32[]{:S(2)}, u32[]{:S(2)}) collective-permute-start(bf16[256,3072]{1,0:T(8,128)(2,1)} %get-tuple-element.67), channel_id=1, source_target_pairs={{0,2},{1,3},{2,0},{3,1},{4,6},{5,7},{6,4},{7,5},{8,10},{9,11},{10,... | collective-permute-start | bytes 4718600 | tf_op jit(solution)/shard_map/ppermute | solution.py:273
  134.2 6.6 %collective-permute-start.17 = (bf16[256,3072]{1,0:T(8,128)(2,1)}, bf16[256,3072]{1,0:T(8,128)(2,1)}, u32[]{:S(2)}, u32[]{:S(2)}) collective-permute-start(bf16[256,3072]{1,0:T(8,128)(2,1)} %collective-permute-done.7.refs_5_.refs_2_), channel_id=1, source_target_pairs={{0,4},{4,0},{8,12},{12,8},{16,20},{20,16},{24,28},{28,24},{1,5},{5... | collective-permute-start | bytes 4718600 | tf_op jit(solution)/shard_map/ppermute | solution.py:273
  134.2 8.3 %collective-permute-start.18 = (bf16[256,3072]{1,0:T(8,128)(2,1)}, bf16[256,3072]{1,0:T(8,128)(2,1)}, u32[]{:S(2)}, u32[]{:S(2)}) collective-permute-start(bf16[256,3072]{1,0:T(8,128)(2,1)} %collective-permute-done.8.refs_6_.refs_3_), channel_id=1, source_target_pairs={{0,4},{4,0},{8,12},{12,8},{16,20},{20,16},{24,28},{28,24},{1,5},{5... | collective-permute-start | bytes 4718600 | tf_op jit(solution)/shard_map/ppermute | solution.py:273
  137.7 6.2 %collective-permute-start.19 = (bf16[320,3072]{1,0:T(8,128)(2,1)}, bf16[320,3072]{1,0:T(8,128)(2,1)}, u32[]{:S(2)}, u32[]{:S(2)}) collective-permute-start(bf16[320,3072]{1,0:T(8,128)(2,1)} %broadcast_select_fusion.refs_6_.refs_1_), channel_id=1, source_target_pairs={{0,4},{4,0},{8,12},{12,8},{16,20},{20,16},{24,28},{28,24},{1,5},{5... | collective-permute-start | bytes 5898248 | tf_op jit(solution)/shard_map/ppermute | solution.py:273
  137.8 45.5 %collective-permute-start.13 = (bf16[320,3072]{1,0:T(8,128)(2,1)}, bf16[320,3072]{1,0:T(8,128)(2,1)}, u32[]{:S(2)}, u32[]{:S(2)}) collective-permute-start(bf16[320,3072]{1,0:T(8,128)(2,1)} %broadcast_select_fusion.refs_6_.refs_1_), channel_id=1, source_target_pairs={{0,1},{1,0},{2,3},{3,2},{4,5},{5,4},{6,7},{7,6},{8,9},{9,8},{10,11... | collective-permute-start | bytes 5898248 | tf_op jit(solution)/shard_map/ppermute | solution.py:273
  139.3 45.2 %collective-permute-start.14 = (bf16[320,3072]{1,0:T(8,128)(2,1)}, bf16[320,3072]{1,0:T(8,128)(2,1)}, u32[]{:S(2)}, u32[]{:S(2)}) collective-permute-start(bf16[320,3072]{1,0:T(8,128)(2,1)} %broadcast_select_fusion.refs_6_.refs_1_), channel_id=1, source_target_pairs={{0,2},{1,3},{2,0},{3,1},{4,6},{5,7},{6,4},{7,5},{8,10},{9,11},{10,... | collective-permute-start | bytes 5898248 | tf_op jit(solution)/shard_map/ppermute | solution.py:273
  140.8 32.7 %collective-permute-start.16 = (bf16[192,3072]{1,0:T(8,128)(2,1)}, bf16[192,3072]{1,0:T(8,128)(2,1)}, u32[]{:S(2)}, u32[]{:S(2)}) collective-permute-start(bf16[192,3072]{1,0:T(8,128)(2,1)} %collective-permute-done.5.refs_1_), channel_id=1, source_target_pairs={{8,16},{12,20},{16,8},{20,12},{9,17},{13,21},{17,9},{21,13},{10,18... | collective-permute-start | bytes 3538952 | tf_op jit(solution)/shard_map/ppermute | solution.py:273
  142.5 31.1 %collective-permute-start.15 = (bf16[192,3072]{1,0:T(8,128)(2,1)}, bf16[192,3072]{1,0:T(8,128)(2,1)}, u32[]{:S(2)}, u32[]{:S(2)}) collective-permute-start(bf16[192,3072]{1,0:T(8,128)(2,1)} %collective-permute-done.6), channel_id=1, source_target_pairs={{8,0},{12,4},{16,24},{20,28},{9,1},{13,5},{17,25},{21,29},{10,2},{... | collective-permute-start | bytes 3538952 | tf_op jit(solution)/shard_map/ppermute | solution.py:273
  184.5 6.3 %collective-permute-start.23 = (bf16[320,3072]{1,0:T(8,128)(2,1)}, bf16[320,3072]{1,0:T(8,128)(2,1)}, u32[]{:S(2)}, u32[]{:S(2)}) collective-permute-start(bf16[320,3072]{1,0:T(8,128)(2,1)} %collective-permute-done.13.x_ref.refs_8_.refs_3_), channel_id=1, source_target_pairs={{0,4},{4,0},{8,12},{12,8},{16,20},{20,16},{24,28},{28,24},{1,5},{5... | collective-permute-start | bytes 5898248 | tf_op jit(solution)/shard_map/ppermute | solution.py:273
  184.5 7.1 %collective-permute-start.24 = (bf16[320,3072]{1,0:T(8,128)(2,1)}, bf16[320,3072]{1,0:T(8,128)(2,1)}, u32[]{:S(2)}, u32[]{:S(2)}) collective-permute-start(bf16[320,3072]{1,0:T(8,128)(2,1)} %collective-permute-done.14.y_ref.refs_9_.refs_4_), channel_id=1, source_target_pairs={{0,4},{4,0},{8,12},{12,8},{16,20},{20,16},{24,28},{28,24},{1,5},{5... | collective-permute-start | bytes 5898248 | tf_op jit(solution)/shard_map/ppermute | solution.py:273
  185.0 30.6 %collective-permute-start.22 = (bf16[192,3072]{1,0:T(8,128)(2,1)}, bf16[192,3072]{1,0:T(8,128)(2,1)}, u32[]{:S(2)}, u32[]{:S(2)}) collective-permute-start(bf16[192,3072]{1,0:T(8,128)(2,1)} %collective-permute-done.16), channel_id=1, source_target_pairs={{8,0},{12,4},{16,24},{20,28},{9,1},{13,5},{17,25},{21,29},{10,2},{... | collective-permute-start | bytes 3538952 | tf_op jit(solution)/shard_map/ppermute | solution.py:273
  188.6 26.9 %collective-permute-start.20 = (bf16[160,3072]{1,0:T(8,128)(2,1)}, bf16[160,3072]{1,0:T(8,128)(2,1)}, u32[]{:S(2)}, u32[]{:S(2)}) collective-permute-start(bf16[160,3072]{1,0:T(8,128)(2,1)} %get-tuple-element.84), channel_id=1, source_target_pairs={{0,1},{1,0},{2,3},{3,2},{4,5},{5,4},{6,7},{7,6},{8,9},{9,8},{10,11... | collective-permute-start | bytes 2949128 | tf_op jit(solution)/shard_map/ppermute | solution.py:273
  189.2 26.3 %collective-permute-start.21 = (bf16[160,3072]{1,0:T(8,128)(2,1)}, bf16[160,3072]{1,0:T(8,128)(2,1)}, u32[]{:S(2)}, u32[]{:S(2)}) collective-permute-start(bf16[160,3072]{1,0:T(8,128)(2,1)} %get-tuple-element.85), channel_id=1, source_target_pairs={{0,2},{1,3},{2,0},{3,1},{4,6},{5,7},{6,4},{7,5},{8,10},{9,11},{10,... | collective-permute-start | bytes 2949128 | tf_op jit(solution)/shard_map/ppermute | solution.py:273
  219.3 7.7 %collective-permute-start.29 = (bf16[384,3072]{1,0:T(8,128)(2,1)}, bf16[384,3072]{1,0:T(8,128)(2,1)}, u32[]{:S(2)}, u32[]{:S(2)}) collective-permute-start(bf16[384,3072]{1,0:T(8,128)(2,1)} %maximum_select_fusion.refs_1_), channel_id=1, source_target_pairs={{0,4},{4,0},{8,12},{12,8},{16,20},{20,16},{24,28},{28,24},{1,5},{5... | collective-permute-start | bytes 7077896 | tf_op jit(solution)/shard_map/ppermute | solution.py:273
  219.4 6.1 %collective-permute-start.27 = (bf16[160,3072]{1,0:T(8,128)(2,1)}, bf16[160,3072]{1,0:T(8,128)(2,1)}, u32[]{:S(2)}, u32[]{:S(2)}) collective-permute-start(bf16[160,3072]{1,0:T(8,128)(2,1)} %collective-permute-done.20.refs_4_.refs_7_), channel_id=1, source_target_pairs={{0,4},{4,0},{8,12},{12,8},{16,20},{20,16},{24,28},{28,24},{1,5},{5... | collective-permute-start | bytes 2949128 | tf_op jit(solution)/shard_map/ppermute | solution.py:273
  219.8 7.2 %collective-permute-start.28 = (bf16[160,3072]{1,0:T(8,128)(2,1)}, bf16[160,3072]{1,0:T(8,128)(2,1)}, u32[]{:S(2)}, u32[]{:S(2)}) collective-permute-start(bf16[160,3072]{1,0:T(8,128)(2,1)} %collective-permute-done.21.refs_5_.refs_8_), channel_id=1, source_target_pairs={{0,4},{4,0},{8,12},{12,8},{16,20},{20,16},{24,28},{28,24},{1,5},{5... | collective-permute-start | bytes 2949128 | tf_op jit(solution)/shard_map/ppermute | solution.py:273
  220.0 53.8 %collective-permute-start.25 = (bf16[384,3072]{1,0:T(8,128)(2,1)}, bf16[384,3072]{1,0:T(8,128)(2,1)}, u32[]{:S(2)}, u32[]{:S(2)}) collective-permute-start(bf16[384,3072]{1,0:T(8,128)(2,1)} %maximum_select_fusion.refs_1_), channel_id=1, source_target_pairs={{0,1},{1,0},{2,3},{3,2},{4,5},{5,4},{6,7},{7,6},{8,9},{9,8},{10,11... | collective-permute-start | bytes 7077896 | tf_op jit(solution)/shard_map/ppermute | solution.py:273
  220.5 53.7 %collective-permute-start.26 = (bf16[384,3072]{1,0:T(8,128)(2,1)}, bf16[384,3072]{1,0:T(8,128)(2,1)}, u32[]{:S(2)}, u32[]{:S(2)}) collective-permute-start(bf16[384,3072]{1,0:T(8,128)(2,1)} %maximum_select_fusion.refs_1_), channel_id=1, source_target_pairs={{0,2},{1,3},{2,0},{3,1},{4,6},{5,7},{6,4},{7,5},{8,10},{9,11},{10,... | collective-permute-start | bytes 7077896 | tf_op jit(solution)/shard_map/ppermute | solution.py:273
  240.1 38.0 %collective-permute-start.30 = (bf16[256,3072]{1,0:T(8,128)(2,1)}, bf16[256,3072]{1,0:T(8,128)(2,1)}, u32[]{:S(2)}, u32[]{:S(2)}) collective-permute-start(bf16[256,3072]{1,0:T(8,128)(2,1)} %get-tuple-element.99), channel_id=1, source_target_pairs={{0,8},{4,12},{8,0},{12,4},{16,24},{20,28},{24,16},{28,20},{1,9},{5... | collective-permute-start | bytes 4718600 | tf_op jit(solution)/shard_map/ppermute | solution.py:273
  278.1 6.9 %collective-permute-start.33 = (bf16[384,3072]{1,0:T(8,128)(2,1)}, bf16[384,3072]{1,0:T(8,128)(2,1)}, u32[]{:S(2)}, u32[]{:S(2)}) collective-permute-start(bf16[384,3072]{1,0:T(8,128)(2,1)} %collective-permute-done.25.x_ref.refs_3_), channel_id=1, source_target_pairs={{0,4},{4,0},{8,12},{12,8},{16,20},{20,16},{24,28},{28,24},{1,5},{5... | collective-permute-start | bytes 7077896 | tf_op jit(solution)/shard_map/ppermute | solution.py:273
  278.1 8.2 %collective-permute-start.34 = (bf16[384,3072]{1,0:T(8,128)(2,1)}, bf16[384,3072]{1,0:T(8,128)(2,1)}, u32[]{:S(2)}, u32[]{:S(2)}) collective-permute-start(bf16[384,3072]{1,0:T(8,128)(2,1)} %collective-permute-done.26.y_ref.refs_4_), channel_id=1, source_target_pairs={{0,4},{4,0},{8,12},{12,8},{16,20},{20,16},{24,28},{28,24},{1,5},{5... | collective-permute-start | bytes 7077896 | tf_op jit(solution)/shard_map/ppermute | solution.py:273
  281.1 30.5 %collective-permute-start.31 = (bf16[192,3072]{1,0:T(8,128)(2,1)}, bf16[192,3072]{1,0:T(8,128)(2,1)}, u32[]{:S(2)}, u32[]{:S(2)}) collective-permute-start(bf16[192,3072]{1,0:T(8,128)(2,1)} %get-tuple-element.104), channel_id=1, source_target_pairs={{0,1},{1,0},{2,3},{3,2},{4,5},{5,4},{6,7},{7,6},{8,9},{9,8},{10,11... | collective-permute-start | bytes 3538952 | tf_op jit(solution)/shard_map/ppermute | solution.py:273
  282.7 28.9 %collective-permute-start.32 = (bf16[192,3072]{1,0:T(8,128)(2,1)}, bf16[192,3072]{1,0:T(8,128)(2,1)}, u32[]{:S(2)}, u32[]{:S(2)}) collective-permute-start(bf16[192,3072]{1,0:T(8,128)(2,1)} %get-tuple-element.105), channel_id=1, source_target_pairs={{0,2},{1,3},{2,0},{3,1},{4,6},{5,7},{6,4},{7,5},{8,10},{9,11},{10,... | collective-permute-start | bytes 3538952 | tf_op jit(solution)/shard_map/ppermute | solution.py:273
  283.2 36.1 %collective-permute-start.37 = (bf16[256,3072]{1,0:T(8,128)(2,1)}, bf16[256,3072]{1,0:T(8,128)(2,1)}, u32[]{:S(2)}, u32[]{:S(2)}) collective-permute-start(bf16[256,3072]{1,0:T(8,128)(2,1)} %get-tuple-element.112), channel_id=1, source_target_pairs={{0,8},{4,12},{8,0},{12,4},{16,24},{20,28},{24,16},{28,20},{1,9},{5... | collective-permute-start | bytes 4718600 | tf_op jit(solution)/shard_map/ppermute | solution.py:273
  311.6 7.7 %collective-permute-start.35 = (bf16[192,3072]{1,0:T(8,128)(2,1)}, bf16[192,3072]{1,0:T(8,128)(2,1)}, u32[]{:S(2)}, u32[]{:S(2)}) collective-permute-start(bf16[192,3072]{1,0:T(8,128)(2,1)} %collective-permute-done.31.refs_1_), channel_id=1, source_target_pairs={{0,4},{4,0},{8,12},{12,8},{16,20},{20,16},{24,28},{28,24},{1,5},{5... | collective-permute-start | bytes 3538952 | tf_op jit(solution)/shard_map/ppermute | solution.py:273
  311.8 7.5 %collective-permute-start.36 = (bf16[192,3072]{1,0:T(8,128)(2,1)}, bf16[192,3072]{1,0:T(8,128)(2,1)}, u32[]{:S(2)}, u32[]{:S(2)}) collective-permute-start(bf16[192,3072]{1,0:T(8,128)(2,1)} %collective-permute-done.32.refs_2_), channel_id=1, source_target_pairs={{0,4},{4,0},{8,12},{12,8},{16,20},{20,16},{24,28},{28,24},{1,5},{5... | collective-permute-start | bytes 3538952 | tf_op jit(solution)/shard_map/ppermute | solution.py:273

commit v4 on v3

--- a/solution.py
+++ b/solution.py
@@ -60,8 +60,8 @@
     blocks = [slice(f * feat, (f + 1) * feat) for f in range(3)]
     i_refs, j_refs = take(len(i_rows)), take(len(spans))
     y_refs = take(n_sums) if has_y else []
-    back_refs = take(n_i) if final else []
-    out_refs = take(n_i if narrow else 3 if final else n_sums)
+    back_ref = take(1)[0] if final else None
+    out_refs = take(3 if final else n_sums)
     ibuf, jbuf, acc, i_sem, j_sem, y_sem, o_sem = take(7)
     packed, b_sem = take(2) if narrow or final else (None, None)
 
@@ -84,8 +84,8 @@
             pltpu.make_async_copy(y_refs[i // per].at[block(i % per)], acc.at[block(i)], y_sem.at[i]).start()
     for t in range(1, tiles):
         fill(jbuf, j_sem, j_refs, spans, t, tile)
-    for i, ref in enumerate(back_refs):
-        pltpu.make_async_copy(ref, packed.at[block(i)], b_sem.at[i]).start()
+    for i in range(n_i if final else 0):
+        pltpu.make_async_copy(back_ref.at[block(i)], packed.at[block(i)], b_sem.at[i]).start()
 
     def wait(ref, sem):
         pltpu.make_async_copy(ref, ref, sem).wait()
@@ -129,10 +129,8 @@
                     def _():
                         if narrow:
                             packed[block(n), :] = acc[block(n), :].astype(jnp.bfloat16)
-                            src, dst = packed.at[block(n)], out_refs[n]
-                        else:
-                            src, dst = acc.at[block(n)], out_refs[n // per].at[block(n % per)]
-                        pltpu.make_async_copy(src, dst, o_sem.at[n]).start()
+                        src = (packed if narrow else acc).at[block(n)]
+                        pltpu.make_async_copy(src, out_refs[n // per].at[block(n % per)], o_sem.at[n]).start()
             return inner
 
         return lax.fori_loop(0, n_i, over_rows, carry)
@@ -155,14 +153,12 @@
     has_y, final = sums is not None, back is not None
     n_sums = len(sums) if has_y else 1
     any_spec = pl.BlockSpec(memory_space=pltpu.HBM)
-    operands = [*lefts, *(r for r, _, _ in rights), *(sums or []), *(back or [])]
+    operands = [*lefts, *(r for r, _, _ in rights), *(sums or []), *([back] if final else [])]
     first_y = len(lefts) + len(rights)
-    if narrow:
-        outs = [jax.ShapeDtypeStruct((ROW_TILE, width), jnp.bfloat16)] * n_i
-    elif final:
+    if final:
         outs = [jax.ShapeDtypeStruct((rows, feat), jnp.float32)] * 3
     else:
-        outs = [jax.ShapeDtypeStruct((rows // n_sums, width), jnp.float32)] * n_sums
+        outs = [jax.ShapeDtypeStruct((rows // n_sums, width), jnp.bfloat16 if narrow else jnp.float32)] * n_sums
     scratch = [
         pltpu.VMEM((rows, width), jnp.bfloat16),
         pltpu.VMEM((total, width), jnp.bfloat16),
@@ -318,18 +314,18 @@
     c_x, c_y = along_x(c), along_y(c)
     e_ds0, e_ds1, c_s = fence((core(e_d0), core(e_d1), core(c)))
     e_d = [e_d0, e_d1, e_ds0, e_ds1]
-    visit_0, visit_1 = pair_sums(guest, [(e_xs, lead, early - lead), e_ys, *e_d], [visit], 1024, narrow=True)
-    visit_0, visit_1, home = fence((visit_0, visit_1, home))
-    back_0 = partner(visit_0)
+    (visit,) = pair_sums(guest, [(e_xs, lead, early - lead), e_ys, *e_d], [visit], 1024, narrow=True)
+    visit, home = fence((visit, home))
+    back = partner(visit)
     (home,) = pair_sums([x], [e, e_s, e_x, e_y, e_xs, e_ys, *e_d], [home], 1280)
-    c_x, c_y, back_0, visit_1, home = fence((c_x, c_y, back_0, visit_1, home))
-
-    back_1 = partner(visit_1)
+    (home,) = pair_sums([x], [c, c_s], [home], 768)
+    c_x, c_y, home = fence((c_x, c_y, home))
+
     c_d0, c_d1 = corner(c_x, c_y)
-    (home,) = pair_sums([x], [c, c_s, c_x, c_y, core(c_x), core(c_y)], [home], 768)
-    c_d0, c_d1, home = fence((c_d0, c_d1, home))
+    (home,) = pair_sums([x], [c_x, c_y, core(c_x), core(c_y)], [home], 768)
+    c_d0, c_d1, back, home = fence((c_d0, c_d1, back, home))
     c_d = [c_d0, c_d1, core(c_d0), core(c_d1)]
-    return tuple(pair_sums([x], c_d, [home], 768, back=[back_0, back_1]))
+    return tuple(pair_sums([x], c_d, [home], 768, back=back))
 
 
 def gram_rows(left, right):

time: 333 us -> 331 us (level)
  waiting for transfers between devices: 75.2 us -> 71 us
  Pallas kernels: 207 us -> 211 us
    pallas_call x8 -> x9, Pallas kernels: 171 us -> 175 us  [pair_sums(): pl.pallas_call(functools.partial(pair_kernel, feat, i_rows, spans, tile,...]
    ppermute x38 -> x37, waiting for transfers between devices: 75.2 us -> 71 us  [move(): return lambda v: lax.ppermute(v, axis, pairs)]
    ppermute x38 -> x37, starting transfers between devices: 42.7 us -> 40.9 us  [move(): return lambda v: lax.ppermute(v, axis, pairs)]
  transfers between devices with their start and end apart: 38 -> 37, of which waited for: 16 -> 16; matrix products, arithmetic and copies ran while one was open for 1% -> 1% of each run, Pallas kernels for 57% -> 59%
where the time goes in v4:
time: 331 us
  Pallas kernels  211 us (64%)
  waiting for transfers between devices  71 us (21%)
  starting transfers between devices  40.9 us (12%)
  other arithmetic  6.73 us (2%)
    pallas_call x9, Pallas kernels, pair_sums(): pl.pallas_call(functools.partial(pair_kernel, feat, i_rows, spans, tile,...  175 us
    ppermute x37, waiting for transfers between devices, move(): return lambda v: lax.ppermute(v, axis, pairs)  71 us
    ppermute x37, starting transfers between devices, move(): return lambda v: lax.ppermute(v, axis, pairs)  40.9 us
    pallas_call x1, Pallas kernels, trace_terms(): pl.pallas_call(functools.partial(trace_kernel, feat), grid=(rows // LANES...  23.9 us
    pallas_call x3, Pallas kernels, cut(): pl.pallas_call(functools.partial(cut_kernel, mid, parts), in_specs=[spec]...  7.75 us
  transfers between devices with their start and end apart: 37, of which 16 were waited for; matrix products, arithmetic and copies ran while one was open for 1% of the time, Pallas kernels for 59%

profile of v4, /device:TPU:0, one launch (start us, length us, event | category | flops | bytes accessed | tf_op | source)
XLA Modules:
  0.0 330.6 jit_solution(8045192836434056809)
XLA Ops:
  0.6 4.0 %shard_map.58 = (bf16[512,3072]{1,0:T(8,128)(2,1)}, bf16[320,3072]{1,0:T(8,128)(2,1)}, bf16[192,3072]{1,0:T(8,128)(2,1)}) custom-call(bf16[512,1024]{1,0:T(8,128)(2,1)} %a_ref.1, bf16[512,1024]{1,0:T(8,128)(2,1)} %b_ref.1, bf16[512,1024]{1,0:T(8,128)(2,1)} %c_ref.1), custom_call_target="tpu_custom_call" | custom-call | flops 512 | bytes 1024 | tf_op jit(solution)/shard_map/pallas_call | solution.py:250
  5.1 2.7 collective-permute-start.2
  7.8 1.9 collective-permute-start.3
  9.7 1.5 collective-permute-start
  11.2 1.5 collective-permute-start.1
  12.7 23.9 %shard_map.59.refs_3_ = f32[512,3072]{1,0:T(8,128)} custom-call(bf16[512,3072]{1,0:T(8,128)(2,1)} %get-tuple-element.54.x_ref.refs_0_.refs_1_.refs_2_), custom_call_target="tpu_custom_call" | custom-call | flops 512 | bytes 3072 | tf_op jit(solution)/shard_map/pallas_call | solution.py:42
  36.6 13.2 %shard_map.60.refs_9_ = f32[512,3072]{1,0:T(8,128)} custom-call(bf16[512,3072]{1,0:T(8,128)(2,1)} %get-tuple-element.54.x_ref.refs_0_.refs_1_.refs_2_, bf16[512,3072]{1,0:T(8,128)(2,1)} %get-tuple-element.54.x_ref.refs_0_.refs_1_.refs_2_, bf16[512,3072]{1,0:T(8,128)(2,1)} %collective-permute-done.4.refs_2_.refs_3_, ...), custom_call_target="tpu_custom_call", output_to_operand_aliasing={{}: (3, {})} | custom-call | flops 512 | bytes 3072 | tf_op jit(solution)/shard_map/pallas_call | solution.py:173
  49.9 1.7 collective-permute-done.2.refs_0_
  51.5 4.8 %collective-permute-start.5 = (bf16[192,3072]{1,0:T(8,128)(2,1)}, bf16[192,3072]{1,0:T(8,128)(2,1)}, u32[]{:S(2)}, u32[]{:S(2)}) collective-permute-start(bf16[192,3072]{1,0:T(8,128)(2,1)} %get-tuple-element.57), channel_id=1, source_target_pairs={{0,8},{4,12},{8,0},{12,4},{16,24},{20,28},{24,16},{28,20},{1,9},{5... | collective-permute-start | bytes 3538952 | tf_op jit(solution)/shard_map/ppermute | solution.py:269
  56.3 1.8 collective-permute-start.6
  58.0 22.1 %collective-permute-done.x_ref.refs_4_.refs_1_ = bf16[512,3072]{1,0:T(8,128)(2,1)} collective-permute-done((bf16[512,3072]{1,0:T(8,128)(2,1)}, bf16[512,3072]{1,0:T(8,128)(2,1)}, u32[]{:S(2)}, u32[]{:S(2)}) %collective-permute-start) | collective-permute-done | bytes 3145760 | tf_op jit(solution)/shard_map/ppermute | solution.py:269
  80.2 1.2 collective-permute-done.1.y_ref.refs_5_.refs_2_
  82.9 1.9 collective-permute-start.10
  84.9 1.3 collective-permute-start.9
  86.1 2.9 shard_map.61
  89.0 1.6 collective-permute-start.7
  90.6 1.5 collective-permute-start.8
  92.9 28.1 %shard_map.62.refs_11_ = f32[512,3072]{1,0:T(8,128)} custom-call(bf16[320,3072]{1,0:T(8,128)(2,1)} %collective-permute-done.2.refs_0_, bf16[192,3072]{1,0:T(8,128)(2,1)} %collective-permute-done.5.refs_1_, bf16[512,3072]{1,0:T(8,128)(2,1)} %get-tuple-element.54.x_ref.refs_0_.refs_1_.refs_2_, bf16[512,3072]{1,0:T(8,128)(2,1)} %collective-permute-done.4.refs_2_.refs_3_, ...), custom_call_target="tpu_custom_call" | custom-call | flops 512 | bytes 3072 | tf_op jit(solution)/shard_map/pallas_call | solution.py:173
  121.1 13.1 %collective-permute-done.9 = bf16[320,3072]{1,0:T(8,128)(2,1)} collective-permute-done((bf16[320,3072]{1,0:T(8,128)(2,1)}, bf16[320,3072]{1,0:T(8,128)(2,1)}, u32[]{:S(2)}, u32[]{:S(2)}) %collective-permute-start.9) | collective-permute-done | bytes 1966112 | tf_op jit(solution)/shard_map/ppermute | solution.py:269
  134.7 3.0 broadcast_select_fusion.refs_6_.refs_1_
  137.8 1.5 collective-permute-start.13
  139.3 1.5 collective-permute-start.14
  140.8 1.7 collective-permute-start.16
  142.5 1.5 collective-permute-start.15
  144.0 29.6 %shard_map.63.refs_11_ = f32[512,3072]{1,0:T(8,128)} custom-call(bf16[512,3072]{1,0:T(8,128)(2,1)} %get-tuple-element.54.x_ref.refs_0_.refs_1_.refs_2_, bf16[512,3072]{1,0:T(8,128)(2,1)} %collective-permute-done.x_ref.refs_4_.refs_1_, bf16[512,3072]{1,0:T(8,128)(2,1)} %collective-permute-done.1.y_ref.refs_5_.refs_2_, ...), custom_call_target="tpu_custom_call", output_to_operand_aliasing={{}: (9, {})} | custom-call | flops 512 | bytes 3072 | tf_op jit(solution)/shard_map/pallas_call | solution.py:173
  173.6 9.7 %collective-permute-done.13.x_ref.refs_8_.refs_3_ = bf16[320,3072]{1,0:T(8,128)(2,1)} collective-permute-done((bf16[320,3072]{1,0:T(8,128)(2,1)}, bf16[320,3072]{1,0:T(8,128)(2,1)}, u32[]{:S(2)}, u32[]{:S(2)}) %collective-permute-start.13) | collective-permute-done | bytes 1966112 | tf_op jit(solution)/shard_map/ppermute | solution.py:269
  183.3 1.2 collective-permute-done.14.y_ref.refs_9_.refs_4_
  185.0 1.3 collective-permute-start.22
  186.3 2.4 shard_map.64
  189.2 1.5 collective-permute-start.21
  191.6 24.0 %shard_map.65.refs_8_ = f32[512,3072]{1,0:T(8,128)} custom-call(bf16[320,3072]{1,0:T(8,128)(2,1)} %collective-permute-done.2.refs_0_, bf16[192,3072]{1,0:T(8,128)(2,1)} %collective-permute-done.5.refs_1_, bf16[256,3072]{1,0:T(8,128)(2,1)} %collective-permute-done.7.refs_5_.refs_2_, ...), custom_call_target="tpu_custom_call", output_to_operand_aliasing={{}: (11, {})} | custom-call | flops 512 | bytes 3072 | tf_op jit(solution)/shard_map/pallas_call | solution.py:173
  215.6 3.7 %maximum_select_fusion.refs_1_ = bf16[384,3072]{1,0:T(8,128)(2,1)} fusion(bf16[192,3072]{1,0:T(8,128)(2,1)} %collective-permute-done.16, bf16[192,3072]{1,0:T(8,128)(2,1)} %collective-permute-done.6, bf16[192,3072]{1,0:T(8,128)(2,1)} %collective-permute-done.22, bf16[192,3072]{1,0:T(8,128)(2,1)} %collective-permute-done.15, pred[]{:T(512)S(6)} %and.4), kind=kLoop, calls=%fused_computation | loop fusion | flops 10616832 | bytes 7077889 | tf_op jit(solution)/shard_map/jit(_where)/select_n | solution.py:313
  220.0 1.5 collective-permute-start.26
  222.0 3.5 %collective-permute-done.27.refs_6_.refs_9_ = bf16[160,3072]{1,0:T(8,128)(2,1)} collective-permute-done((bf16[160,3072]{1,0:T(8,128)(2,1)}, bf16[160,3072]{1,0:T(8,128)(2,1)}, u32[]{:S(2)}, u32[]{:S(2)}) %collective-permute-start.27) | collective-permute-done | bytes 983072 | tf_op jit(solution)/shard_map/ppermute | solution.py:269
  225.6 1.4 collective-permute-done.28.refs_7_.refs_10_
  227.0 13.1 %shard_map.66 = bf16[512,3072]{1,0:T(8,128)(2,1)} custom-call(bf16[320,3072]{1,0:T(8,128)(2,1)} %collective-permute-done.2.refs_0_, bf16[192,3072]{1,0:T(8,128)(2,1)} %collective-permute-done.5.refs_1_, bf16[320,3072]{1,0:T(8,128)(2,1)} %collective-permute-done.23.refs_10_.refs_2_.refs_5_, bf16[320,3072]{1,0:T(8,128)(2,1)} %collective-permute-done.24.refs_3_.refs_6_, ...), custom_call_target="tpu_custom_call" | custom-call | flops 512 | bytes 3072 | tf_op jit(solution)/shard_map/pallas_call | solution.py:173
  240.1 2.9 collective-permute-start.32
  243.0 25.0 %shard_map.67.refs_3_ = f32[512,3072]{1,0:T(8,128)} custom-call(bf16[512,3072]{1,0:T(8,128)(2,1)} %get-tuple-element.54.x_ref.refs_0_.refs_1_.refs_2_, bf16[320,3072]{1,0:T(8,128)(2,1)} %broadcast_select_fusion.refs_6_.refs_1_, bf16[320,3072]{1,0:T(8,128)(2,1)} %collective-permute-done.19.refs_7_.refs_2_, ...), custom_call_target="tpu_custom_call", output_to_operand_aliasing={{}: (11, {})} | custom-call | flops 512 | bytes 3072 | tf_op jit(solution)/shard_map/pallas_call | solution.py:173
  267.9 11.9 %shard_map.68.refs_5_ = f32[512,3072]{1,0:T(8,128)} custom-call(bf16[512,3072]{1,0:T(8,128)(2,1)} %get-tuple-element.54.x_ref.refs_0_.refs_1_.refs_2_, bf16[384,3072]{1,0:T(8,128)(2,1)} %maximum_select_fusion.refs_1_, bf16[384,3072]{1,0:T(8,128)(2,1)} %collective-permute-done.29.refs_2_, f32[512,3072]{1,0:T(8,128)} %shard_map.67.refs_3_), custom_call_target="tpu_custom_call", output_to_operand_aliasing={{}: (3, {})} | custom-call | flops 512 | bytes 3072 | tf_op jit(solution)/shard_map/pallas_call | solution.py:173
  280.5 2.5 shard_map.69
  283.0 1.6 collective-permute-start.30
  285.1 3.1 collective-permute-done.34.refs_4_
  288.2 17.5 %shard_map.70.refs_5_ = f32[512,3072]{1,0:T(8,128)} custom-call(bf16[512,3072]{1,0:T(8,128)(2,1)} %get-tuple-element.54.x_ref.refs_0_.refs_1_.refs_2_, bf16[384,3072]{1,0:T(8,128)(2,1)} %collective-permute-done.25.x_ref.refs_1_, bf16[384,3072]{1,0:T(8,128)(2,1)} %collective-permute-done.26.y_ref.refs_2_, ...), custom_call_target="tpu_custom_call", output_to_operand_aliasing={{}: (5, {})} | custom-call | flops 512 | bytes 3072 | tf_op jit(solution)/shard_map/pallas_call | solution.py:173
  305.7 5.7 %collective-permute-done.30.refs_1_ = bf16[192,3072]{1,0:T(8,128)(2,1)} collective-permute-done((bf16[192,3072]{1,0:T(8,128)(2,1)}, bf16[192,3072]{1,0:T(8,128)(2,1)}, u32[]{:S(2)}, u32[]{:S(2)}) %collective-permute-start.30) | collective-permute-done | bytes 1179680 | tf_op jit(solution)/shard_map/ppermute | solution.py:269
  311.4 1.2 collective-permute-done.31.refs_2_
  313.1 2.7 collective-permute-done.35.refs_3_
  315.8 1.7 collective-permute-done.36.refs_4_
  317.5 12.9 %shard_map.71 = (f32[512,1024]{1,0:T(8,128)}, f32[512,1024]{1,0:T(8,128)}, f32[512,1024]{1,0:T(8,128)}) custom-call(bf16[512,3072]{1,0:T(8,128)(2,1)} %get-tuple-element.54.x_ref.refs_0_.refs_1_.refs_2_, bf16[192,3072]{1,0:T(8,128)(2,1)} %collective-permute-done.30.refs_1_, bf16[192,3072]{1,0:T(8,128)(2,1)} %collective-permute-done.31.refs_2_, ...), custom_call_target="tpu_custom_call" | custom-call | flops 512 | bytes 3072 | tf_op jit(solution)/shard_map/pallas_call | solution.py:173
  (42 shorter events, 8.2 us)
Async XLA Ops:
  4.6 32.0 %collective-permute-start.4 = (bf16[512,3072]{1,0:T(8,128)(2,1)}, bf16[512,3072]{1,0:T(8,128)(2,1)}, u32[]{:S(2)}, u32[]{:S(2)}) collective-permute-start(bf16[512,3072]{1,0:T(8,128)(2,1)} %get-tuple-element.54.x_ref.refs_0_.refs_1_.refs_2_), channel_id=1, source_target_pairs={{0,4},{4,0},{8,12},{12,8},{16,20},{20,16},{24,28},{28,24},{1,5},{5... | collective-permute-start | bytes 9437192 | tf_op jit(solution)/shard_map/ppermute | solution.py:269
  5.1 46.4 %collective-permute-start.2 = (bf16[320,3072]{1,0:T(8,128)(2,1)}, bf16[320,3072]{1,0:T(8,128)(2,1)}, u32[]{:S(2)}, u32[]{:S(2)}) collective-permute-start(bf16[320,3072]{1,0:T(8,128)(2,1)} %get-tuple-element.55), channel_id=1, source_target_pairs={{0,8},{4,12},{8,0},{12,4},{16,24},{20,28},{24,16},{28,20},{1,9},{5... | collective-permute-start | bytes 5898248 | tf_op jit(solution)/shard_map/ppermute | solution.py:269
  7.8 43.7 %collective-permute-start.3 = (bf16[320,3072]{1,0:T(8,128)(2,1)}, bf16[320,3072]{1,0:T(8,128)(2,1)}, u32[]{:S(2)}, u32[]{:S(2)}) collective-permute-start(bf16[320,3072]{1,0:T(8,128)(2,1)} %get-tuple-element.55), channel_id=1, source_target_pairs={{8,16},{12,20},{16,8},{20,12},{9,17},{13,21},{17,9},{21,13},{10,18... | collective-permute-start | bytes 5898248 | tf_op jit(solution)/shard_map/ppermute | solution.py:269
  9.7 70.5 %collective-permute-start = (bf16[512,3072]{1,0:T(8,128)(2,1)}, bf16[512,3072]{1,0:T(8,128)(2,1)}, u32[]{:S(2)}, u32[]{:S(2)}) collective-permute-start(bf16[512,3072]{1,0:T(8,128)(2,1)} %get-tuple-element.54.x_ref.refs_0_.refs_1_.refs_2_), channel_id=1, source_target_pairs={{0,1},{1,0},{2,3},{3,2},{4,5},{5,4},{6,7},{7,6},{8,9},{9,8},{10,11... | collective-permute-start | bytes 9437192 | tf_op jit(solution)/shard_map/ppermute | solution.py:269
  11.2 70.2 %collective-permute-start.1 = (bf16[512,3072]{1,0:T(8,128)(2,1)}, bf16[512,3072]{1,0:T(8,128)(2,1)}, u32[]{:S(2)}, u32[]{:S(2)}) collective-permute-start(bf16[512,3072]{1,0:T(8,128)(2,1)} %get-tuple-element.54.x_ref.refs_0_.refs_1_.refs_2_), channel_id=1, source_target_pairs={{0,2},{1,3},{2,0},{3,1},{4,6},{5,7},{6,4},{7,5},{8,10},{9,11},{10,... | collective-permute-start | bytes 9437192 | tf_op jit(solution)/shard_map/ppermute | solution.py:269
  51.5 30.9 %collective-permute-start.5 = (bf16[192,3072]{1,0:T(8,128)(2,1)}, bf16[192,3072]{1,0:T(8,128)(2,1)}, u32[]{:S(2)}, u32[]{:S(2)}) collective-permute-start(bf16[192,3072]{1,0:T(8,128)(2,1)} %get-tuple-element.57), channel_id=1, source_target_pairs={{0,8},{4,12},{8,0},{12,4},{16,24},{20,28},{24,16},{28,20},{1,9},{5... | collective-permute-start | bytes 3538952 | tf_op jit(solution)/shard_map/ppermute | solution.py:269
  56.3 26.1 %collective-permute-start.6 = (bf16[192,3072]{1,0:T(8,128)(2,1)}, bf16[192,3072]{1,0:T(8,128)(2,1)}, u32[]{:S(2)}, u32[]{:S(2)}) collective-permute-start(bf16[192,3072]{1,0:T(8,128)(2,1)} %get-tuple-element.57), channel_id=1, source_target_pairs={{8,16},{12,20},{16,8},{20,12},{9,17},{13,21},{17,9},{21,13},{10,18... | collective-permute-start | bytes 3538952 | tf_op jit(solution)/shard_map/ppermute | solution.py:269
  82.4 8.2 %collective-permute-start.11 = (bf16[512,3072]{1,0:T(8,128)(2,1)}, bf16[512,3072]{1,0:T(8,128)(2,1)}, u32[]{:S(2)}, u32[]{:S(2)}) collective-permute-start(bf16[512,3072]{1,0:T(8,128)(2,1)} %collective-permute-done.x_ref.refs_4_.refs_1_), channel_id=1, source_target_pairs={{0,4},{4,0},{8,12},{12,8},{16,20},{20,16},{24,28},{28,24},{1,5},{5... | collective-permute-start | bytes 9437192 | tf_op jit(solution)/shard_map/ppermute | solution.py:269
  82.4 10.5 %collective-permute-start.12 = (bf16[512,3072]{1,0:T(8,128)(2,1)}, bf16[512,3072]{1,0:T(8,128)(2,1)}, u32[]{:S(2)}, u32[]{:S(2)}) collective-permute-start(bf16[512,3072]{1,0:T(8,128)(2,1)} %collective-permute-done.1.y_ref.refs_5_.refs_2_), channel_id=1, source_target_pairs={{0,4},{4,0},{8,12},{12,8},{16,20},{20,16},{24,28},{28,24},{1,5},{5... | collective-permute-start | bytes 9437192 | tf_op jit(solution)/shard_map/ppermute | solution.py:269
  82.9 38.1 %collective-permute-start.10 = (bf16[320,3072]{1,0:T(8,128)(2,1)}, bf16[320,3072]{1,0:T(8,128)(2,1)}, u32[]{:S(2)}, u32[]{:S(2)}) collective-permute-start(bf16[320,3072]{1,0:T(8,128)(2,1)} %collective-permute-done.2.refs_0_), channel_id=1, source_target_pairs={{8,16},{12,20},{16,8},{20,12},{9,17},{13,21},{17,9},{21,13},{10,18... | collective-permute-start | bytes 5898248 | tf_op jit(solution)/shard_map/ppermute | solution.py:269
  84.9 49.3 %collective-permute-start.9 = (bf16[320,3072]{1,0:T(8,128)(2,1)}, bf16[320,3072]{1,0:T(8,128)(2,1)}, u32[]{:S(2)}, u32[]{:S(2)}) collective-permute-start(bf16[320,3072]{1,0:T(8,128)(2,1)} %collective-permute-done.3), channel_id=1, source_target_pairs={{8,0},{12,4},{16,24},{20,28},{9,1},{13,5},{17,25},{21,29},{10,2},{... | collective-permute-start | bytes 5898248 | tf_op jit(solution)/shard_map/ppermute | solution.py:269
  89.0 45.1 %collective-permute-start.7 = (bf16[256,3072]{1,0:T(8,128)(2,1)}, bf16[256,3072]{1,0:T(8,128)(2,1)}, u32[]{:S(2)}, u32[]{:S(2)}) collective-permute-start(bf16[256,3072]{1,0:T(8,128)(2,1)} %get-tuple-element.62), channel_id=1, source_target_pairs={{0,1},{1,0},{2,3},{3,2},{4,5},{5,4},{6,7},{7,6},{8,9},{9,8},{10,11... | collective-permute-start | bytes 4718600 | tf_op jit(solution)/shard_map/ppermute | solution.py:269
  90.6 43.6 %collective-permute-start.8 = (bf16[256,3072]{1,0:T(8,128)(2,1)}, bf16[256,3072]{1,0:T(8,128)(2,1)}, u32[]{:S(2)}, u32[]{:S(2)}) collective-permute-start(bf16[256,3072]{1,0:T(8,128)(2,1)} %get-tuple-element.63), channel_id=1, source_target_pairs={{0,2},{1,3},{2,0},{3,1},{4,6},{5,7},{6,4},{7,5},{8,10},{9,11},{10,... | collective-permute-start | bytes 4718600 | tf_op jit(solution)/shard_map/ppermute | solution.py:269
  134.2 6.6 %collective-permute-start.17 = (bf16[256,3072]{1,0:T(8,128)(2,1)}, bf16[256,3072]{1,0:T(8,128)(2,1)}, u32[]{:S(2)}, u32[]{:S(2)}) collective-permute-start(bf16[256,3072]{1,0:T(8,128)(2,1)} %collective-permute-done.7.refs_5_.refs_2_), channel_id=1, source_target_pairs={{0,4},{4,0},{8,12},{12,8},{16,20},{20,16},{24,28},{28,24},{1,5},{5... | collective-permute-start | bytes 4718600 | tf_op jit(solution)/shard_map/ppermute | solution.py:269
  134.2 8.3 %collective-permute-start.18 = (bf16[256,3072]{1,0:T(8,128)(2,1)}, bf16[256,3072]{1,0:T(8,128)(2,1)}, u32[]{:S(2)}, u32[]{:S(2)}) collective-permute-start(bf16[256,3072]{1,0:T(8,128)(2,1)} %collective-permute-done.8.refs_6_.refs_3_), channel_id=1, source_target_pairs={{0,4},{4,0},{8,12},{12,8},{16,20},{20,16},{24,28},{28,24},{1,5},{5... | collective-permute-start | bytes 4718600 | tf_op jit(solution)/shard_map/ppermute | solution.py:269
  137.7 6.3 %collective-permute-start.19 = (bf16[320,3072]{1,0:T(8,128)(2,1)}, bf16[320,3072]{1,0:T(8,128)(2,1)}, u32[]{:S(2)}, u32[]{:S(2)}) collective-permute-start(bf16[320,3072]{1,0:T(8,128)(2,1)} %broadcast_select_fusion.refs_6_.refs_1_), channel_id=1, source_target_pairs={{0,4},{4,0},{8,12},{12,8},{16,20},{20,16},{24,28},{28,24},{1,5},{5... | collective-permute-start | bytes 5898248 | tf_op jit(solution)/shard_map/ppermute | solution.py:269
  137.8 45.5 %collective-permute-start.13 = (bf16[320,3072]{1,0:T(8,128)(2,1)}, bf16[320,3072]{1,0:T(8,128)(2,1)}, u32[]{:S(2)}, u32[]{:S(2)}) collective-permute-start(bf16[320,3072]{1,0:T(8,128)(2,1)} %broadcast_select_fusion.refs_6_.refs_1_), channel_id=1, source_target_pairs={{0,1},{1,0},{2,3},{3,2},{4,5},{5,4},{6,7},{7,6},{8,9},{9,8},{10,11... | collective-permute-start | bytes 5898248 | tf_op jit(solution)/shard_map/ppermute | solution.py:269
  139.3 45.2 %collective-permute-start.14 = (bf16[320,3072]{1,0:T(8,128)(2,1)}, bf16[320,3072]{1,0:T(8,128)(2,1)}, u32[]{:S(2)}, u32[]{:S(2)}) collective-permute-start(bf16[320,3072]{1,0:T(8,128)(2,1)} %broadcast_select_fusion.refs_6_.refs_1_), channel_id=1, source_target_pairs={{0,2},{1,3},{2,0},{3,1},{4,6},{5,7},{6,4},{7,5},{8,10},{9,11},{10,... | collective-permute-start | bytes 5898248 | tf_op jit(solution)/shard_map/ppermute | solution.py:269
  140.8 32.8 %collective-permute-start.16 = (bf16[192,3072]{1,0:T(8,128)(2,1)}, bf16[192,3072]{1,0:T(8,128)(2,1)}, u32[]{:S(2)}, u32[]{:S(2)}) collective-permute-start(bf16[192,3072]{1,0:T(8,128)(2,1)} %collective-permute-done.5.refs_1_), channel_id=1, source_target_pairs={{8,16},{12,20},{16,8},{20,12},{9,17},{13,21},{17,9},{21,13},{10,18... | collective-permute-start | bytes 3538952 | tf_op jit(solution)/shard_map/ppermute | solution.py:269
  142.5 31.1 %collective-permute-start.15 = (bf16[192,3072]{1,0:T(8,128)(2,1)}, bf16[192,3072]{1,0:T(8,128)(2,1)}, u32[]{:S(2)}, u32[]{:S(2)}) collective-permute-start(bf16[192,3072]{1,0:T(8,128)(2,1)} %collective-permute-done.6), channel_id=1, source_target_pairs={{8,0},{12,4},{16,24},{20,28},{9,1},{13,5},{17,25},{21,29},{10,2},{... | collective-permute-start | bytes 3538952 | tf_op jit(solution)/shard_map/ppermute | solution.py:269
  184.5 6.3 %collective-permute-start.23 = (bf16[320,3072]{1,0:T(8,128)(2,1)}, bf16[320,3072]{1,0:T(8,128)(2,1)}, u32[]{:S(2)}, u32[]{:S(2)}) collective-permute-start(bf16[320,3072]{1,0:T(8,128)(2,1)} %collective-permute-done.13.x_ref.refs_8_.refs_3_), channel_id=1, source_target_pairs={{0,4},{4,0},{8,12},{12,8},{16,20},{20,16},{24,28},{28,24},{1,5},{5... | collective-permute-start | bytes 5898248 | tf_op jit(solution)/shard_map/ppermute | solution.py:269
  184.5 7.1 %collective-permute-start.24 = (bf16[320,3072]{1,0:T(8,128)(2,1)}, bf16[320,3072]{1,0:T(8,128)(2,1)}, u32[]{:S(2)}, u32[]{:S(2)}) collective-permute-start(bf16[320,3072]{1,0:T(8,128)(2,1)} %collective-permute-done.14.y_ref.refs_9_.refs_4_), channel_id=1, source_target_pairs={{0,4},{4,0},{8,12},{12,8},{16,20},{20,16},{24,28},{28,24},{1,5},{5... | collective-permute-start | bytes 5898248 | tf_op jit(solution)/shard_map/ppermute | solution.py:269
  185.0 30.6 %collective-permute-start.22 = (bf16[192,3072]{1,0:T(8,128)(2,1)}, bf16[192,3072]{1,0:T(8,128)(2,1)}, u32[]{:S(2)}, u32[]{:S(2)}) collective-permute-start(bf16[192,3072]{1,0:T(8,128)(2,1)} %collective-permute-done.16), channel_id=1, source_target_pairs={{8,0},{12,4},{16,24},{20,28},{9,1},{13,5},{17,25},{21,29},{10,2},{... | collective-permute-start | bytes 3538952 | tf_op jit(solution)/shard_map/ppermute | solution.py:269
  188.6 26.9 %collective-permute-start.20 = (bf16[160,3072]{1,0:T(8,128)(2,1)}, bf16[160,3072]{1,0:T(8,128)(2,1)}, u32[]{:S(2)}, u32[]{:S(2)}) collective-permute-start(bf16[160,3072]{1,0:T(8,128)(2,1)} %get-tuple-element.80), channel_id=1, source_target_pairs={{0,1},{1,0},{2,3},{3,2},{4,5},{5,4},{6,7},{7,6},{8,9},{9,8},{10,11... | collective-permute-start | bytes 2949128 | tf_op jit(solution)/shard_map/ppermute | solution.py:269
  189.2 26.3 %collective-permute-start.21 = (bf16[160,3072]{1,0:T(8,128)(2,1)}, bf16[160,3072]{1,0:T(8,128)(2,1)}, u32[]{:S(2)}, u32[]{:S(2)}) collective-permute-start(bf16[160,3072]{1,0:T(8,128)(2,1)} %get-tuple-element.81), channel_id=1, source_target_pairs={{0,2},{1,3},{2,0},{3,1},{4,6},{5,7},{6,4},{7,5},{8,10},{9,11},{10,... | collective-permute-start | bytes 2949128 | tf_op jit(solution)/shard_map/ppermute | solution.py:269
  219.3 7.7 %collective-permute-start.29 = (bf16[384,3072]{1,0:T(8,128)(2,1)}, bf16[384,3072]{1,0:T(8,128)(2,1)}, u32[]{:S(2)}, u32[]{:S(2)}) collective-permute-start(bf16[384,3072]{1,0:T(8,128)(2,1)} %maximum_select_fusion.refs_1_), channel_id=1, source_target_pairs={{0,4},{4,0},{8,12},{12,8},{16,20},{20,16},{24,28},{28,24},{1,5},{5... | collective-permute-start | bytes 7077896 | tf_op jit(solution)/shard_map/ppermute | solution.py:269
  219.5 60.4 %collective-permute-start.25 = (bf16[384,3072]{1,0:T(8,128)(2,1)}, bf16[384,3072]{1,0:T(8,128)(2,1)}, u32[]{:S(2)}, u32[]{:S(2)}) collective-permute-start(bf16[384,3072]{1,0:T(8,128)(2,1)} %maximum_select_fusion.refs_1_), channel_id=1, source_target_pairs={{0,1},{1,0},{2,3},{3,2},{4,5},{5,4},{6,7},{7,6},{8,9},{9,8},{10,11... | collective-permute-start | bytes 7077896 | tf_op jit(solution)/shard_map/ppermute | solution.py:269
  220.0 59.9 %collective-permute-start.26 = (bf16[384,3072]{1,0:T(8,128)(2,1)}, bf16[384,3072]{1,0:T(8,128)(2,1)}, u32[]{:S(2)}, u32[]{:S(2)}) collective-permute-start(bf16[384,3072]{1,0:T(8,128)(2,1)} %maximum_select_fusion.refs_1_), channel_id=1, source_target_pairs={{0,2},{1,3},{2,0},{3,1},{4,6},{5,7},{6,4},{7,5},{8,10},{9,11},{10,... | collective-permute-start | bytes 7077896 | tf_op jit(solution)/shard_map/ppermute | solution.py:269
  221.5 4.1 %collective-permute-start.27 = (bf16[160,3072]{1,0:T(8,128)(2,1)}, bf16[160,3072]{1,0:T(8,128)(2,1)}, u32[]{:S(2)}, u32[]{:S(2)}) collective-permute-start(bf16[160,3072]{1,0:T(8,128)(2,1)} %collective-permute-done.20.refs_4_.refs_7_), channel_id=1, source_target_pairs={{0,4},{4,0},{8,12},{12,8},{16,20},{20,16},{24,28},{28,24},{1,5},{5... | collective-permute-start | bytes 2949128 | tf_op jit(solution)/shard_map/ppermute | solution.py:269
  221.5 5.5 %collective-permute-start.28 = (bf16[160,3072]{1,0:T(8,128)(2,1)}, bf16[160,3072]{1,0:T(8,128)(2,1)}, u32[]{:S(2)}, u32[]{:S(2)}) collective-permute-start(bf16[160,3072]{1,0:T(8,128)(2,1)} %collective-permute-done.21.refs_5_.refs_8_), channel_id=1, source_target_pairs={{0,4},{4,0},{8,12},{12,8},{16,20},{20,16},{24,28},{28,24},{1,5},{5... | collective-permute-start | bytes 2949128 | tf_op jit(solution)/shard_map/ppermute | solution.py:269
  240.1 72.5 %collective-permute-start.32 = (bf16[512,3072]{1,0:T(8,128)(2,1)}, bf16[512,3072]{1,0:T(8,128)(2,1)}, u32[]{:S(2)}, u32[]{:S(2)}) collective-permute-start(bf16[512,3072]{1,0:T(8,128)(2,1)} %shard_map.66), channel_id=1, source_target_pairs={{0,8},{4,12},{8,0},{12,4},{16,24},{20,28},{24,16},{28,20},{1,9},{5... | collective-permute-start | bytes 9437192 | tf_op jit(solution)/shard_map/ppermute | solution.py:269
  279.9 5.2 %collective-permute-start.33 = (bf16[384,3072]{1,0:T(8,128)(2,1)}, bf16[384,3072]{1,0:T(8,128)(2,1)}, u32[]{:S(2)}, u32[]{:S(2)}) collective-permute-start(bf16[384,3072]{1,0:T(8,128)(2,1)} %collective-permute-done.25.x_ref.refs_1_), channel_id=1, source_target_pairs={{0,4},{4,0},{8,12},{12,8},{16,20},{20,16},{24,28},{28,24},{1,5},{5... | collective-permute-start | bytes 7077896 | tf_op jit(solution)/shard_map/ppermute | solution.py:269
  280.0 8.2 %collective-permute-start.34 = (bf16[384,3072]{1,0:T(8,128)(2,1)}, bf16[384,3072]{1,0:T(8,128)(2,1)}, u32[]{:S(2)}, u32[]{:S(2)}) collective-permute-start(bf16[384,3072]{1,0:T(8,128)(2,1)} %collective-permute-done.26.y_ref.refs_2_), channel_id=1, source_target_pairs={{0,4},{4,0},{8,12},{12,8},{16,20},{20,16},{24,28},{28,24},{1,5},{5... | collective-permute-start | bytes 7077896 | tf_op jit(solution)/shard_map/ppermute | solution.py:269
  283.0 28.3 %collective-permute-start.30 = (bf16[192,3072]{1,0:T(8,128)(2,1)}, bf16[192,3072]{1,0:T(8,128)(2,1)}, u32[]{:S(2)}, u32[]{:S(2)}) collective-permute-start(bf16[192,3072]{1,0:T(8,128)(2,1)} %get-tuple-element.97), channel_id=1, source_target_pairs={{0,1},{1,0},{2,3},{3,2},{4,5},{5,4},{6,7},{7,6},{8,9},{9,8},{10,11... | collective-permute-start | bytes 3538952 | tf_op jit(solution)/shard_map/ppermute | solution.py:269
  284.6 28.0 %collective-permute-start.31 = (bf16[192,3072]{1,0:T(8,128)(2,1)}, bf16[192,3072]{1,0:T(8,128)(2,1)}, u32[]{:S(2)}, u32[]{:S(2)}) collective-permute-start(bf16[192,3072]{1,0:T(8,128)(2,1)} %get-tuple-element.98), channel_id=1, source_target_pairs={{0,2},{1,3},{2,0},{3,1},{4,6},{5,7},{6,4},{7,5},{8,10},{9,11},{10,... | collective-permute-start | bytes 3538952 | tf_op jit(solution)/shard_map/ppermute | solution.py:269
  312.6 3.2 collective-permute-start.35
  312.6 4.9 %collective-permute-start.36 = (bf16[192,3072]{1,0:T(8,128)(2,1)}, bf16[192,3072]{1,0:T(8,128)(2,1)}, u32[]{:S(2)}, u32[]{:S(2)}) collective-permute-start(bf16[192,3072]{1,0:T(8,128)(2,1)} %collective-permute-done.31.refs_2_), channel_id=1, source_target_pairs={{0,4},{4,0},{8,12},{12,8},{16,20},{20,16},{24,28},{28,24},{1,5},{5... | collective-permute-start | bytes 3538952 | tf_op jit(solution)/shard_map/ppermute | solution.py:269

commit v5 on v4

--- a/solution.py
+++ b/solution.py
@@ -300,7 +300,8 @@
     x_ds0, x_ds1, e_s = fence((core(x_d0), core(x_d1), core(e)))
     x_d = [x_d0, x_d1, x_ds0, x_ds1]
     out_c0, next_c = outward(far_c), across(guest_c)
-    (home,) = pair_sums([x], [x_x, x_y, x_xs, x_ys, *x_d], [home], 1024)
+    ahead = rows - early
+    (home,) = pair_sums([x], [x_x, x_y, x_xs, x_ys, *x_d, e, (e_s, 0, ahead)], [home], 1792)
     e_x, e_y, out_c0, next_c, home = fence((e_x, e_y, out_c0, next_c, home))
 
     e_d0, e_d1 = corner(e_x, e_y)
@@ -312,12 +313,13 @@
 
     c = jnp.where(inner, jnp.concatenate([far_c, next_c]), jnp.concatenate([out_c0, out_c1]))
     c_x, c_y = along_x(c), along_y(c)
-    e_ds0, e_ds1, c_s = fence((core(e_d0), core(e_d1), core(c)))
+    e_ds0, e_ds1 = fence((core(e_d0), core(e_d1)))
+    c_s = core(c)
     e_d = [e_d0, e_d1, e_ds0, e_ds1]
     (visit,) = pair_sums(guest, [(e_xs, lead, early - lead), e_ys, *e_d], [visit], 1024, narrow=True)
     visit, home = fence((visit, home))
     back = partner(visit)
-    (home,) = pair_sums([x], [e, e_s, e_x, e_y, e_xs, e_ys, *e_d], [home], 1280)
+    (home,) = pair_sums([x], [(e_s, ahead, early - ahead), e_x, e_y, e_xs, e_ys, *e_d], [home], 1024)
     (home,) = pair_sums([x], [c, c_s], [home], 768)
     c_x, c_y, home = fence((c_x, c_y, home))
 

time: 331 us -> 330 us (level)
  transfers between devices with their start and end apart: 37 -> 37, of which waited for: 16 -> 17; matrix products, arithmetic and copies ran while one was open for 1% -> 1% of each run, Pallas kernels for 59% -> 59%
where the time goes in v5:
time: 330 us
  Pallas kernels  210 us (64%)
  waiting for transfers between devices  70.8 us (21%)
  starting transfers between devices  40.9 us (12%)
  other arithmetic  6.73 us (2%)
    pallas_call x9, Pallas kernels, pair_sums(): pl.pallas_call(functools.partial(pair_kernel, feat, i_rows, spans, tile,...  175 us
    ppermute x37, waiting for transfers between devices, move(): return lambda v: lax.ppermute(v, axis, pairs)  70.8 us
    ppermute x37, starting transfers between devices, move(): return lambda v: lax.ppermute(v, axis, pairs)  40.9 us
    pallas_call x1, Pallas kernels, trace_terms(): pl.pallas_call(functools.partial(trace_kernel, feat), grid=(rows // LANES...  23.9 us
    pallas_call x3, Pallas kernels, cut(): pl.pallas_call(functools.partial(cut_kernel, mid, parts), in_specs=[spec]...  7.75 us
  transfers between devices with their start and end apart: 37, of which 17 were waited for; matrix products, arithmetic and copies ran while one was open for 1% of the time, Pallas kernels for 59%

profile of v5, /device:TPU:0, one launch (start us, length us, event | category | flops | bytes accessed | tf_op | source)
XLA Modules:
  0.0 329.7 jit_solution(8524003753029488224)
XLA Ops:
  0.6 4.0 %shard_map.58 = (bf16[512,3072]{1,0:T(8,128)(2,1)}, bf16[320,3072]{1,0:T(8,128)(2,1)}, bf16[192,3072]{1,0:T(8,128)(2,1)}) custom-call(bf16[512,1024]{1,0:T(8,128)(2,1)} %a_ref.1, bf16[512,1024]{1,0:T(8,128)(2,1)} %b_ref.1, bf16[512,1024]{1,0:T(8,128)(2,1)} %c_ref.1), custom_call_target="tpu_custom_call" | custom-call | flops 512 | bytes 1024 | tf_op jit(solution)/shard_map/pallas_call | solution.py:250
  5.1 2.7 collective-permute-start.2
  7.8 1.9 collective-permute-start.3
  9.7 1.5 collective-permute-start
  11.2 1.5 collective-permute-start.1
  12.7 23.9 %shard_map.59.refs_3_ = f32[512,3072]{1,0:T(8,128)} custom-call(bf16[512,3072]{1,0:T(8,128)(2,1)} %get-tuple-element.53.x_ref.refs_0_.refs_1_.refs_2_), custom_call_target="tpu_custom_call" | custom-call | flops 512 | bytes 3072 | tf_op jit(solution)/shard_map/pallas_call | solution.py:42
  36.6 13.2 %shard_map.60.refs_11_ = f32[512,3072]{1,0:T(8,128)} custom-call(bf16[512,3072]{1,0:T(8,128)(2,1)} %get-tuple-element.53.x_ref.refs_0_.refs_1_.refs_2_, bf16[512,3072]{1,0:T(8,128)(2,1)} %get-tuple-element.53.x_ref.refs_0_.refs_1_.refs_2_, bf16[512,3072]{1,0:T(8,128)(2,1)} %collective-permute-done.4.refs_2_.refs_3_, ...), custom_call_target="tpu_custom_call", output_to_operand_aliasing={{}: (3, {})} | custom-call | flops 512 | bytes 3072 | tf_op jit(solution)/shard_map/pallas_call | solution.py:173
  49.9 1.7 collective-permute-done.2.refs_0_
  51.5 4.8 %collective-permute-start.5 = (bf16[192,3072]{1,0:T(8,128)(2,1)}, bf16[192,3072]{1,0:T(8,128)(2,1)}, u32[]{:S(2)}, u32[]{:S(2)}) collective-permute-start(bf16[192,3072]{1,0:T(8,128)(2,1)} %get-tuple-element.56), channel_id=1, source_target_pairs={{0,8},{4,12},{8,0},{12,4},{16,24},{20,28},{24,16},{28,20},{1,9},{5... | collective-permute-start | bytes 3538952 | tf_op jit(solution)/shard_map/ppermute | solution.py:269
  56.3 1.8 collective-permute-start.6
  58.0 22.1 %collective-permute-done.x_ref.refs_4_.refs_1_ = bf16[512,3072]{1,0:T(8,128)(2,1)} collective-permute-done((bf16[512,3072]{1,0:T(8,128)(2,1)}, bf16[512,3072]{1,0:T(8,128)(2,1)}, u32[]{:S(2)}, u32[]{:S(2)}) %collective-permute-start) | collective-permute-done | bytes 3145760 | tf_op jit(solution)/shard_map/ppermute | solution.py:269
  80.2 1.2 collective-permute-done.1.y_ref.refs_5_.refs_2_
  82.9 1.9 collective-permute-start.10
  84.9 1.3 collective-permute-start.9
  86.1 2.9 shard_map.61
  89.0 1.6 collective-permute-start.7
  90.6 1.5 collective-permute-start.8
  92.9 28.1 %shard_map.62.refs_11_ = f32[512,3072]{1,0:T(8,128)} custom-call(bf16[320,3072]{1,0:T(8,128)(2,1)} %collective-permute-done.2.refs_0_, bf16[192,3072]{1,0:T(8,128)(2,1)} %collective-permute-done.5.refs_1_, bf16[512,3072]{1,0:T(8,128)(2,1)} %get-tuple-element.53.x_ref.refs_0_.refs_1_.refs_2_, bf16[512,3072]{1,0:T(8,128)(2,1)} %collective-permute-done.4.refs_2_.refs_3_, ...), custom_call_target="tpu_custom_call" | custom-call | flops 512 | bytes 3072 | tf_op jit(solution)/shard_map/pallas_call | solution.py:173
  121.1 13.1 %collective-permute-done.9 = bf16[320,3072]{1,0:T(8,128)(2,1)} collective-permute-done((bf16[320,3072]{1,0:T(8,128)(2,1)}, bf16[320,3072]{1,0:T(8,128)(2,1)}, u32[]{:S(2)}, u32[]{:S(2)}) %collective-permute-start.9) | collective-permute-done | bytes 1966112 | tf_op jit(solution)/shard_map/ppermute | solution.py:269
  134.7 3.0 broadcast_select_fusion.refs_9_.refs_6_
  137.8 1.5 collective-permute-start.13
  139.3 1.5 collective-permute-start.14
  140.8 1.7 collective-permute-start.16
  142.5 1.5 collective-permute-start.15
  144.0 33.0 %shard_map.63.refs_10_ = f32[512,3072]{1,0:T(8,128)} custom-call(bf16[512,3072]{1,0:T(8,128)(2,1)} %get-tuple-element.53.x_ref.refs_0_.refs_1_.refs_2_, bf16[512,3072]{1,0:T(8,128)(2,1)} %collective-permute-done.x_ref.refs_4_.refs_1_, bf16[512,3072]{1,0:T(8,128)(2,1)} %collective-permute-done.1.y_ref.refs_5_.refs_2_, ...), custom_call_target="tpu_custom_call", output_to_operand_aliasing={{}: (11, {})} | custom-call | flops 512 | bytes 3072 | tf_op jit(solution)/shard_map/pallas_call | solution.py:173
  177.0 6.3 %collective-permute-done.13.x_ref.refs_8_.refs_2_ = bf16[320,3072]{1,0:T(8,128)(2,1)} collective-permute-done((bf16[320,3072]{1,0:T(8,128)(2,1)}, bf16[320,3072]{1,0:T(8,128)(2,1)}, u32[]{:S(2)}, u32[]{:S(2)}) %collective-permute-start.13) | collective-permute-done | bytes 1966112 | tf_op jit(solution)/shard_map/ppermute | solution.py:269
  185.0 1.3 collective-permute-start.22
  186.3 2.4 shard_map.64
  189.2 1.5 collective-permute-start.21
  191.6 24.0 %shard_map.65.refs_8_ = f32[512,3072]{1,0:T(8,128)} custom-call(bf16[320,3072]{1,0:T(8,128)(2,1)} %collective-permute-done.2.refs_0_, bf16[192,3072]{1,0:T(8,128)(2,1)} %collective-permute-done.5.refs_1_, bf16[256,3072]{1,0:T(8,128)(2,1)} %collective-permute-done.7.refs_5_.refs_2_, ...), custom_call_target="tpu_custom_call", output_to_operand_aliasing={{}: (11, {})} | custom-call | flops 512 | bytes 3072 | tf_op jit(solution)/shard_map/pallas_call | solution.py:173
  215.6 3.7 %maximum_select_fusion.refs_1_ = bf16[384,3072]{1,0:T(8,128)(2,1)} fusion(bf16[192,3072]{1,0:T(8,128)(2,1)} %collective-permute-done.16, bf16[192,3072]{1,0:T(8,128)(2,1)} %collective-permute-done.6, bf16[192,3072]{1,0:T(8,128)(2,1)} %collective-permute-done.22, bf16[192,3072]{1,0:T(8,128)(2,1)} %collective-permute-done.15, pred[]{:T(512)S(6)} %and.4), kind=kLoop, calls=%fused_computation | loop fusion | flops 10616832 | bytes 7077889 | tf_op jit(solution)/shard_map/jit(_where)/select_n | solution.py:314
  220.0 1.5 collective-permute-start.26
  222.0 3.5 %collective-permute-done.28.refs_6_.refs_8_ = bf16[160,3072]{1,0:T(8,128)(2,1)} collective-permute-done((bf16[160,3072]{1,0:T(8,128)(2,1)}, bf16[160,3072]{1,0:T(8,128)(2,1)}, u32[]{:S(2)}, u32[]{:S(2)}) %collective-permute-start.28) | collective-permute-done | bytes 983072 | tf_op jit(solution)/shard_map/ppermute | solution.py:269
  225.6 1.4 collective-permute-done.29.refs_7_.refs_9_
  227.0 13.1 %shard_map.66 = bf16[512,3072]{1,0:T(8,128)(2,1)} custom-call(bf16[320,3072]{1,0:T(8,128)(2,1)} %collective-permute-done.2.refs_0_, bf16[192,3072]{1,0:T(8,128)(2,1)} %collective-permute-done.5.refs_1_, bf16[320,3072]{1,0:T(8,128)(2,1)} %collective-permute-done.23.refs_10_.refs_2_.refs_4_, bf16[320,3072]{1,0:T(8,128)(2,1)} %collective-permute-done.24.refs_3_.refs_5_, ...), custom_call_target="tpu_custom_call" | custom-call | flops 512 | bytes 3072 | tf_op jit(solution)/shard_map/pallas_call | solution.py:173
  240.1 2.9 collective-permute-start.32
  242.9 20.8 %shard_map.67.refs_3_ = f32[512,3072]{1,0:T(8,128)} custom-call(bf16[512,3072]{1,0:T(8,128)(2,1)} %get-tuple-element.53.x_ref.refs_0_.refs_1_.refs_2_, bf16[320,3072]{1,0:T(8,128)(2,1)} %collective-permute-done.19.refs_10_.refs_7_.refs_1_, bf16[320,3072]{1,0:T(8,128)(2,1)} %collective-permute-done.13.x_ref.refs_8_.refs_2_, ...), custom_call_target="tpu_custom_call", output_to_operand_aliasing={{}: (10, {})} | custom-call | flops 512 | bytes 3072 | tf_op jit(solution)/shard_map/pallas_call | solution.py:173
  263.8 11.9 %shard_map.68.refs_5_ = f32[512,3072]{1,0:T(8,128)} custom-call(bf16[512,3072]{1,0:T(8,128)(2,1)} %get-tuple-element.53.x_ref.refs_0_.refs_1_.refs_2_, bf16[384,3072]{1,0:T(8,128)(2,1)} %maximum_select_fusion.refs_1_, bf16[384,3072]{1,0:T(8,128)(2,1)} %collective-permute-done.27.refs_2_, f32[512,3072]{1,0:T(8,128)} %shard_map.67.refs_3_), custom_call_target="tpu_custom_call", output_to_operand_aliasing={{}: (3, {})} | custom-call | flops 512 | bytes 3072 | tf_op jit(solution)/shard_map/pallas_call | solution.py:173
  276.3 2.5 shard_map.69
  278.9 1.6 collective-permute-start.30
  281.0 3.1 collective-permute-done.34.refs_4_
  284.1 17.5 %shard_map.70.refs_5_ = f32[512,3072]{1,0:T(8,128)} custom-call(bf16[512,3072]{1,0:T(8,128)(2,1)} %get-tuple-element.53.x_ref.refs_0_.refs_1_.refs_2_, bf16[384,3072]{1,0:T(8,128)(2,1)} %collective-permute-done.25.x_ref.refs_1_, bf16[384,3072]{1,0:T(8,128)(2,1)} %collective-permute-done.26.y_ref.refs_2_, ...), custom_call_target="tpu_custom_call", output_to_operand_aliasing={{}: (5, {})} | custom-call | flops 512 | bytes 3072 | tf_op jit(solution)/shard_map/pallas_call | solution.py:173
  301.6 5.7 %collective-permute-done.30.refs_1_ = bf16[192,3072]{1,0:T(8,128)(2,1)} collective-permute-done((bf16[192,3072]{1,0:T(8,128)(2,1)}, bf16[192,3072]{1,0:T(8,128)(2,1)}, u32[]{:S(2)}, u32[]{:S(2)}) %collective-permute-start.30) | collective-permute-done | bytes 1179680 | tf_op jit(solution)/shard_map/ppermute | solution.py:269
  307.2 1.2 collective-permute-done.31.refs_2_
  308.4 3.2 collective-permute-done.32.refs_6_
  312.2 2.7 collective-permute-done.35.refs_3_
  314.9 1.7 collective-permute-done.36.refs_4_
  316.5 12.9 %shard_map.71 = (f32[512,1024]{1,0:T(8,128)}, f32[512,1024]{1,0:T(8,128)}, f32[512,1024]{1,0:T(8,128)}) custom-call(bf16[512,3072]{1,0:T(8,128)(2,1)} %get-tuple-element.53.x_ref.refs_0_.refs_1_.refs_2_, bf16[192,3072]{1,0:T(8,128)(2,1)} %collective-permute-done.30.refs_1_, bf16[192,3072]{1,0:T(8,128)(2,1)} %collective-permute-done.31.refs_2_, ...), custom_call_target="tpu_custom_call" | custom-call | flops 512 | bytes 3072 | tf_op jit(solution)/shard_map/pallas_call | solution.py:173
  (42 shorter events, 9.4 us)
Async XLA Ops:
  4.6 32.0 %collective-permute-start.4 = (bf16[512,3072]{1,0:T(8,128)(2,1)}, bf16[512,3072]{1,0:T(8,128)(2,1)}, u32[]{:S(2)}, u32[]{:S(2)}) collective-permute-start(bf16[512,3072]{1,0:T(8,128)(2,1)} %get-tuple-element.53.x_ref.refs_0_.refs_1_.refs_2_), channel_id=1, source_target_pairs={{0,4},{4,0},{8,12},{12,8},{16,20},{20,16},{24,28},{28,24},{1,5},{5... | collective-permute-start | bytes 9437192 | tf_op jit(solution)/shard_map/ppermute | solution.py:269
  5.1 46.4 %collective-permute-start.2 = (bf16[320,3072]{1,0:T(8,128)(2,1)}, bf16[320,3072]{1,0:T(8,128)(2,1)}, u32[]{:S(2)}, u32[]{:S(2)}) collective-permute-start(bf16[320,3072]{1,0:T(8,128)(2,1)} %get-tuple-element.54), channel_id=1, source_target_pairs={{0,8},{4,12},{8,0},{12,4},{16,24},{20,28},{24,16},{28,20},{1,9},{5... | collective-permute-start | bytes 5898248 | tf_op jit(solution)/shard_map/ppermute | solution.py:269
  7.8 43.7 %collective-permute-start.3 = (bf16[320,3072]{1,0:T(8,128)(2,1)}, bf16[320,3072]{1,0:T(8,128)(2,1)}, u32[]{:S(2)}, u32[]{:S(2)}) collective-permute-start(bf16[320,3072]{1,0:T(8,128)(2,1)} %get-tuple-element.54), channel_id=1, source_target_pairs={{8,16},{12,20},{16,8},{20,12},{9,17},{13,21},{17,9},{21,13},{10,18... | collective-permute-start | bytes 5898248 | tf_op jit(solution)/shard_map/ppermute | solution.py:269
  9.7 70.5 %collective-permute-start = (bf16[512,3072]{1,0:T(8,128)(2,1)}, bf16[512,3072]{1,0:T(8,128)(2,1)}, u32[]{:S(2)}, u32[]{:S(2)}) collective-permute-start(bf16[512,3072]{1,0:T(8,128)(2,1)} %get-tuple-element.53.x_ref.refs_0_.refs_1_.refs_2_), channel_id=1, source_target_pairs={{0,1},{1,0},{2,3},{3,2},{4,5},{5,4},{6,7},{7,6},{8,9},{9,8},{10,11... | collective-permute-start | bytes 9437192 | tf_op jit(solution)/shard_map/ppermute | solution.py:269
  11.2 70.2 %collective-permute-start.1 = (bf16[512,3072]{1,0:T(8,128)(2,1)}, bf16[512,3072]{1,0:T(8,128)(2,1)}, u32[]{:S(2)}, u32[]{:S(2)}) collective-permute-start(bf16[512,3072]{1,0:T(8,128)(2,1)} %get-tuple-element.53.x_ref.refs_0_.refs_1_.refs_2_), channel_id=1, source_target_pairs={{0,2},{1,3},{2,0},{3,1},{4,6},{5,7},{6,4},{7,5},{8,10},{9,11},{10,... | collective-permute-start | bytes 9437192 | tf_op jit(solution)/shard_map/ppermute | solution.py:269
  51.5 30.9 %collective-permute-start.5 = (bf16[192,3072]{1,0:T(8,128)(2,1)}, bf16[192,3072]{1,0:T(8,128)(2,1)}, u32[]{:S(2)}, u32[]{:S(2)}) collective-permute-start(bf16[192,3072]{1,0:T(8,128)(2,1)} %get-tuple-element.56), channel_id=1, source_target_pairs={{0,8},{4,12},{8,0},{12,4},{16,24},{20,28},{24,16},{28,20},{1,9},{5... | collective-permute-start | bytes 3538952 | tf_op jit(solution)/shard_map/ppermute | solution.py:269
  56.3 26.1 %collective-permute-start.6 = (bf16[192,3072]{1,0:T(8,128)(2,1)}, bf16[192,3072]{1,0:T(8,128)(2,1)}, u32[]{:S(2)}, u32[]{:S(2)}) collective-permute-start(bf16[192,3072]{1,0:T(8,128)(2,1)} %get-tuple-element.56), channel_id=1, source_target_pairs={{8,16},{12,20},{16,8},{20,12},{9,17},{13,21},{17,9},{21,13},{10,18... | collective-permute-start | bytes 3538952 | tf_op jit(solution)/shard_map/ppermute | solution.py:269
  82.4 8.2 %collective-permute-start.11 = (bf16[512,3072]{1,0:T(8,128)(2,1)}, bf16[512,3072]{1,0:T(8,128)(2,1)}, u32[]{:S(2)}, u32[]{:S(2)}) collective-permute-start(bf16[512,3072]{1,0:T(8,128)(2,1)} %collective-permute-done.x_ref.refs_4_.refs_1_), channel_id=1, source_target_pairs={{0,4},{4,0},{8,12},{12,8},{16,20},{20,16},{24,28},{28,24},{1,5},{5... | collective-permute-start | bytes 9437192 | tf_op jit(solution)/shard_map/ppermute | solution.py:269
  82.4 10.5 %collective-permute-start.12 = (bf16[512,3072]{1,0:T(8,128)(2,1)}, bf16[512,3072]{1,0:T(8,128)(2,1)}, u32[]{:S(2)}, u32[]{:S(2)}) collective-permute-start(bf16[512,3072]{1,0:T(8,128)(2,1)} %collective-permute-done.1.y_ref.refs_5_.refs_2_), channel_id=1, source_target_pairs={{0,4},{4,0},{8,12},{12,8},{16,20},{20,16},{24,28},{28,24},{1,5},{5... | collective-permute-start | bytes 9437192 | tf_op jit(solution)/shard_map/ppermute | solution.py:269
  82.9 38.1 %collective-permute-start.10 = (bf16[320,3072]{1,0:T(8,128)(2,1)}, bf16[320,3072]{1,0:T(8,128)(2,1)}, u32[]{:S(2)}, u32[]{:S(2)}) collective-permute-start(bf16[320,3072]{1,0:T(8,128)(2,1)} %collective-permute-done.2.refs_0_), channel_id=1, source_target_pairs={{8,16},{12,20},{16,8},{20,12},{9,17},{13,21},{17,9},{21,13},{10,18... | collective-permute-start | bytes 5898248 | tf_op jit(solution)/shard_map/ppermute | solution.py:269
  84.9 49.3 %collective-permute-start.9 = (bf16[320,3072]{1,0:T(8,128)(2,1)}, bf16[320,3072]{1,0:T(8,128)(2,1)}, u32[]{:S(2)}, u32[]{:S(2)}) collective-permute-start(bf16[320,3072]{1,0:T(8,128)(2,1)} %collective-permute-done.3), channel_id=1, source_target_pairs={{8,0},{12,4},{16,24},{20,28},{9,1},{13,5},{17,25},{21,29},{10,2},{... | collective-permute-start | bytes 5898248 | tf_op jit(solution)/shard_map/ppermute | solution.py:269
  89.0 45.1 %collective-permute-start.7 = (bf16[256,3072]{1,0:T(8,128)(2,1)}, bf16[256,3072]{1,0:T(8,128)(2,1)}, u32[]{:S(2)}, u32[]{:S(2)}) collective-permute-start(bf16[256,3072]{1,0:T(8,128)(2,1)} %get-tuple-element.61), channel_id=1, source_target_pairs={{0,1},{1,0},{2,3},{3,2},{4,5},{5,4},{6,7},{7,6},{8,9},{9,8},{10,11... | collective-permute-start | bytes 4718600 | tf_op jit(solution)/shard_map/ppermute | solution.py:269
  90.6 43.6 %collective-permute-start.8 = (bf16[256,3072]{1,0:T(8,128)(2,1)}, bf16[256,3072]{1,0:T(8,128)(2,1)}, u32[]{:S(2)}, u32[]{:S(2)}) collective-permute-start(bf16[256,3072]{1,0:T(8,128)(2,1)} %get-tuple-element.62), channel_id=1, source_target_pairs={{0,2},{1,3},{2,0},{3,1},{4,6},{5,7},{6,4},{7,5},{8,10},{9,11},{10,... | collective-permute-start | bytes 4718600 | tf_op jit(solution)/shard_map/ppermute | solution.py:269
  134.2 6.6 %collective-permute-start.17 = (bf16[256,3072]{1,0:T(8,128)(2,1)}, bf16[256,3072]{1,0:T(8,128)(2,1)}, u32[]{:S(2)}, u32[]{:S(2)}) collective-permute-start(bf16[256,3072]{1,0:T(8,128)(2,1)} %collective-permute-done.7.refs_5_.refs_2_), channel_id=1, source_target_pairs={{0,4},{4,0},{8,12},{12,8},{16,20},{20,16},{24,28},{28,24},{1,5},{5... | collective-permute-start | bytes 4718600 | tf_op jit(solution)/shard_map/ppermute | solution.py:269
  134.2 8.3 %collective-permute-start.18 = (bf16[256,3072]{1,0:T(8,128)(2,1)}, bf16[256,3072]{1,0:T(8,128)(2,1)}, u32[]{:S(2)}, u32[]{:S(2)}) collective-permute-start(bf16[256,3072]{1,0:T(8,128)(2,1)} %collective-permute-done.8.refs_6_.refs_3_), channel_id=1, source_target_pairs={{0,4},{4,0},{8,12},{12,8},{16,20},{20,16},{24,28},{28,24},{1,5},{5... | collective-permute-start | bytes 4718600 | tf_op jit(solution)/shard_map/ppermute | solution.py:269
  137.7 6.3 %collective-permute-start.19 = (bf16[320,3072]{1,0:T(8,128)(2,1)}, bf16[320,3072]{1,0:T(8,128)(2,1)}, u32[]{:S(2)}, u32[]{:S(2)}) collective-permute-start(bf16[320,3072]{1,0:T(8,128)(2,1)} %broadcast_select_fusion.refs_9_.refs_6_), channel_id=1, source_target_pairs={{0,4},{4,0},{8,12},{12,8},{16,20},{20,16},{24,28},{28,24},{1,5},{5... | collective-permute-start | bytes 5898248 | tf_op jit(solution)/shard_map/ppermute | solution.py:269
  137.8 45.5 %collective-permute-start.13 = (bf16[320,3072]{1,0:T(8,128)(2,1)}, bf16[320,3072]{1,0:T(8,128)(2,1)}, u32[]{:S(2)}, u32[]{:S(2)}) collective-permute-start(bf16[320,3072]{1,0:T(8,128)(2,1)} %broadcast_select_fusion.refs_9_.refs_6_), channel_id=1, source_target_pairs={{0,1},{1,0},{2,3},{3,2},{4,5},{5,4},{6,7},{7,6},{8,9},{9,8},{10,11... | collective-permute-start | bytes 5898248 | tf_op jit(solution)/shard_map/ppermute | solution.py:269
  139.3 45.2 %collective-permute-start.14 = (bf16[320,3072]{1,0:T(8,128)(2,1)}, bf16[320,3072]{1,0:T(8,128)(2,1)}, u32[]{:S(2)}, u32[]{:S(2)}) collective-permute-start(bf16[320,3072]{1,0:T(8,128)(2,1)} %broadcast_select_fusion.refs_9_.refs_6_), channel_id=1, source_target_pairs={{0,2},{1,3},{2,0},{3,1},{4,6},{5,7},{6,4},{7,5},{8,10},{9,11},{10,... | collective-permute-start | bytes 5898248 | tf_op jit(solution)/shard_map/ppermute | solution.py:269
  140.8 36.2 %collective-permute-start.16 = (bf16[192,3072]{1,0:T(8,128)(2,1)}, bf16[192,3072]{1,0:T(8,128)(2,1)}, u32[]{:S(2)}, u32[]{:S(2)}) collective-permute-start(bf16[192,3072]{1,0:T(8,128)(2,1)} %collective-permute-done.5.refs_1_), channel_id=1, source_target_pairs={{8,16},{12,20},{16,8},{20,12},{9,17},{13,21},{17,9},{21,13},{10,18... | collective-permute-start | bytes 3538952 | tf_op jit(solution)/shard_map/ppermute | solution.py:269
  142.5 34.5 %collective-permute-start.15 = (bf16[192,3072]{1,0:T(8,128)(2,1)}, bf16[192,3072]{1,0:T(8,128)(2,1)}, u32[]{:S(2)}, u32[]{:S(2)}) collective-permute-start(bf16[192,3072]{1,0:T(8,128)(2,1)} %collective-permute-done.6), channel_id=1, source_target_pairs={{8,0},{12,4},{16,24},{20,28},{9,1},{13,5},{17,25},{21,29},{10,2},{... | collective-permute-start | bytes 3538952 | tf_op jit(solution)/shard_map/ppermute | solution.py:269
  184.5 6.3 %collective-permute-start.23 = (bf16[320,3072]{1,0:T(8,128)(2,1)}, bf16[320,3072]{1,0:T(8,128)(2,1)}, u32[]{:S(2)}, u32[]{:S(2)}) collective-permute-start(bf16[320,3072]{1,0:T(8,128)(2,1)} %collective-permute-done.13.x_ref.refs_8_.refs_2_), channel_id=1, source_target_pairs={{0,4},{4,0},{8,12},{12,8},{16,20},{20,16},{24,28},{28,24},{1,5},{5... | collective-permute-start | bytes 5898248 | tf_op jit(solution)/shard_map/ppermute | solution.py:269
  184.5 7.1 %collective-permute-start.24 = (bf16[320,3072]{1,0:T(8,128)(2,1)}, bf16[320,3072]{1,0:T(8,128)(2,1)}, u32[]{:S(2)}, u32[]{:S(2)}) collective-permute-start(bf16[320,3072]{1,0:T(8,128)(2,1)} %collective-permute-done.14.y_ref.refs_9_.refs_3_), channel_id=1, source_target_pairs={{0,4},{4,0},{8,12},{12,8},{16,20},{20,16},{24,28},{28,24},{1,5},{5... | collective-permute-start | bytes 5898248 | tf_op jit(solution)/shard_map/ppermute | solution.py:269
  185.0 30.6 %collective-permute-start.22 = (bf16[192,3072]{1,0:T(8,128)(2,1)}, bf16[192,3072]{1,0:T(8,128)(2,1)}, u32[]{:S(2)}, u32[]{:S(2)}) collective-permute-start(bf16[192,3072]{1,0:T(8,128)(2,1)} %collective-permute-done.16), channel_id=1, source_target_pairs={{8,0},{12,4},{16,24},{20,28},{9,1},{13,5},{17,25},{21,29},{10,2},{... | collective-permute-start | bytes 3538952 | tf_op jit(solution)/shard_map/ppermute | solution.py:269
  188.6 26.9 %collective-permute-start.20 = (bf16[160,3072]{1,0:T(8,128)(2,1)}, bf16[160,3072]{1,0:T(8,128)(2,1)}, u32[]{:S(2)}, u32[]{:S(2)}) collective-permute-start(bf16[160,3072]{1,0:T(8,128)(2,1)} %get-tuple-element.80), channel_id=1, source_target_pairs={{0,1},{1,0},{2,3},{3,2},{4,5},{5,4},{6,7},{7,6},{8,9},{9,8},{10,11... | collective-permute-start | bytes 2949128 | tf_op jit(solution)/shard_map/ppermute | solution.py:269
  189.2 26.3 %collective-permute-start.21 = (bf16[160,3072]{1,0:T(8,128)(2,1)}, bf16[160,3072]{1,0:T(8,128)(2,1)}, u32[]{:S(2)}, u32[]{:S(2)}) collective-permute-start(bf16[160,3072]{1,0:T(8,128)(2,1)} %get-tuple-element.81), channel_id=1, source_target_pairs={{0,2},{1,3},{2,0},{3,1},{4,6},{5,7},{6,4},{7,5},{8,10},{9,11},{10,... | collective-permute-start | bytes 2949128 | tf_op jit(solution)/shard_map/ppermute | solution.py:269
  219.3 44.5 %collective-permute-start.27 = (bf16[384,3072]{1,0:T(8,128)(2,1)}, bf16[384,3072]{1,0:T(8,128)(2,1)}, u32[]{:S(2)}, u32[]{:S(2)}) collective-permute-start(bf16[384,3072]{1,0:T(8,128)(2,1)} %maximum_select_fusion.refs_1_), channel_id=1, source_target_pairs={{0,4},{4,0},{8,12},{12,8},{16,20},{20,16},{24,28},{28,24},{1,5},{5... | collective-permute-start | bytes 7077896 | tf_op jit(solution)/shard_map/ppermute | solution.py:269
  219.5 56.3 %collective-permute-start.25 = (bf16[384,3072]{1,0:T(8,128)(2,1)}, bf16[384,3072]{1,0:T(8,128)(2,1)}, u32[]{:S(2)}, u32[]{:S(2)}) collective-permute-start(bf16[384,3072]{1,0:T(8,128)(2,1)} %maximum_select_fusion.refs_1_), channel_id=1, source_target_pairs={{0,1},{1,0},{2,3},{3,2},{4,5},{5,4},{6,7},{7,6},{8,9},{9,8},{10,11... | collective-permute-start | bytes 7077896 | tf_op jit(solution)/shard_map/ppermute | solution.py:269
  220.0 55.8 %collective-permute-start.26 = (bf16[384,3072]{1,0:T(8,128)(2,1)}, bf16[384,3072]{1,0:T(8,128)(2,1)}, u32[]{:S(2)}, u32[]{:S(2)}) collective-permute-start(bf16[384,3072]{1,0:T(8,128)(2,1)} %maximum_select_fusion.refs_1_), channel_id=1, source_target_pairs={{0,2},{1,3},{2,0},{3,1},{4,6},{5,7},{6,4},{7,5},{8,10},{9,11},{10,... | collective-permute-start | bytes 7077896 | tf_op jit(solution)/shard_map/ppermute | solution.py:269
  221.5 4.1 %collective-permute-start.28 = (bf16[160,3072]{1,0:T(8,128)(2,1)}, bf16[160,3072]{1,0:T(8,128)(2,1)}, u32[]{:S(2)}, u32[]{:S(2)}) collective-permute-start(bf16[160,3072]{1,0:T(8,128)(2,1)} %collective-permute-done.20.refs_4_.refs_6_), channel_id=1, source_target_pairs={{0,4},{4,0},{8,12},{12,8},{16,20},{20,16},{24,28},{28,24},{1,5},{5... | collective-permute-start | bytes 2949128 | tf_op jit(solution)/shard_map/ppermute | solution.py:269
  221.5 5.5 %collective-permute-start.29 = (bf16[160,3072]{1,0:T(8,128)(2,1)}, bf16[160,3072]{1,0:T(8,128)(2,1)}, u32[]{:S(2)}, u32[]{:S(2)}) collective-permute-start(bf16[160,3072]{1,0:T(8,128)(2,1)} %collective-permute-done.21.refs_5_.refs_7_), channel_id=1, source_target_pairs={{0,4},{4,0},{8,12},{12,8},{16,20},{20,16},{24,28},{28,24},{1,5},{5... | collective-permute-start | bytes 2949128 | tf_op jit(solution)/shard_map/ppermute | solution.py:269
  240.1 71.6 %collective-permute-start.32 = (bf16[512,3072]{1,0:T(8,128)(2,1)}, bf16[512,3072]{1,0:T(8,128)(2,1)}, u32[]{:S(2)}, u32[]{:S(2)}) collective-permute-start(bf16[512,3072]{1,0:T(8,128)(2,1)} %shard_map.66), channel_id=1, source_target_pairs={{0,8},{4,12},{8,0},{12,4},{16,24},{20,28},{24,16},{28,20},{1,9},{5... | collective-permute-start | bytes 9437192 | tf_op jit(solution)/shard_map/ppermute | solution.py:269
  275.8 5.2 %collective-permute-start.33 = (bf16[384,3072]{1,0:T(8,128)(2,1)}, bf16[384,3072]{1,0:T(8,128)(2,1)}, u32[]{:S(2)}, u32[]{:S(2)}) collective-permute-start(bf16[384,3072]{1,0:T(8,128)(2,1)} %collective-permute-done.25.x_ref.refs_1_), channel_id=1, source_target_pairs={{0,4},{4,0},{8,12},{12,8},{16,20},{20,16},{24,28},{28,24},{1,5},{5... | collective-permute-start | bytes 7077896 | tf_op jit(solution)/shard_map/ppermute | solution.py:269
  275.9 8.2 %collective-permute-start.34 = (bf16[384,3072]{1,0:T(8,128)(2,1)}, bf16[384,3072]{1,0:T(8,128)(2,1)}, u32[]{:S(2)}, u32[]{:S(2)}) collective-permute-start(bf16[384,3072]{1,0:T(8,128)(2,1)} %collective-permute-done.26.y_ref.refs_2_), channel_id=1, source_target_pairs={{0,4},{4,0},{8,12},{12,8},{16,20},{20,16},{24,28},{28,24},{1,5},{5... | collective-permute-start | bytes 7077896 | tf_op jit(solution)/shard_map/ppermute | solution.py:269
  278.9 28.3 %collective-permute-start.30 = (bf16[192,3072]{1,0:T(8,128)(2,1)}, bf16[192,3072]{1,0:T(8,128)(2,1)}, u32[]{:S(2)}, u32[]{:S(2)}) collective-permute-start(bf16[192,3072]{1,0:T(8,128)(2,1)} %get-tuple-element.95), channel_id=1, source_target_pairs={{0,1},{1,0},{2,3},{3,2},{4,5},{5,4},{6,7},{7,6},{8,9},{9,8},{10,11... | collective-permute-start | bytes 3538952 | tf_op jit(solution)/shard_map/ppermute | solution.py:269
  280.4 28.0 %collective-permute-start.31 = (bf16[192,3072]{1,0:T(8,128)(2,1)}, bf16[192,3072]{1,0:T(8,128)(2,1)}, u32[]{:S(2)}, u32[]{:S(2)}) collective-permute-start(bf16[192,3072]{1,0:T(8,128)(2,1)} %get-tuple-element.96), channel_id=1, source_target_pairs={{0,2},{1,3},{2,0},{3,1},{4,6},{5,7},{6,4},{7,5},{8,10},{9,11},{10,... | collective-permute-start | bytes 3538952 | tf_op jit(solution)/shard_map/ppermute | solution.py:269
  311.7 3.2 collective-permute-start.35
  311.7 4.9 %collective-permute-start.36 = (bf16[192,3072]{1,0:T(8,128)(2,1)}, bf16[192,3072]{1,0:T(8,128)(2,1)}, u32[]{:S(2)}, u32[]{:S(2)}) collective-permute-start(bf16[192,3072]{1,0:T(8,128)(2,1)} %collective-permute-done.31.refs_2_), channel_id=1, source_target_pairs={{0,4},{4,0},{8,12},{12,8},{16,20},{20,16},{24,28},{28,24},{1,5},{5... | collective-permute-start | bytes 3538952 | tf_op jit(solution)/shard_map/ppermute | solution.py:269

commit v6 on v5

--- a/solution.py
+++ b/solution.py
@@ -312,9 +312,8 @@
     e_d0, e_d1, out_c1, visit = fence((e_d0, e_d1, out_c1, visit))
 
     c = jnp.where(inner, jnp.concatenate([far_c, next_c]), jnp.concatenate([out_c0, out_c1]))
-    c_x, c_y = along_x(c), along_y(c)
-    e_ds0, e_ds1 = fence((core(e_d0), core(e_d1)))
-    c_s = core(c)
+    c, e_ds0, e_ds1 = fence((c, core(e_d0), core(e_d1)))
+    c_x, c_y, c_s = along_x(c), along_y(c), core(c)
     e_d = [e_d0, e_d1, e_ds0, e_ds1]
     (visit,) = pair_sums(guest, [(e_xs, lead, early - lead), e_ys, *e_d], [visit], 1024, narrow=True)
     visit, home = fence((visit, home))

time: 330 us -> 325 us (0.985)
  waiting for transfers between devices: 70.8 us -> 65.1 us
    ppermute x37, waiting for transfers between devices: 70.8 us -> 65.1 us  [move(): return lambda v: lax.ppermute(v, axis, pairs)]
  transfers between devices with their start and end apart: 37 -> 37, of which waited for: 17 -> 17; matrix products, arithmetic and copies ran while one was open for 1% -> 2% of each run, Pallas kernels for 59% -> 60%
where the time goes in v6:
time: 325 us
  Pallas kernels  210 us (65%)
  waiting for transfers between devices  65.1 us (20%)
  starting transfers between devices  41.7 us (13%)
  other arithmetic  6.72 us (2%)
    pallas_call x9, Pallas kernels, pair_sums(): pl.pallas_call(functools.partial(pair_kernel, feat, i_rows, spans, tile,...  175 us
    ppermute x37, waiting for transfers between devices, move(): return lambda v: lax.ppermute(v, axis, pairs)  65.1 us
    ppermute x37, starting transfers between devices, move(): return lambda v: lax.ppermute(v, axis, pairs)  41.7 us
    pallas_call x1, Pallas kernels, trace_terms(): pl.pallas_call(functools.partial(trace_kernel, feat), grid=(rows // LANES...  23.9 us
    pallas_call x3, Pallas kernels, cut(): pl.pallas_call(functools.partial(cut_kernel, mid, parts), in_specs=[spec]...  7.75 us
  transfers between devices with their start and end apart: 37, of which 17 were waited for; matrix products, arithmetic and copies ran while one was open for 2% of the time, Pallas kernels for 60%

profile of v6, /device:TPU:0, one launch (start us, length us, event | category | flops | bytes accessed | tf_op | source)
XLA Modules:
  0.0 324.7 jit_solution(12823540271748871944)
XLA Ops:
  0.6 4.0 %shard_map.58 = (bf16[512,3072]{1,0:T(8,128)(2,1)}, bf16[320,3072]{1,0:T(8,128)(2,1)}, bf16[192,3072]{1,0:T(8,128)(2,1)}) custom-call(bf16[512,1024]{1,0:T(8,128)(2,1)} %a_ref.1, bf16[512,1024]{1,0:T(8,128)(2,1)} %b_ref.1, bf16[512,1024]{1,0:T(8,128)(2,1)} %c_ref.1), custom_call_target="tpu_custom_call" | custom-call | flops 512 | bytes 1024 | tf_op jit(solution)/shard_map/pallas_call | solution.py:250
  5.1 2.7 collective-permute-start.2
  7.8 2.0 collective-permute-start.3
  9.8 1.5 collective-permute-start
  11.3 1.5 collective-permute-start.1
  12.8 23.9 %shard_map.59.refs_3_ = f32[512,3072]{1,0:T(8,128)} custom-call(bf16[512,3072]{1,0:T(8,128)(2,1)} %get-tuple-element.54.x_ref.refs_0_.refs_1_.refs_2_), custom_call_target="tpu_custom_call" | custom-call | flops 512 | bytes 3072 | tf_op jit(solution)/shard_map/pallas_call | solution.py:42
  36.7 13.2 %shard_map.60.refs_11_ = f32[512,3072]{1,0:T(8,128)} custom-call(bf16[512,3072]{1,0:T(8,128)(2,1)} %get-tuple-element.54.x_ref.refs_0_.refs_1_.refs_2_, bf16[512,3072]{1,0:T(8,128)(2,1)} %get-tuple-element.54.x_ref.refs_0_.refs_1_.refs_2_, bf16[512,3072]{1,0:T(8,128)(2,1)} %collective-permute-done.4.refs_2_.refs_3_, ...), custom_call_target="tpu_custom_call", output_to_operand_aliasing={{}: (3, {})} | custom-call | flops 512 | bytes 3072 | tf_op jit(solution)/shard_map/pallas_call | solution.py:173
  50.0 1.6 collective-permute-done.2.refs_0_
  51.5 4.8 %collective-permute-start.5 = (bf16[192,3072]{1,0:T(8,128)(2,1)}, bf16[192,3072]{1,0:T(8,128)(2,1)}, u32[]{:S(2)}, u32[]{:S(2)}) collective-permute-start(bf16[192,3072]{1,0:T(8,128)(2,1)} %get-tuple-element.57), channel_id=1, source_target_pairs={{0,8},{4,12},{8,0},{12,4},{16,24},{20,28},{24,16},{28,20},{1,9},{5... | collective-permute-start | bytes 3538952 | tf_op jit(solution)/shard_map/ppermute | solution.py:269
  56.3 1.7 collective-permute-start.6
  58.0 22.3 %collective-permute-done.x_ref.refs_4_.refs_1_ = bf16[512,3072]{1,0:T(8,128)(2,1)} collective-permute-done((bf16[512,3072]{1,0:T(8,128)(2,1)}, bf16[512,3072]{1,0:T(8,128)(2,1)}, u32[]{:S(2)}, u32[]{:S(2)}) %collective-permute-start) | collective-permute-done | bytes 3145760 | tf_op jit(solution)/shard_map/ppermute | solution.py:269
  80.3 1.2 collective-permute-done.1.y_ref.refs_5_.refs_2_
  81.5 0.9 collective-permute-done.5.refs_1_
  82.9 1.9 collective-permute-start.10
  84.8 1.3 collective-permute-start.9
  86.1 2.9 shard_map.61
  89.0 1.6 collective-permute-start.7
  90.5 1.5 collective-permute-start.8
  92.9 28.1 %shard_map.62.refs_11_ = f32[512,3072]{1,0:T(8,128)} custom-call(bf16[320,3072]{1,0:T(8,128)(2,1)} %collective-permute-done.2.refs_0_, bf16[192,3072]{1,0:T(8,128)(2,1)} %collective-permute-done.5.refs_1_, bf16[512,3072]{1,0:T(8,128)(2,1)} %get-tuple-element.54.x_ref.refs_0_.refs_1_.refs_2_, bf16[512,3072]{1,0:T(8,128)(2,1)} %collective-permute-done.4.refs_2_.refs_3_, ...), custom_call_target="tpu_custom_call" | custom-call | flops 512 | bytes 3072 | tf_op jit(solution)/shard_map/pallas_call | solution.py:173
  121.1 13.1 %collective-permute-done.9 = bf16[320,3072]{1,0:T(8,128)(2,1)} collective-permute-done((bf16[320,3072]{1,0:T(8,128)(2,1)}, bf16[320,3072]{1,0:T(8,128)(2,1)}, u32[]{:S(2)}, u32[]{:S(2)}) %collective-permute-start.9) | collective-permute-done | bytes 1966112 | tf_op jit(solution)/shard_map/ppermute | solution.py:269
  134.7 3.0 broadcast_select_fusion.refs_9_.refs_6_
  137.8 1.5 collective-permute-start.13
  139.3 1.5 collective-permute-start.14
  140.8 1.7 collective-permute-start.16
  142.5 1.5 collective-permute-start.15
  143.9 33.0 %shard_map.63.refs_10_ = f32[512,3072]{1,0:T(8,128)} custom-call(bf16[512,3072]{1,0:T(8,128)(2,1)} %get-tuple-element.54.x_ref.refs_0_.refs_1_.refs_2_, bf16[512,3072]{1,0:T(8,128)(2,1)} %collective-permute-done.x_ref.refs_4_.refs_1_, bf16[512,3072]{1,0:T(8,128)(2,1)} %collective-permute-done.1.y_ref.refs_5_.refs_2_, ...), custom_call_target="tpu_custom_call", output_to_operand_aliasing={{}: (11, {})} | custom-call | flops 512 | bytes 3072 | tf_op jit(solution)/shard_map/pallas_call | solution.py:173
  177.0 6.3 %collective-permute-done.13.x_ref.refs_8_.refs_2_ = bf16[320,3072]{1,0:T(8,128)(2,1)} collective-permute-done((bf16[320,3072]{1,0:T(8,128)(2,1)}, bf16[320,3072]{1,0:T(8,128)(2,1)}, u32[]{:S(2)}, u32[]{:S(2)}) %collective-permute-start.13) | collective-permute-done | bytes 1966112 | tf_op jit(solution)/shard_map/ppermute | solution.py:269
  183.3 1.2 collective-permute-done.14.y_ref.refs_9_.refs_3_
  185.0 1.3 collective-permute-start.22
  186.3 2.4 shard_map.64
  189.2 1.5 collective-permute-start.21
  191.6 24.0 %shard_map.65.refs_8_ = f32[512,3072]{1,0:T(8,128)} custom-call(bf16[320,3072]{1,0:T(8,128)(2,1)} %collective-permute-done.2.refs_0_, bf16[192,3072]{1,0:T(8,128)(2,1)} %collective-permute-done.5.refs_1_, bf16[256,3072]{1,0:T(8,128)(2,1)} %collective-permute-done.7.refs_5_.refs_2_, ...), custom_call_target="tpu_custom_call", output_to_operand_aliasing={{}: (11, {})} | custom-call | flops 512 | bytes 3072 | tf_op jit(solution)/shard_map/pallas_call | solution.py:173
  216.2 3.7 %maximum_select_fusion.refs_1_ = bf16[384,3072]{1,0:T(8,128)(2,1)} fusion(bf16[192,3072]{1,0:T(8,128)(2,1)} %collective-permute-done.16, bf16[192,3072]{1,0:T(8,128)(2,1)} %collective-permute-done.6, bf16[192,3072]{1,0:T(8,128)(2,1)} %collective-permute-done.22, bf16[192,3072]{1,0:T(8,128)(2,1)} %collective-permute-done.15, pred[]{:T(512)S(6)} %and.4), kind=kLoop, calls=%fused_computation | loop fusion | flops 10616832 | bytes 7077889 | tf_op jit(solution)/shard_map/jit(_where)/select_n | solution.py:314
  220.8 1.4 collective-permute-start.28
  222.2 13.1 %shard_map.66 = bf16[512,3072]{1,0:T(8,128)(2,1)} custom-call(bf16[320,3072]{1,0:T(8,128)(2,1)} %collective-permute-done.2.refs_0_, bf16[192,3072]{1,0:T(8,128)(2,1)} %collective-permute-done.5.refs_1_, bf16[320,3072]{1,0:T(8,128)(2,1)} %collective-permute-done.23.refs_10_.refs_2_.refs_4_, bf16[320,3072]{1,0:T(8,128)(2,1)} %collective-permute-done.24.refs_3_.refs_5_, ...), custom_call_target="tpu_custom_call" | custom-call | flops 512 | bytes 3072 | tf_op jit(solution)/shard_map/pallas_call | solution.py:173
  235.3 2.8 collective-permute-start.32
  238.1 20.8 %shard_map.67.refs_3_ = f32[512,3072]{1,0:T(8,128)} custom-call(bf16[512,3072]{1,0:T(8,128)(2,1)} %get-tuple-element.54.x_ref.refs_0_.refs_1_.refs_2_, bf16[320,3072]{1,0:T(8,128)(2,1)} %collective-permute-done.19.refs_10_.refs_7_.refs_1_, bf16[320,3072]{1,0:T(8,128)(2,1)} %collective-permute-done.13.x_ref.refs_8_.refs_2_, ...), custom_call_target="tpu_custom_call", output_to_operand_aliasing={{}: (10, {})} | custom-call | flops 512 | bytes 3072 | tf_op jit(solution)/shard_map/pallas_call | solution.py:173
  258.9 11.9 %shard_map.68.refs_5_ = f32[512,3072]{1,0:T(8,128)} custom-call(bf16[512,3072]{1,0:T(8,128)(2,1)} %get-tuple-element.54.x_ref.refs_0_.refs_1_.refs_2_, bf16[384,3072]{1,0:T(8,128)(2,1)} %maximum_select_fusion.refs_1_, bf16[384,3072]{1,0:T(8,128)(2,1)} %collective-permute-done.29.refs_2_, f32[512,3072]{1,0:T(8,128)} %shard_map.67.refs_3_), custom_call_target="tpu_custom_call", output_to_operand_aliasing={{}: (3, {})} | custom-call | flops 512 | bytes 3072 | tf_op jit(solution)/shard_map/pallas_call | solution.py:173
  270.9 3.1 collective-permute-done.27.x_ref.refs_1_
  274.8 2.5 shard_map.69
  277.4 1.4 collective-permute-start.30
  278.8 1.5 collective-permute-start.31
  280.3 2.2 collective-permute-done.34.refs_4_
  282.6 17.5 %shard_map.70.refs_5_ = f32[512,3072]{1,0:T(8,128)} custom-call(bf16[512,3072]{1,0:T(8,128)(2,1)} %get-tuple-element.54.x_ref.refs_0_.refs_1_.refs_2_, bf16[384,3072]{1,0:T(8,128)(2,1)} %collective-permute-done.27.x_ref.refs_1_, bf16[384,3072]{1,0:T(8,128)(2,1)} %collective-permute-done.28.y_ref.refs_2_, ...), custom_call_target="tpu_custom_call", output_to_operand_aliasing={{}: (5, {})} | custom-call | flops 512 | bytes 3072 | tf_op jit(solution)/shard_map/pallas_call | solution.py:173
  300.1 6.4 %collective-permute-done.32.refs_6_ = bf16[512,3072]{1,0:T(8,128)(2,1)} collective-permute-done((bf16[512,3072]{1,0:T(8,128)(2,1)}, bf16[512,3072]{1,0:T(8,128)(2,1)}, u32[]{:S(2)}, u32[]{:S(2)}) %collective-permute-start.32) | collective-permute-done | bytes 3145760 | tf_op jit(solution)/shard_map/ppermute | solution.py:269
  307.2 2.7 collective-permute-done.35.refs_3_
  309.9 1.7 collective-permute-done.36.refs_4_
  311.6 12.9 %shard_map.71 = (f32[512,1024]{1,0:T(8,128)}, f32[512,1024]{1,0:T(8,128)}, f32[512,1024]{1,0:T(8,128)}) custom-call(bf16[512,3072]{1,0:T(8,128)(2,1)} %get-tuple-element.54.x_ref.refs_0_.refs_1_.refs_2_, bf16[192,3072]{1,0:T(8,128)(2,1)} %collective-permute-done.30.refs_1_, bf16[192,3072]{1,0:T(8,128)(2,1)} %collective-permute-done.31.refs_2_, ...), custom_call_target="tpu_custom_call" | custom-call | flops 512 | bytes 3072 | tf_op jit(solution)/shard_map/pallas_call | solution.py:173
  (42 shorter events, 7.6 us)
Async XLA Ops:
  4.6 32.1 %collective-permute-start.4 = (bf16[512,3072]{1,0:T(8,128)(2,1)}, bf16[512,3072]{1,0:T(8,128)(2,1)}, u32[]{:S(2)}, u32[]{:S(2)}) collective-permute-start(bf16[512,3072]{1,0:T(8,128)(2,1)} %get-tuple-element.54.x_ref.refs_0_.refs_1_.refs_2_), channel_id=1, source_target_pairs={{0,4},{4,0},{8,12},{12,8},{16,20},{20,16},{24,28},{28,24},{1,5},{5... | collective-permute-start | bytes 9437192 | tf_op jit(solution)/shard_map/ppermute | solution.py:269
  5.1 46.4 %collective-permute-start.2 = (bf16[320,3072]{1,0:T(8,128)(2,1)}, bf16[320,3072]{1,0:T(8,128)(2,1)}, u32[]{:S(2)}, u32[]{:S(2)}) collective-permute-start(bf16[320,3072]{1,0:T(8,128)(2,1)} %get-tuple-element.55), channel_id=1, source_target_pairs={{0,8},{4,12},{8,0},{12,4},{16,24},{20,28},{24,16},{28,20},{1,9},{5... | collective-permute-start | bytes 5898248 | tf_op jit(solution)/shard_map/ppermute | solution.py:269
  7.8 43.7 %collective-permute-start.3 = (bf16[320,3072]{1,0:T(8,128)(2,1)}, bf16[320,3072]{1,0:T(8,128)(2,1)}, u32[]{:S(2)}, u32[]{:S(2)}) collective-permute-start(bf16[320,3072]{1,0:T(8,128)(2,1)} %get-tuple-element.55), channel_id=1, source_target_pairs={{8,16},{12,20},{16,8},{20,12},{9,17},{13,21},{17,9},{21,13},{10,18... | collective-permute-start | bytes 5898248 | tf_op jit(solution)/shard_map/ppermute | solution.py:269
  9.8 70.5 %collective-permute-start = (bf16[512,3072]{1,0:T(8,128)(2,1)}, bf16[512,3072]{1,0:T(8,128)(2,1)}, u32[]{:S(2)}, u32[]{:S(2)}) collective-permute-start(bf16[512,3072]{1,0:T(8,128)(2,1)} %get-tuple-element.54.x_ref.refs_0_.refs_1_.refs_2_), channel_id=1, source_target_pairs={{0,1},{1,0},{2,3},{3,2},{4,5},{5,4},{6,7},{7,6},{8,9},{9,8},{10,11... | collective-permute-start | bytes 9437192 | tf_op jit(solution)/shard_map/ppermute | solution.py:269
  11.3 70.2 %collective-permute-start.1 = (bf16[512,3072]{1,0:T(8,128)(2,1)}, bf16[512,3072]{1,0:T(8,128)(2,1)}, u32[]{:S(2)}, u32[]{:S(2)}) collective-permute-start(bf16[512,3072]{1,0:T(8,128)(2,1)} %get-tuple-element.54.x_ref.refs_0_.refs_1_.refs_2_), channel_id=1, source_target_pairs={{0,2},{1,3},{2,0},{3,1},{4,6},{5,7},{6,4},{7,5},{8,10},{9,11},{10,... | collective-permute-start | bytes 9437192 | tf_op jit(solution)/shard_map/ppermute | solution.py:269
  51.5 30.9 %collective-permute-start.5 = (bf16[192,3072]{1,0:T(8,128)(2,1)}, bf16[192,3072]{1,0:T(8,128)(2,1)}, u32[]{:S(2)}, u32[]{:S(2)}) collective-permute-start(bf16[192,3072]{1,0:T(8,128)(2,1)} %get-tuple-element.57), channel_id=1, source_target_pairs={{0,8},{4,12},{8,0},{12,4},{16,24},{20,28},{24,16},{28,20},{1,9},{5... | collective-permute-start | bytes 3538952 | tf_op jit(solution)/shard_map/ppermute | solution.py:269
  56.3 26.1 %collective-permute-start.6 = (bf16[192,3072]{1,0:T(8,128)(2,1)}, bf16[192,3072]{1,0:T(8,128)(2,1)}, u32[]{:S(2)}, u32[]{:S(2)}) collective-permute-start(bf16[192,3072]{1,0:T(8,128)(2,1)} %get-tuple-element.57), channel_id=1, source_target_pairs={{8,16},{12,20},{16,8},{20,12},{9,17},{13,21},{17,9},{21,13},{10,18... | collective-permute-start | bytes 3538952 | tf_op jit(solution)/shard_map/ppermute | solution.py:269
  82.4 8.1 %collective-permute-start.11 = (bf16[512,3072]{1,0:T(8,128)(2,1)}, bf16[512,3072]{1,0:T(8,128)(2,1)}, u32[]{:S(2)}, u32[]{:S(2)}) collective-permute-start(bf16[512,3072]{1,0:T(8,128)(2,1)} %collective-permute-done.x_ref.refs_4_.refs_1_), channel_id=1, source_target_pairs={{0,4},{4,0},{8,12},{12,8},{16,20},{20,16},{24,28},{28,24},{1,5},{5... | collective-permute-start | bytes 9437192 | tf_op jit(solution)/shard_map/ppermute | solution.py:269
  82.4 10.5 %collective-permute-start.12 = (bf16[512,3072]{1,0:T(8,128)(2,1)}, bf16[512,3072]{1,0:T(8,128)(2,1)}, u32[]{:S(2)}, u32[]{:S(2)}) collective-permute-start(bf16[512,3072]{1,0:T(8,128)(2,1)} %collective-permute-done.1.y_ref.refs_5_.refs_2_), channel_id=1, source_target_pairs={{0,4},{4,0},{8,12},{12,8},{16,20},{20,16},{24,28},{28,24},{1,5},{5... | collective-permute-start | bytes 9437192 | tf_op jit(solution)/shard_map/ppermute | solution.py:269
  82.9 38.1 %collective-permute-start.10 = (bf16[320,3072]{1,0:T(8,128)(2,1)}, bf16[320,3072]{1,0:T(8,128)(2,1)}, u32[]{:S(2)}, u32[]{:S(2)}) collective-permute-start(bf16[320,3072]{1,0:T(8,128)(2,1)} %collective-permute-done.2.refs_0_), channel_id=1, source_target_pairs={{8,16},{12,20},{16,8},{20,12},{9,17},{13,21},{17,9},{21,13},{10,18... | collective-permute-start | bytes 5898248 | tf_op jit(solution)/shard_map/ppermute | solution.py:269
  84.8 49.3 %collective-permute-start.9 = (bf16[320,3072]{1,0:T(8,128)(2,1)}, bf16[320,3072]{1,0:T(8,128)(2,1)}, u32[]{:S(2)}, u32[]{:S(2)}) collective-permute-start(bf16[320,3072]{1,0:T(8,128)(2,1)} %collective-permute-done.3), channel_id=1, source_target_pairs={{8,0},{12,4},{16,24},{20,28},{9,1},{13,5},{17,25},{21,29},{10,2},{... | collective-permute-start | bytes 5898248 | tf_op jit(solution)/shard_map/ppermute | solution.py:269
  89.0 45.2 %collective-permute-start.7 = (bf16[256,3072]{1,0:T(8,128)(2,1)}, bf16[256,3072]{1,0:T(8,128)(2,1)}, u32[]{:S(2)}, u32[]{:S(2)}) collective-permute-start(bf16[256,3072]{1,0:T(8,128)(2,1)} %get-tuple-element.62), channel_id=1, source_target_pairs={{0,1},{1,0},{2,3},{3,2},{4,5},{5,4},{6,7},{7,6},{8,9},{9,8},{10,11... | collective-permute-start | bytes 4718600 | tf_op jit(solution)/shard_map/ppermute | solution.py:269
  90.5 43.6 %collective-permute-start.8 = (bf16[256,3072]{1,0:T(8,128)(2,1)}, bf16[256,3072]{1,0:T(8,128)(2,1)}, u32[]{:S(2)}, u32[]{:S(2)}) collective-permute-start(bf16[256,3072]{1,0:T(8,128)(2,1)} %get-tuple-element.63), channel_id=1, source_target_pairs={{0,2},{1,3},{2,0},{3,1},{4,6},{5,7},{6,4},{7,5},{8,10},{9,11},{10,... | collective-permute-start | bytes 4718600 | tf_op jit(solution)/shard_map/ppermute | solution.py:269
  134.2 6.6 %collective-permute-start.17 = (bf16[256,3072]{1,0:T(8,128)(2,1)}, bf16[256,3072]{1,0:T(8,128)(2,1)}, u32[]{:S(2)}, u32[]{:S(2)}) collective-permute-start(bf16[256,3072]{1,0:T(8,128)(2,1)} %collective-permute-done.7.refs_5_.refs_2_), channel_id=1, source_target_pairs={{0,4},{4,0},{8,12},{12,8},{16,20},{20,16},{24,28},{28,24},{1,5},{5... | collective-permute-start | bytes 4718600 | tf_op jit(solution)/shard_map/ppermute | solution.py:269
  134.2 8.3 %collective-permute-start.18 = (bf16[256,3072]{1,0:T(8,128)(2,1)}, bf16[256,3072]{1,0:T(8,128)(2,1)}, u32[]{:S(2)}, u32[]{:S(2)}) collective-permute-start(bf16[256,3072]{1,0:T(8,128)(2,1)} %collective-permute-done.8.refs_6_.refs_3_), channel_id=1, source_target_pairs={{0,4},{4,0},{8,12},{12,8},{16,20},{20,16},{24,28},{28,24},{1,5},{5... | collective-permute-start | bytes 4718600 | tf_op jit(solution)/shard_map/ppermute | solution.py:269
  137.7 6.2 %collective-permute-start.19 = (bf16[320,3072]{1,0:T(8,128)(2,1)}, bf16[320,3072]{1,0:T(8,128)(2,1)}, u32[]{:S(2)}, u32[]{:S(2)}) collective-permute-start(bf16[320,3072]{1,0:T(8,128)(2,1)} %broadcast_select_fusion.refs_9_.refs_6_), channel_id=1, source_target_pairs={{0,4},{4,0},{8,12},{12,8},{16,20},{20,16},{24,28},{28,24},{1,5},{5... | collective-permute-start | bytes 5898248 | tf_op jit(solution)/shard_map/ppermute | solution.py:269
  137.8 45.5 %collective-permute-start.13 = (bf16[320,3072]{1,0:T(8,128)(2,1)}, bf16[320,3072]{1,0:T(8,128)(2,1)}, u32[]{:S(2)}, u32[]{:S(2)}) collective-permute-start(bf16[320,3072]{1,0:T(8,128)(2,1)} %broadcast_select_fusion.refs_9_.refs_6_), channel_id=1, source_target_pairs={{0,1},{1,0},{2,3},{3,2},{4,5},{5,4},{6,7},{7,6},{8,9},{9,8},{10,11... | collective-permute-start | bytes 5898248 | tf_op jit(solution)/shard_map/ppermute | solution.py:269
  139.3 45.2 %collective-permute-start.14 = (bf16[320,3072]{1,0:T(8,128)(2,1)}, bf16[320,3072]{1,0:T(8,128)(2,1)}, u32[]{:S(2)}, u32[]{:S(2)}) collective-permute-start(bf16[320,3072]{1,0:T(8,128)(2,1)} %broadcast_select_fusion.refs_9_.refs_6_), channel_id=1, source_target_pairs={{0,2},{1,3},{2,0},{3,1},{4,6},{5,7},{6,4},{7,5},{8,10},{9,11},{10,... | collective-permute-start | bytes 5898248 | tf_op jit(solution)/shard_map/ppermute | solution.py:269
  140.8 36.2 %collective-permute-start.16 = (bf16[192,3072]{1,0:T(8,128)(2,1)}, bf16[192,3072]{1,0:T(8,128)(2,1)}, u32[]{:S(2)}, u32[]{:S(2)}) collective-permute-start(bf16[192,3072]{1,0:T(8,128)(2,1)} %collective-permute-done.5.refs_1_), channel_id=1, source_target_pairs={{8,16},{12,20},{16,8},{20,12},{9,17},{13,21},{17,9},{21,13},{10,18... | collective-permute-start | bytes 3538952 | tf_op jit(solution)/shard_map/ppermute | solution.py:269
  142.5 34.5 %collective-permute-start.15 = (bf16[192,3072]{1,0:T(8,128)(2,1)}, bf16[192,3072]{1,0:T(8,128)(2,1)}, u32[]{:S(2)}, u32[]{:S(2)}) collective-permute-start(bf16[192,3072]{1,0:T(8,128)(2,1)} %collective-permute-done.6), channel_id=1, source_target_pairs={{8,0},{12,4},{16,24},{20,28},{9,1},{13,5},{17,25},{21,29},{10,2},{... | collective-permute-start | bytes 3538952 | tf_op jit(solution)/shard_map/ppermute | solution.py:269
  184.5 6.3 %collective-permute-start.23 = (bf16[320,3072]{1,0:T(8,128)(2,1)}, bf16[320,3072]{1,0:T(8,128)(2,1)}, u32[]{:S(2)}, u32[]{:S(2)}) collective-permute-start(bf16[320,3072]{1,0:T(8,128)(2,1)} %collective-permute-done.13.x_ref.refs_8_.refs_2_), channel_id=1, source_target_pairs={{0,4},{4,0},{8,12},{12,8},{16,20},{20,16},{24,28},{28,24},{1,5},{5... | collective-permute-start | bytes 5898248 | tf_op jit(solution)/shard_map/ppermute | solution.py:269
  184.5 7.1 %collective-permute-start.24 = (bf16[320,3072]{1,0:T(8,128)(2,1)}, bf16[320,3072]{1,0:T(8,128)(2,1)}, u32[]{:S(2)}, u32[]{:S(2)}) collective-permute-start(bf16[320,3072]{1,0:T(8,128)(2,1)} %collective-permute-done.14.y_ref.refs_9_.refs_3_), channel_id=1, source_target_pairs={{0,4},{4,0},{8,12},{12,8},{16,20},{20,16},{24,28},{28,24},{1,5},{5... | collective-permute-start | bytes 5898248 | tf_op jit(solution)/shard_map/ppermute | solution.py:269
  185.0 30.6 %collective-permute-start.22 = (bf16[192,3072]{1,0:T(8,128)(2,1)}, bf16[192,3072]{1,0:T(8,128)(2,1)}, u32[]{:S(2)}, u32[]{:S(2)}) collective-permute-start(bf16[192,3072]{1,0:T(8,128)(2,1)} %collective-permute-done.16), channel_id=1, source_target_pairs={{8,0},{12,4},{16,24},{20,28},{9,1},{13,5},{17,25},{21,29},{10,2},{... | collective-permute-start | bytes 3538952 | tf_op jit(solution)/shard_map/ppermute | solution.py:269
  188.6 26.9 %collective-permute-start.20 = (bf16[160,3072]{1,0:T(8,128)(2,1)}, bf16[160,3072]{1,0:T(8,128)(2,1)}, u32[]{:S(2)}, u32[]{:S(2)}) collective-permute-start(bf16[160,3072]{1,0:T(8,128)(2,1)} %get-tuple-element.81), channel_id=1, source_target_pairs={{0,1},{1,0},{2,3},{3,2},{4,5},{5,4},{6,7},{7,6},{8,9},{9,8},{10,11... | collective-permute-start | bytes 2949128 | tf_op jit(solution)/shard_map/ppermute | solution.py:269
  189.2 26.3 %collective-permute-start.21 = (bf16[160,3072]{1,0:T(8,128)(2,1)}, bf16[160,3072]{1,0:T(8,128)(2,1)}, u32[]{:S(2)}, u32[]{:S(2)}) collective-permute-start(bf16[160,3072]{1,0:T(8,128)(2,1)} %get-tuple-element.82), channel_id=1, source_target_pairs={{0,2},{1,3},{2,0},{3,1},{4,6},{5,7},{6,4},{7,5},{8,10},{9,11},{10,... | collective-permute-start | bytes 2949128 | tf_op jit(solution)/shard_map/ppermute | solution.py:269
  215.6 4.3 %collective-permute-start.25 = (bf16[160,3072]{1,0:T(8,128)(2,1)}, bf16[160,3072]{1,0:T(8,128)(2,1)}, u32[]{:S(2)}, u32[]{:S(2)}) collective-permute-start(bf16[160,3072]{1,0:T(8,128)(2,1)} %collective-permute-done.20.refs_4_.refs_6_), channel_id=1, source_target_pairs={{0,4},{4,0},{8,12},{12,8},{16,20},{20,16},{24,28},{28,24},{1,5},{5... | collective-permute-start | bytes 2949128 | tf_op jit(solution)/shard_map/ppermute | solution.py:269
  215.8 4.2 %collective-permute-start.26 = (bf16[160,3072]{1,0:T(8,128)(2,1)}, bf16[160,3072]{1,0:T(8,128)(2,1)}, u32[]{:S(2)}, u32[]{:S(2)}) collective-permute-start(bf16[160,3072]{1,0:T(8,128)(2,1)} %collective-permute-done.21.refs_5_.refs_7_), channel_id=1, source_target_pairs={{0,4},{4,0},{8,12},{12,8},{16,20},{20,16},{24,28},{28,24},{1,5},{5... | collective-permute-start | bytes 2949128 | tf_op jit(solution)/shard_map/ppermute | solution.py:269
  220.0 39.0 %collective-permute-start.29 = (bf16[384,3072]{1,0:T(8,128)(2,1)}, bf16[384,3072]{1,0:T(8,128)(2,1)}, u32[]{:S(2)}, u32[]{:S(2)}) collective-permute-start(bf16[384,3072]{1,0:T(8,128)(2,1)} %maximum_select_fusion.refs_1_), channel_id=1, source_target_pairs={{0,4},{4,0},{8,12},{12,8},{16,20},{20,16},{24,28},{28,24},{1,5},{5... | collective-permute-start | bytes 7077896 | tf_op jit(solution)/shard_map/ppermute | solution.py:269
  220.1 53.8 %collective-permute-start.27 = (bf16[384,3072]{1,0:T(8,128)(2,1)}, bf16[384,3072]{1,0:T(8,128)(2,1)}, u32[]{:S(2)}, u32[]{:S(2)}) collective-permute-start(bf16[384,3072]{1,0:T(8,128)(2,1)} %maximum_select_fusion.refs_1_), channel_id=1, source_target_pairs={{0,1},{1,0},{2,3},{3,2},{4,5},{5,4},{6,7},{7,6},{8,9},{9,8},{10,11... | collective-permute-start | bytes 7077896 | tf_op jit(solution)/shard_map/ppermute | solution.py:269
  220.8 53.5 %collective-permute-start.28 = (bf16[384,3072]{1,0:T(8,128)(2,1)}, bf16[384,3072]{1,0:T(8,128)(2,1)}, u32[]{:S(2)}, u32[]{:S(2)}) collective-permute-start(bf16[384,3072]{1,0:T(8,128)(2,1)} %maximum_select_fusion.refs_1_), channel_id=1, source_target_pairs={{0,2},{1,3},{2,0},{3,1},{4,6},{5,7},{6,4},{7,5},{8,10},{9,11},{10,... | collective-permute-start | bytes 7077896 | tf_op jit(solution)/shard_map/ppermute | solution.py:269
  235.3 71.2 %collective-permute-start.32 = (bf16[512,3072]{1,0:T(8,128)(2,1)}, bf16[512,3072]{1,0:T(8,128)(2,1)}, u32[]{:S(2)}, u32[]{:S(2)}) collective-permute-start(bf16[512,3072]{1,0:T(8,128)(2,1)} %shard_map.66), channel_id=1, source_target_pairs={{0,8},{4,12},{8,0},{12,4},{16,24},{20,28},{24,16},{28,20},{1,9},{5... | collective-permute-start | bytes 9437192 | tf_op jit(solution)/shard_map/ppermute | solution.py:269
  274.3 6.0 %collective-permute-start.33 = (bf16[384,3072]{1,0:T(8,128)(2,1)}, bf16[384,3072]{1,0:T(8,128)(2,1)}, u32[]{:S(2)}, u32[]{:S(2)}) collective-permute-start(bf16[384,3072]{1,0:T(8,128)(2,1)} %collective-permute-done.27.x_ref.refs_1_), channel_id=1, source_target_pairs={{0,4},{4,0},{8,12},{12,8},{16,20},{20,16},{24,28},{28,24},{1,5},{5... | collective-permute-start | bytes 7077896 | tf_op jit(solution)/shard_map/ppermute | solution.py:269
  274.3 8.2 %collective-permute-start.34 = (bf16[384,3072]{1,0:T(8,128)(2,1)}, bf16[384,3072]{1,0:T(8,128)(2,1)}, u32[]{:S(2)}, u32[]{:S(2)}) collective-permute-start(bf16[384,3072]{1,0:T(8,128)(2,1)} %collective-permute-done.28.y_ref.refs_2_), channel_id=1, source_target_pairs={{0,4},{4,0},{8,12},{12,8},{16,20},{20,16},{24,28},{28,24},{1,5},{5... | collective-permute-start | bytes 7077896 | tf_op jit(solution)/shard_map/ppermute | solution.py:269
  277.4 29.1 %collective-permute-start.30 = (bf16[192,3072]{1,0:T(8,128)(2,1)}, bf16[192,3072]{1,0:T(8,128)(2,1)}, u32[]{:S(2)}, u32[]{:S(2)}) collective-permute-start(bf16[192,3072]{1,0:T(8,128)(2,1)} %get-tuple-element.97), channel_id=1, source_target_pairs={{0,1},{1,0},{2,3},{3,2},{4,5},{5,4},{6,7},{7,6},{8,9},{9,8},{10,11... | collective-permute-start | bytes 3538952 | tf_op jit(solution)/shard_map/ppermute | solution.py:269
  278.8 27.9 %collective-permute-start.31 = (bf16[192,3072]{1,0:T(8,128)(2,1)}, bf16[192,3072]{1,0:T(8,128)(2,1)}, u32[]{:S(2)}, u32[]{:S(2)}) collective-permute-start(bf16[192,3072]{1,0:T(8,128)(2,1)} %get-tuple-element.98), channel_id=1, source_target_pairs={{0,2},{1,3},{2,0},{3,1},{4,6},{5,7},{6,4},{7,5},{8,10},{9,11},{10,... | collective-permute-start | bytes 3538952 | tf_op jit(solution)/shard_map/ppermute | solution.py:269
  306.7 3.2 collective-permute-start.35
  306.7 4.9 %collective-permute-start.36 = (bf16[192,3072]{1,0:T(8,128)(2,1)}, bf16[192,3072]{1,0:T(8,128)(2,1)}, u32[]{:S(2)}, u32[]{:S(2)}) collective-permute-start(bf16[192,3072]{1,0:T(8,128)(2,1)} %collective-permute-done.31.refs_2_), channel_id=1, source_target_pairs={{0,4},{4,0},{8,12},{12,8},{16,20},{20,16},{24,28},{28,24},{1,5},{5... | collective-permute-start | bytes 3538952 | tf_op jit(solution)/shard_map/ppermute | solution.py:269

commit v7 on v6

--- a/solution.py
+++ b/solution.py
@@ -257,12 +257,51 @@
     )(a, b, c)
 
 
+def pick_kernel(rows, parts, flag_ref, *refs):
+    count = len(rows)
+    out_ref, buf, sem = refs[2 * count :]
+    spans = []
+    for n, size in enumerate(rows):
+        for m in range(parts):
+            spans.append((n, m * size // parts, sum(rows[:n]) + m * size // parts, size // parts))
+
+    def load(sources):
+        for k, (n, src, dst, size) in enumerate(spans):
+            pltpu.make_async_copy(sources[n].at[pl.ds(src, size)], buf.at[pl.ds(dst, size)], sem.at[0, k]).start()
+
+    pl.when(flag_ref[0] == 1)(lambda: load(refs[:count]))
+    pl.when(flag_ref[0] != 1)(lambda: load(refs[count : 2 * count]))
+    stores = []
+    for k, (_, _, dst, size) in enumerate(spans):
+        part = buf.at[pl.ds(dst, size)]
+        pltpu.make_async_copy(part, part, sem.at[0, k]).wait()
+        stores.append(pltpu.make_async_copy(part, out_ref.at[pl.ds(dst, size)], sem.at[1, k]))
+        stores[-1].start()
+    for store in stores:
+        store.wait()
+
+
+def pick(flag, ones, others):
+    rows, width = [v.shape[0] for v in ones], ones[0].shape[1]
+    parts = 2
+    spec = pl.BlockSpec(memory_space=pltpu.HBM)
+    out = jax.ShapeDtypeStruct((sum(rows), width), ones[0].dtype)
+    return pl.pallas_call(
+        functools.partial(pick_kernel, rows, parts),
+        in_specs=[pl.BlockSpec(memory_space=pltpu.SMEM)] + [spec] * (2 * len(ones)),
+        out_specs=spec,
+        out_shape=out,
+        scratch_shapes=[pltpu.VMEM(out.shape, out.dtype), pltpu.SemaphoreType.DMA((2, parts * len(ones)))],
+        cost_estimate=pl.CostEstimate(flops=out.shape[0], bytes_accessed=width, transcendentals=0),
+    )(flag, *ones, *others)
+
+
 def near_shards(factor_a, factor_b, factor_c):
     rows = factor_a.shape[0]
     early = rows * 5 // 8
     x, part_a, part_c = side_by_side(factor_a, factor_b, factor_c, early)
     row = lax.axis_index("row")
-    inner = (row >= 2) & (row < 6)
+    inner = ((row >= 2) & (row < 6)).astype(jnp.int32).reshape(1)
     fence = lax.optimization_barrier
 
     def move(axis, pairs):
@@ -295,7 +334,7 @@
     (visit,) = pair_sums(guest, [x, x_s, x_x, x_y, x_xs, x_ys], None, 1024)
     x_d0, x_d1, out_a, next_b, visit = fence((x_d0, x_d1, out_a, next_b, visit))
 
-    e = jnp.where(inner, next_b, out_a)
+    e = pick(inner, [next_b], [out_a])
     e_x, e_y = along_x(e), along_y(e)
     x_ds0, x_ds1, e_s = fence((core(x_d0), core(x_d1), core(e)))
     x_d = [x_d0, x_d1, x_ds0, x_ds1]
@@ -311,7 +350,7 @@
     (visit,) = pair_sums(guest, [*x_d, e, e_s, e_x, e_y, (e_xs, 0, lead)], [visit], 1280)
     e_d0, e_d1, out_c1, visit = fence((e_d0, e_d1, out_c1, visit))
 
-    c = jnp.where(inner, jnp.concatenate([far_c, next_c]), jnp.concatenate([out_c0, out_c1]))
+    c = pick(inner, [far_c, next_c], [out_c0, out_c1])
     c, e_ds0, e_ds1 = fence((c, core(e_d0), core(e_d1)))
     c_x, c_y, c_s = along_x(c), along_y(c), core(c)
     e_d = [e_d0, e_d1, e_ds0, e_ds1]

time: 325 us -> 325 us (level)
  other arithmetic: 6.72 us -> 0 us
  Pallas kernels: 210 us -> 215 us
    select_n x2 -> x0, other arithmetic: 6.72 us -> none  [the longest x1 3.7 us: near_shards(): jnp.where(inner, jnp.concatenate([far_c, next_c]), jnp.concatenate([out_c...]
    pallas_call x0 -> x2, Pallas kernels: none -> 5.08 us  [pick(): pl.pallas_call(functools.partial(pick_kernel, rows, parts), in_specs=[pl....]
  transfers between devices with their start and end apart: 37 -> 37, of which waited for: 17 -> 17; matrix products, arithmetic and copies ran while one was open for 2% -> 0% of each run, Pallas kernels for 60% -> 61%
where the time goes in v7:
time: 325 us; the launch traced here: 324 us
  Pallas kernels  215 us (66%)
  waiting for transfers between devices  66.2 us (20%)
  starting transfers between devices  41.8 us (13%)
    pallas_call x9, Pallas kernels, pair_sums(): pl.pallas_call(functools.partial(pair_kernel, feat, i_rows, spans, tile,...  175 us
    ppermute x37, waiting for transfers between devices, move(): return lambda v: lax.ppermute(v, axis, pairs)  66.2 us
    ppermute x37, starting transfers between devices, move(): return lambda v: lax.ppermute(v, axis, pairs)  41.8 us
    pallas_call x1, Pallas kernels, trace_terms(): pl.pallas_call(functools.partial(trace_kernel, feat), grid=(rows // LANES...  23.9 us
    pallas_call x3, Pallas kernels, cut(): pl.pallas_call(functools.partial(cut_kernel, mid, parts), in_specs=[spec]...  7.75 us
  transfers between devices with their start and end apart: 37, of which 17 were waited for; matrix products, arithmetic and copies ran while one was open for 0% of the time, Pallas kernels for 61%

profile of v7, /device:TPU:0, one launch (start us, length us, event | category | flops | bytes accessed | tf_op | source)
XLA Modules:
  0.0 324.3 jit_solution(13693958143692617262)
XLA Ops:
  0.6 4.0 %shard_map.58 = (bf16[512,3072]{1,0:T(8,128)(2,1)}, bf16[320,3072]{1,0:T(8,128)(2,1)}, bf16[192,3072]{1,0:T(8,128)(2,1)}) custom-call(bf16[512,1024]{1,0:T(8,128)(2,1)} %a_ref.1, bf16[512,1024]{1,0:T(8,128)(2,1)} %b_ref.1, bf16[512,1024]{1,0:T(8,128)(2,1)} %c_ref.1), custom_call_target="tpu_custom_call" | custom-call | flops 512 | bytes 1024 | tf_op jit(solution)/shard_map/pallas_call | solution.py:250
  5.1 2.7 collective-permute-start.2
  7.8 2.0 collective-permute-start.3
  9.8 1.5 collective-permute-start
  11.3 1.5 collective-permute-start.1
  12.8 23.9 %shard_map.59.refs_3_ = f32[512,3072]{1,0:T(8,128)} custom-call(bf16[512,3072]{1,0:T(8,128)(2,1)} %get-tuple-element.54.x_ref.refs_0_.refs_1_.refs_2_), custom_call_target="tpu_custom_call" | custom-call | flops 512 | bytes 3072 | tf_op jit(solution)/shard_map/pallas_call | solution.py:42
  36.7 13.2 %shard_map.60.refs_11_ = f32[512,3072]{1,0:T(8,128)} custom-call(bf16[512,3072]{1,0:T(8,128)(2,1)} %get-tuple-element.54.x_ref.refs_0_.refs_1_.refs_2_, bf16[512,3072]{1,0:T(8,128)(2,1)} %get-tuple-element.54.x_ref.refs_0_.refs_1_.refs_2_, bf16[512,3072]{1,0:T(8,128)(2,1)} %collective-permute-done.4.refs_2_.refs_3_, ...), custom_call_target="tpu_custom_call", output_to_operand_aliasing={{}: (3, {})} | custom-call | flops 512 | bytes 3072 | tf_op jit(solution)/shard_map/pallas_call | solution.py:173
  50.0 1.6 collective-permute-done.2.refs_0_
  51.5 4.8 %collective-permute-start.5 = (bf16[192,3072]{1,0:T(8,128)(2,1)}, bf16[192,3072]{1,0:T(8,128)(2,1)}, u32[]{:S(2)}, u32[]{:S(2)}) collective-permute-start(bf16[192,3072]{1,0:T(8,128)(2,1)} %get-tuple-element.57), channel_id=1, source_target_pairs={{0,8},{4,12},{8,0},{12,4},{16,24},{20,28},{24,16},{28,20},{1,9},{5... | collective-permute-start | bytes 3538952 | tf_op jit(solution)/shard_map/ppermute | solution.py:308
  56.3 1.7 collective-permute-start.6
  58.0 22.3 %collective-permute-done.x_ref.refs_4_.refs_1_ = bf16[512,3072]{1,0:T(8,128)(2,1)} collective-permute-done((bf16[512,3072]{1,0:T(8,128)(2,1)}, bf16[512,3072]{1,0:T(8,128)(2,1)}, u32[]{:S(2)}, u32[]{:S(2)}) %collective-permute-start) | collective-permute-done | bytes 3145760 | tf_op jit(solution)/shard_map/ppermute | solution.py:308
  80.3 1.2 collective-permute-done.1.y_ref.refs_5_.refs_2_
  82.9 2.0 collective-permute-start.10
  84.9 1.3 collective-permute-start.9
  86.2 2.9 shard_map.61
  89.0 1.6 collective-permute-start.7
  90.6 1.5 collective-permute-start.8
  92.9 28.1 %shard_map.62.refs_11_ = f32[512,3072]{1,0:T(8,128)} custom-call(bf16[320,3072]{1,0:T(8,128)(2,1)} %collective-permute-done.2.refs_0_, bf16[192,3072]{1,0:T(8,128)(2,1)} %collective-permute-done.5.refs_1_, bf16[512,3072]{1,0:T(8,128)(2,1)} %get-tuple-element.54.x_ref.refs_0_.refs_1_.refs_2_, bf16[512,3072]{1,0:T(8,128)(2,1)} %collective-permute-done.4.refs_2_.refs_3_, ...), custom_call_target="tpu_custom_call" | custom-call | flops 512 | bytes 3072 | tf_op jit(solution)/shard_map/pallas_call | solution.py:173
  121.1 13.1 %collective-permute-done.9.refs_1_ = bf16[320,3072]{1,0:T(8,128)(2,1)} collective-permute-done((bf16[320,3072]{1,0:T(8,128)(2,1)}, bf16[320,3072]{1,0:T(8,128)(2,1)}, u32[]{:S(2)}, u32[]{:S(2)}) %collective-permute-start.9) | collective-permute-done | bytes 1966112 | tf_op jit(solution)/shard_map/ppermute | solution.py:308
  134.7 2.5 shard_map.63.refs_9_.refs_6_
  137.3 1.5 collective-permute-start.13
  138.8 1.5 collective-permute-start.14
  140.3 1.7 collective-permute-start.16
  142.0 1.5 collective-permute-start.15
  143.5 33.0 %shard_map.64.refs_10_ = f32[512,3072]{1,0:T(8,128)} custom-call(bf16[512,3072]{1,0:T(8,128)(2,1)} %get-tuple-element.54.x_ref.refs_0_.refs_1_.refs_2_, bf16[512,3072]{1,0:T(8,128)(2,1)} %collective-permute-done.x_ref.refs_4_.refs_1_, bf16[512,3072]{1,0:T(8,128)(2,1)} %collective-permute-done.1.y_ref.refs_5_.refs_2_, ...), custom_call_target="tpu_custom_call", output_to_operand_aliasing={{}: (11, {})} | custom-call | flops 512 | bytes 3072 | tf_op jit(solution)/shard_map/pallas_call | solution.py:173
  176.5 6.3 %collective-permute-done.13.x_ref.refs_8_.refs_2_ = bf16[320,3072]{1,0:T(8,128)(2,1)} collective-permute-done((bf16[320,3072]{1,0:T(8,128)(2,1)}, bf16[320,3072]{1,0:T(8,128)(2,1)}, u32[]{:S(2)}, u32[]{:S(2)}) %collective-permute-start.13) | collective-permute-done | bytes 1966112 | tf_op jit(solution)/shard_map/ppermute | solution.py:308
  182.8 1.2 collective-permute-done.14.y_ref.refs_9_.refs_3_
  184.5 1.3 collective-permute-start.22
  185.8 2.4 shard_map.65
  188.8 1.5 collective-permute-start.21
  191.2 24.0 %shard_map.66.refs_8_ = f32[512,3072]{1,0:T(8,128)} custom-call(bf16[320,3072]{1,0:T(8,128)(2,1)} %collective-permute-done.2.refs_0_, bf16[192,3072]{1,0:T(8,128)(2,1)} %collective-permute-done.5.refs_1_, bf16[256,3072]{1,0:T(8,128)(2,1)} %collective-permute-done.7.refs_5_.refs_2_, ...), custom_call_target="tpu_custom_call", output_to_operand_aliasing={{}: (11, {})} | custom-call | flops 512 | bytes 3072 | tf_op jit(solution)/shard_map/pallas_call | solution.py:173
  215.7 2.6 shard_map.67.refs_1_
  218.3 1.2 collective-permute-done.26.refs_7_.refs_9_
  220.4 1.4 collective-permute-start.28
  221.8 13.1 %shard_map.68 = bf16[512,3072]{1,0:T(8,128)(2,1)} custom-call(bf16[320,3072]{1,0:T(8,128)(2,1)} %collective-permute-done.2.refs_0_, bf16[192,3072]{1,0:T(8,128)(2,1)} %collective-permute-done.5.refs_1_, bf16[320,3072]{1,0:T(8,128)(2,1)} %collective-permute-done.23.refs_10_.refs_2_.refs_4_, bf16[320,3072]{1,0:T(8,128)(2,1)} %collective-permute-done.24.refs_3_.refs_5_, ...), custom_call_target="tpu_custom_call" | custom-call | flops 512 | bytes 3072 | tf_op jit(solution)/shard_map/pallas_call | solution.py:173
  234.9 2.8 collective-permute-start.32
  237.7 20.8 %shard_map.69.refs_3_ = f32[512,3072]{1,0:T(8,128)} custom-call(bf16[512,3072]{1,0:T(8,128)(2,1)} %get-tuple-element.54.x_ref.refs_0_.refs_1_.refs_2_, bf16[320,3072]{1,0:T(8,128)(2,1)} %collective-permute-done.19.refs_10_.refs_7_.refs_1_, bf16[320,3072]{1,0:T(8,128)(2,1)} %collective-permute-done.13.x_ref.refs_8_.refs_2_, ...), custom_call_target="tpu_custom_call", output_to_operand_aliasing={{}: (10, {})} | custom-call | flops 512 | bytes 3072 | tf_op jit(solution)/shard_map/pallas_call | solution.py:173
  258.6 11.9 %shard_map.70.refs_5_ = f32[512,3072]{1,0:T(8,128)} custom-call(bf16[512,3072]{1,0:T(8,128)(2,1)} %get-tuple-element.54.x_ref.refs_0_.refs_1_.refs_2_, bf16[384,3072]{1,0:T(8,128)(2,1)} %shard_map.67.refs_1_, bf16[384,3072]{1,0:T(8,128)(2,1)} %collective-permute-done.29.refs_2_, f32[512,3072]{1,0:T(8,128)} %shard_map.69.refs_3_), custom_call_target="tpu_custom_call", output_to_operand_aliasing={{}: (3, {})} | custom-call | flops 512 | bytes 3072 | tf_op jit(solution)/shard_map/pallas_call | solution.py:173
  270.5 3.0 collective-permute-done.27.x_ref.refs_1_
  274.4 2.5 shard_map.71
  277.0 1.4 collective-permute-start.30
  278.4 1.5 collective-permute-start.31
  279.9 2.3 collective-permute-done.34.refs_4_
  282.2 17.5 %shard_map.72.refs_5_ = f32[512,3072]{1,0:T(8,128)} custom-call(bf16[512,3072]{1,0:T(8,128)(2,1)} %get-tuple-element.54.x_ref.refs_0_.refs_1_.refs_2_, bf16[384,3072]{1,0:T(8,128)(2,1)} %collective-permute-done.27.x_ref.refs_1_, bf16[384,3072]{1,0:T(8,128)(2,1)} %collective-permute-done.28.y_ref.refs_2_, ...), custom_call_target="tpu_custom_call", output_to_operand_aliasing={{}: (5, {})} | custom-call | flops 512 | bytes 3072 | tf_op jit(solution)/shard_map/pallas_call | solution.py:173
  299.6 6.4 %collective-permute-done.32.refs_6_ = bf16[512,3072]{1,0:T(8,128)(2,1)} collective-permute-done((bf16[512,3072]{1,0:T(8,128)(2,1)}, bf16[512,3072]{1,0:T(8,128)(2,1)}, u32[]{:S(2)}, u32[]{:S(2)}) %collective-permute-start.32) | collective-permute-done | bytes 3145760 | tf_op jit(solution)/shard_map/ppermute | solution.py:308
  306.8 2.7 collective-permute-done.35.refs_3_
  309.5 1.7 collective-permute-done.36.refs_4_
  311.2 12.9 %shard_map.73 = (f32[512,1024]{1,0:T(8,128)}, f32[512,1024]{1,0:T(8,128)}, f32[512,1024]{1,0:T(8,128)}) custom-call(bf16[512,3072]{1,0:T(8,128)(2,1)} %get-tuple-element.54.x_ref.refs_0_.refs_1_.refs_2_, bf16[192,3072]{1,0:T(8,128)(2,1)} %collective-permute-done.30.refs_1_, bf16[192,3072]{1,0:T(8,128)(2,1)} %collective-permute-done.31.refs_2_, ...), custom_call_target="tpu_custom_call" | custom-call | flops 512 | bytes 3072 | tf_op jit(solution)/shard_map/pallas_call | solution.py:173
  (42 shorter events, 8.4 us)
Async XLA Ops:
  4.6 32.1 %collective-permute-start.4 = (bf16[512,3072]{1,0:T(8,128)(2,1)}, bf16[512,3072]{1,0:T(8,128)(2,1)}, u32[]{:S(2)}, u32[]{:S(2)}) collective-permute-start(bf16[512,3072]{1,0:T(8,128)(2,1)} %get-tuple-element.54.x_ref.refs_0_.refs_1_.refs_2_), channel_id=1, source_target_pairs={{0,4},{4,0},{8,12},{12,8},{16,20},{20,16},{24,28},{28,24},{1,5},{5... | collective-permute-start | bytes 9437192 | tf_op jit(solution)/shard_map/ppermute | solution.py:308
  5.1 46.4 %collective-permute-start.2 = (bf16[320,3072]{1,0:T(8,128)(2,1)}, bf16[320,3072]{1,0:T(8,128)(2,1)}, u32[]{:S(2)}, u32[]{:S(2)}) collective-permute-start(bf16[320,3072]{1,0:T(8,128)(2,1)} %get-tuple-element.55), channel_id=1, source_target_pairs={{0,8},{4,12},{8,0},{12,4},{16,24},{20,28},{24,16},{28,20},{1,9},{5... | collective-permute-start | bytes 5898248 | tf_op jit(solution)/shard_map/ppermute | solution.py:308
  7.8 43.7 %collective-permute-start.3 = (bf16[320,3072]{1,0:T(8,128)(2,1)}, bf16[320,3072]{1,0:T(8,128)(2,1)}, u32[]{:S(2)}, u32[]{:S(2)}) collective-permute-start(bf16[320,3072]{1,0:T(8,128)(2,1)} %get-tuple-element.55), channel_id=1, source_target_pairs={{8,16},{12,20},{16,8},{20,12},{9,17},{13,21},{17,9},{21,13},{10,18... | collective-permute-start | bytes 5898248 | tf_op jit(solution)/shard_map/ppermute | solution.py:308
  9.8 70.5 %collective-permute-start = (bf16[512,3072]{1,0:T(8,128)(2,1)}, bf16[512,3072]{1,0:T(8,128)(2,1)}, u32[]{:S(2)}, u32[]{:S(2)}) collective-permute-start(bf16[512,3072]{1,0:T(8,128)(2,1)} %get-tuple-element.54.x_ref.refs_0_.refs_1_.refs_2_), channel_id=1, source_target_pairs={{0,1},{1,0},{2,3},{3,2},{4,5},{5,4},{6,7},{7,6},{8,9},{9,8},{10,11... | collective-permute-start | bytes 9437192 | tf_op jit(solution)/shard_map/ppermute | solution.py:308
  11.3 70.2 %collective-permute-start.1 = (bf16[512,3072]{1,0:T(8,128)(2,1)}, bf16[512,3072]{1,0:T(8,128)(2,1)}, u32[]{:S(2)}, u32[]{:S(2)}) collective-permute-start(bf16[512,3072]{1,0:T(8,128)(2,1)} %get-tuple-element.54.x_ref.refs_0_.refs_1_.refs_2_), channel_id=1, source_target_pairs={{0,2},{1,3},{2,0},{3,1},{4,6},{5,7},{6,4},{7,5},{8,10},{9,11},{10,... | collective-permute-start | bytes 9437192 | tf_op jit(solution)/shard_map/ppermute | solution.py:308
  51.5 30.9 %collective-permute-start.5 = (bf16[192,3072]{1,0:T(8,128)(2,1)}, bf16[192,3072]{1,0:T(8,128)(2,1)}, u32[]{:S(2)}, u32[]{:S(2)}) collective-permute-start(bf16[192,3072]{1,0:T(8,128)(2,1)} %get-tuple-element.57), channel_id=1, source_target_pairs={{0,8},{4,12},{8,0},{12,4},{16,24},{20,28},{24,16},{28,20},{1,9},{5... | collective-permute-start | bytes 3538952 | tf_op jit(solution)/shard_map/ppermute | solution.py:308
  56.3 26.1 %collective-permute-start.6 = (bf16[192,3072]{1,0:T(8,128)(2,1)}, bf16[192,3072]{1,0:T(8,128)(2,1)}, u32[]{:S(2)}, u32[]{:S(2)}) collective-permute-start(bf16[192,3072]{1,0:T(8,128)(2,1)} %get-tuple-element.57), channel_id=1, source_target_pairs={{8,16},{12,20},{16,8},{20,12},{9,17},{13,21},{17,9},{21,13},{10,18... | collective-permute-start | bytes 3538952 | tf_op jit(solution)/shard_map/ppermute | solution.py:308
  82.4 8.2 %collective-permute-start.11 = (bf16[512,3072]{1,0:T(8,128)(2,1)}, bf16[512,3072]{1,0:T(8,128)(2,1)}, u32[]{:S(2)}, u32[]{:S(2)}) collective-permute-start(bf16[512,3072]{1,0:T(8,128)(2,1)} %collective-permute-done.x_ref.refs_4_.refs_1_), channel_id=1, source_target_pairs={{0,4},{4,0},{8,12},{12,8},{16,20},{20,16},{24,28},{28,24},{1,5},{5... | collective-permute-start | bytes 9437192 | tf_op jit(solution)/shard_map/ppermute | solution.py:308
  82.4 10.5 %collective-permute-start.12 = (bf16[512,3072]{1,0:T(8,128)(2,1)}, bf16[512,3072]{1,0:T(8,128)(2,1)}, u32[]{:S(2)}, u32[]{:S(2)}) collective-permute-start(bf16[512,3072]{1,0:T(8,128)(2,1)} %collective-permute-done.1.y_ref.refs_5_.refs_2_), channel_id=1, source_target_pairs={{0,4},{4,0},{8,12},{12,8},{16,20},{20,16},{24,28},{28,24},{1,5},{5... | collective-permute-start | bytes 9437192 | tf_op jit(solution)/shard_map/ppermute | solution.py:308
  82.9 38.1 %collective-permute-start.10 = (bf16[320,3072]{1,0:T(8,128)(2,1)}, bf16[320,3072]{1,0:T(8,128)(2,1)}, u32[]{:S(2)}, u32[]{:S(2)}) collective-permute-start(bf16[320,3072]{1,0:T(8,128)(2,1)} %collective-permute-done.2.refs_0_), channel_id=1, source_target_pairs={{8,16},{12,20},{16,8},{20,12},{9,17},{13,21},{17,9},{21,13},{10,18... | collective-permute-start | bytes 5898248 | tf_op jit(solution)/shard_map/ppermute | solution.py:308
  84.9 49.3 %collective-permute-start.9 = (bf16[320,3072]{1,0:T(8,128)(2,1)}, bf16[320,3072]{1,0:T(8,128)(2,1)}, u32[]{:S(2)}, u32[]{:S(2)}) collective-permute-start(bf16[320,3072]{1,0:T(8,128)(2,1)} %collective-permute-done.3), channel_id=1, source_target_pairs={{8,0},{12,4},{16,24},{20,28},{9,1},{13,5},{17,25},{21,29},{10,2},{... | collective-permute-start | bytes 5898248 | tf_op jit(solution)/shard_map/ppermute | solution.py:308
  89.0 45.1 %collective-permute-start.7 = (bf16[256,3072]{1,0:T(8,128)(2,1)}, bf16[256,3072]{1,0:T(8,128)(2,1)}, u32[]{:S(2)}, u32[]{:S(2)}) collective-permute-start(bf16[256,3072]{1,0:T(8,128)(2,1)} %get-tuple-element.62), channel_id=1, source_target_pairs={{0,1},{1,0},{2,3},{3,2},{4,5},{5,4},{6,7},{7,6},{8,9},{9,8},{10,11... | collective-permute-start | bytes 4718600 | tf_op jit(solution)/shard_map/ppermute | solution.py:308
  90.6 43.6 %collective-permute-start.8 = (bf16[256,3072]{1,0:T(8,128)(2,1)}, bf16[256,3072]{1,0:T(8,128)(2,1)}, u32[]{:S(2)}, u32[]{:S(2)}) collective-permute-start(bf16[256,3072]{1,0:T(8,128)(2,1)} %get-tuple-element.63), channel_id=1, source_target_pairs={{0,2},{1,3},{2,0},{3,1},{4,6},{5,7},{6,4},{7,5},{8,10},{9,11},{10,... | collective-permute-start | bytes 4718600 | tf_op jit(solution)/shard_map/ppermute | solution.py:308
  134.2 6.2 %collective-permute-start.17 = (bf16[256,3072]{1,0:T(8,128)(2,1)}, bf16[256,3072]{1,0:T(8,128)(2,1)}, u32[]{:S(2)}, u32[]{:S(2)}) collective-permute-start(bf16[256,3072]{1,0:T(8,128)(2,1)} %collective-permute-done.7.refs_5_.refs_2_), channel_id=1, source_target_pairs={{0,4},{4,0},{8,12},{12,8},{16,20},{20,16},{24,28},{28,24},{1,5},{5... | collective-permute-start | bytes 4718600 | tf_op jit(solution)/shard_map/ppermute | solution.py:308
  134.2 7.8 %collective-permute-start.18 = (bf16[256,3072]{1,0:T(8,128)(2,1)}, bf16[256,3072]{1,0:T(8,128)(2,1)}, u32[]{:S(2)}, u32[]{:S(2)}) collective-permute-start(bf16[256,3072]{1,0:T(8,128)(2,1)} %collective-permute-done.8.refs_6_.refs_3_), channel_id=1, source_target_pairs={{0,4},{4,0},{8,12},{12,8},{16,20},{20,16},{24,28},{28,24},{1,5},{5... | collective-permute-start | bytes 4718600 | tf_op jit(solution)/shard_map/ppermute | solution.py:308
  137.2 6.3 %collective-permute-start.19 = (bf16[320,3072]{1,0:T(8,128)(2,1)}, bf16[320,3072]{1,0:T(8,128)(2,1)}, u32[]{:S(2)}, u32[]{:S(2)}) collective-permute-start(bf16[320,3072]{1,0:T(8,128)(2,1)} %shard_map.63.refs_9_.refs_6_), channel_id=1, source_target_pairs={{0,4},{4,0},{8,12},{12,8},{16,20},{20,16},{24,28},{28,24},{1,5},{5... | collective-permute-start | bytes 5898248 | tf_op jit(solution)/shard_map/ppermute | solution.py:308
  137.3 45.5 %collective-permute-start.13 = (bf16[320,3072]{1,0:T(8,128)(2,1)}, bf16[320,3072]{1,0:T(8,128)(2,1)}, u32[]{:S(2)}, u32[]{:S(2)}) collective-permute-start(bf16[320,3072]{1,0:T(8,128)(2,1)} %shard_map.63.refs_9_.refs_6_), channel_id=1, source_target_pairs={{0,1},{1,0},{2,3},{3,2},{4,5},{5,4},{6,7},{7,6},{8,9},{9,8},{10,11... | collective-permute-start | bytes 5898248 | tf_op jit(solution)/shard_map/ppermute | solution.py:308
  138.8 45.2 %collective-permute-start.14 = (bf16[320,3072]{1,0:T(8,128)(2,1)}, bf16[320,3072]{1,0:T(8,128)(2,1)}, u32[]{:S(2)}, u32[]{:S(2)}) collective-permute-start(bf16[320,3072]{1,0:T(8,128)(2,1)} %shard_map.63.refs_9_.refs_6_), channel_id=1, source_target_pairs={{0,2},{1,3},{2,0},{3,1},{4,6},{5,7},{6,4},{7,5},{8,10},{9,11},{10,... | collective-permute-start | bytes 5898248 | tf_op jit(solution)/shard_map/ppermute | solution.py:308
  140.3 36.1 %collective-permute-start.16 = (bf16[192,3072]{1,0:T(8,128)(2,1)}, bf16[192,3072]{1,0:T(8,128)(2,1)}, u32[]{:S(2)}, u32[]{:S(2)}) collective-permute-start(bf16[192,3072]{1,0:T(8,128)(2,1)} %collective-permute-done.5.refs_1_), channel_id=1, source_target_pairs={{8,16},{12,20},{16,8},{20,12},{9,17},{13,21},{17,9},{21,13},{10,18... | collective-permute-start | bytes 3538952 | tf_op jit(solution)/shard_map/ppermute | solution.py:308
  142.0 34.5 %collective-permute-start.15 = (bf16[192,3072]{1,0:T(8,128)(2,1)}, bf16[192,3072]{1,0:T(8,128)(2,1)}, u32[]{:S(2)}, u32[]{:S(2)}) collective-permute-start(bf16[192,3072]{1,0:T(8,128)(2,1)} %collective-permute-done.6.refs_0_), channel_id=1, source_target_pairs={{8,0},{12,4},{16,24},{20,28},{9,1},{13,5},{17,25},{21,29},{10,2},{... | collective-permute-start | bytes 3538952 | tf_op jit(solution)/shard_map/ppermute | solution.py:308
  184.0 6.3 %collective-permute-start.23 = (bf16[320,3072]{1,0:T(8,128)(2,1)}, bf16[320,3072]{1,0:T(8,128)(2,1)}, u32[]{:S(2)}, u32[]{:S(2)}) collective-permute-start(bf16[320,3072]{1,0:T(8,128)(2,1)} %collective-permute-done.13.x_ref.refs_8_.refs_2_), channel_id=1, source_target_pairs={{0,4},{4,0},{8,12},{12,8},{16,20},{20,16},{24,28},{28,24},{1,5},{5... | collective-permute-start | bytes 5898248 | tf_op jit(solution)/shard_map/ppermute | solution.py:308
  184.0 7.1 %collective-permute-start.24 = (bf16[320,3072]{1,0:T(8,128)(2,1)}, bf16[320,3072]{1,0:T(8,128)(2,1)}, u32[]{:S(2)}, u32[]{:S(2)}) collective-permute-start(bf16[320,3072]{1,0:T(8,128)(2,1)} %collective-permute-done.14.y_ref.refs_9_.refs_3_), channel_id=1, source_target_pairs={{0,4},{4,0},{8,12},{12,8},{16,20},{20,16},{24,28},{28,24},{1,5},{5... | collective-permute-start | bytes 5898248 | tf_op jit(solution)/shard_map/ppermute | solution.py:308
  184.5 30.6 %collective-permute-start.22 = (bf16[192,3072]{1,0:T(8,128)(2,1)}, bf16[192,3072]{1,0:T(8,128)(2,1)}, u32[]{:S(2)}, u32[]{:S(2)}) collective-permute-start(bf16[192,3072]{1,0:T(8,128)(2,1)} %collective-permute-done.16.refs_1_), channel_id=1, source_target_pairs={{8,0},{12,4},{16,24},{20,28},{9,1},{13,5},{17,25},{21,29},{10,2},{... | collective-permute-start | bytes 3538952 | tf_op jit(solution)/shard_map/ppermute | solution.py:308
  188.2 26.9 %collective-permute-start.20 = (bf16[160,3072]{1,0:T(8,128)(2,1)}, bf16[160,3072]{1,0:T(8,128)(2,1)}, u32[]{:S(2)}, u32[]{:S(2)}) collective-permute-start(bf16[160,3072]{1,0:T(8,128)(2,1)} %get-tuple-element.81), channel_id=1, source_target_pairs={{0,1},{1,0},{2,3},{3,2},{4,5},{5,4},{6,7},{7,6},{8,9},{9,8},{10,11... | collective-permute-start | bytes 2949128 | tf_op jit(solution)/shard_map/ppermute | solution.py:308
  188.8 26.3 %collective-permute-start.21 = (bf16[160,3072]{1,0:T(8,128)(2,1)}, bf16[160,3072]{1,0:T(8,128)(2,1)}, u32[]{:S(2)}, u32[]{:S(2)}) collective-permute-start(bf16[160,3072]{1,0:T(8,128)(2,1)} %get-tuple-element.82), channel_id=1, source_target_pairs={{0,2},{1,3},{2,0},{3,1},{4,6},{5,7},{6,4},{7,5},{8,10},{9,11},{10,... | collective-permute-start | bytes 2949128 | tf_op jit(solution)/shard_map/ppermute | solution.py:308
  215.2 3.2 collective-permute-start.25
  215.4 4.2 %collective-permute-start.26 = (bf16[160,3072]{1,0:T(8,128)(2,1)}, bf16[160,3072]{1,0:T(8,128)(2,1)}, u32[]{:S(2)}, u32[]{:S(2)}) collective-permute-start(bf16[160,3072]{1,0:T(8,128)(2,1)} %collective-permute-done.21.refs_5_.refs_7_), channel_id=1, source_target_pairs={{0,4},{4,0},{8,12},{12,8},{16,20},{20,16},{24,28},{28,24},{1,5},{5... | collective-permute-start | bytes 2949128 | tf_op jit(solution)/shard_map/ppermute | solution.py:308
  219.6 39.0 %collective-permute-start.29 = (bf16[384,3072]{1,0:T(8,128)(2,1)}, bf16[384,3072]{1,0:T(8,128)(2,1)}, u32[]{:S(2)}, u32[]{:S(2)}) collective-permute-start(bf16[384,3072]{1,0:T(8,128)(2,1)} %shard_map.67.refs_1_), channel_id=1, source_target_pairs={{0,4},{4,0},{8,12},{12,8},{16,20},{20,16},{24,28},{28,24},{1,5},{5... | collective-permute-start | bytes 7077896 | tf_op jit(solution)/shard_map/ppermute | solution.py:308
  219.7 53.8 %collective-permute-start.27 = (bf16[384,3072]{1,0:T(8,128)(2,1)}, bf16[384,3072]{1,0:T(8,128)(2,1)}, u32[]{:S(2)}, u32[]{:S(2)}) collective-permute-start(bf16[384,3072]{1,0:T(8,128)(2,1)} %shard_map.67.refs_1_), channel_id=1, source_target_pairs={{0,1},{1,0},{2,3},{3,2},{4,5},{5,4},{6,7},{7,6},{8,9},{9,8},{10,11... | collective-permute-start | bytes 7077896 | tf_op jit(solution)/shard_map/ppermute | solution.py:308
  220.4 53.5 %collective-permute-start.28 = (bf16[384,3072]{1,0:T(8,128)(2,1)}, bf16[384,3072]{1,0:T(8,128)(2,1)}, u32[]{:S(2)}, u32[]{:S(2)}) collective-permute-start(bf16[384,3072]{1,0:T(8,128)(2,1)} %shard_map.67.refs_1_), channel_id=1, source_target_pairs={{0,2},{1,3},{2,0},{3,1},{4,6},{5,7},{6,4},{7,5},{8,10},{9,11},{10,... | collective-permute-start | bytes 7077896 | tf_op jit(solution)/shard_map/ppermute | solution.py:308
  234.9 71.2 %collective-permute-start.32 = (bf16[512,3072]{1,0:T(8,128)(2,1)}, bf16[512,3072]{1,0:T(8,128)(2,1)}, u32[]{:S(2)}, u32[]{:S(2)}) collective-permute-start(bf16[512,3072]{1,0:T(8,128)(2,1)} %shard_map.68), channel_id=1, source_target_pairs={{0,8},{4,12},{8,0},{12,4},{16,24},{20,28},{24,16},{28,20},{1,9},{5... | collective-permute-start | bytes 9437192 | tf_op jit(solution)/shard_map/ppermute | solution.py:308
  273.9 6.0 %collective-permute-start.33 = (bf16[384,3072]{1,0:T(8,128)(2,1)}, bf16[384,3072]{1,0:T(8,128)(2,1)}, u32[]{:S(2)}, u32[]{:S(2)}) collective-permute-start(bf16[384,3072]{1,0:T(8,128)(2,1)} %collective-permute-done.27.x_ref.refs_1_), channel_id=1, source_target_pairs={{0,4},{4,0},{8,12},{12,8},{16,20},{20,16},{24,28},{28,24},{1,5},{5... | collective-permute-start | bytes 7077896 | tf_op jit(solution)/shard_map/ppermute | solution.py:308
  273.9 8.2 %collective-permute-start.34 = (bf16[384,3072]{1,0:T(8,128)(2,1)}, bf16[384,3072]{1,0:T(8,128)(2,1)}, u32[]{:S(2)}, u32[]{:S(2)}) collective-permute-start(bf16[384,3072]{1,0:T(8,128)(2,1)} %collective-permute-done.28.y_ref.refs_2_), channel_id=1, source_target_pairs={{0,4},{4,0},{8,12},{12,8},{16,20},{20,16},{24,28},{28,24},{1,5},{5... | collective-permute-start | bytes 7077896 | tf_op jit(solution)/shard_map/ppermute | solution.py:308
  277.0 29.1 %collective-permute-start.30 = (bf16[192,3072]{1,0:T(8,128)(2,1)}, bf16[192,3072]{1,0:T(8,128)(2,1)}, u32[]{:S(2)}, u32[]{:S(2)}) collective-permute-start(bf16[192,3072]{1,0:T(8,128)(2,1)} %get-tuple-element.97), channel_id=1, source_target_pairs={{0,1},{1,0},{2,3},{3,2},{4,5},{5,4},{6,7},{7,6},{8,9},{9,8},{10,11... | collective-permute-start | bytes 3538952 | tf_op jit(solution)/shard_map/ppermute | solution.py:308
  278.4 27.9 %collective-permute-start.31 = (bf16[192,3072]{1,0:T(8,128)(2,1)}, bf16[192,3072]{1,0:T(8,128)(2,1)}, u32[]{:S(2)}, u32[]{:S(2)}) collective-permute-start(bf16[192,3072]{1,0:T(8,128)(2,1)} %get-tuple-element.98), channel_id=1, source_target_pairs={{0,2},{1,3},{2,0},{3,1},{4,6},{5,7},{6,4},{7,5},{8,10},{9,11},{10,... | collective-permute-start | bytes 3538952 | tf_op jit(solution)/shard_map/ppermute | solution.py:308
  306.3 3.2 collective-permute-start.35
  306.3 4.9 %collective-permute-start.36 = (bf16[192,3072]{1,0:T(8,128)(2,1)}, bf16[192,3072]{1,0:T(8,128)(2,1)}, u32[]{:S(2)}, u32[]{:S(2)}) collective-permute-start(bf16[192,3072]{1,0:T(8,128)(2,1)} %collective-permute-done.31.refs_2_), channel_id=1, source_target_pairs={{0,4},{4,0},{8,12},{12,8},{16,20},{20,16},{24,28},{28,24},{1,5},{5... | collective-permute-start | bytes 3538952 | tf_op jit(solution)/shard_map/ppermute | solution.py:308
